TPU v7x, 512 devices: a whole 4x4x16 slice. The times are simulated.
512 devices in a mesh: seq: 64 (over y, z), head: 8 (over x, core).
Axes of the slice: x: 4, y: 4, z: 16, core: 2. Of those that a mesh axis runs over, the one named last changes fastest.
Arguments:
- queries: bfloat16 [65536, 2048], P('seq', 'head'), may hold values from -140 to 140
- context_grad: bfloat16 [65536, 2048], P('seq', 'head'), may hold values from -6 to 6
- database: bfloat16 [1024, 128, 1024], P('seq'), may hold values from -6 to 6
- neighbour_ids: int32 [1024, 2], P('seq'), may hold values from 0 to 1023, as said below
- owner_map: int32 [1024], replicated, may hold values from 0 to 1023, as said below
- key_weight: bfloat16 [1024, 2048], P('seq', 'head'), may hold values from -0.1875 to 0.1875
- value_weight: bfloat16 [1024, 2048], P('seq', 'head'), may hold values from -0.1875 to 0.1875
Outputs:
- context: bfloat16 [65536, 2048], P('seq', 'head')
- query_grad: bfloat16 [65536, 2048], P('seq', 'head')
Inputs may be any that keep to these rules, and one draw needn't show every extreme that they name: A permutation: row id r is stored at position owner_map[r] of database, on index owner_map[r] // 16 of seq. `neighbour_ids`: through owner_map, the 32 neighbours named by the rows of one index of seq are stored at most 1 on any one index of seq; in every draw one index of seq stores exactly 1 of them for every index of seq.
All inputs are finite; a program needn't handle non-finite values.
Results may differ from a plain program's by a relative error of at most 0.015.
The roundings to bfloat16 on the way count: a program that leaves them out, or rounds other values in their place, can miss the bound.
Values may be sent and summed in bfloat16 or wider, within the bound.
No kernel may reach another device: no remote copies, remote signals or barrier semaphores. Data moves between devices by JAX's collectives and lax.ppermute only.
A program may use at most 64 MiB of HBM per device.

v0:
```python
import jax
import jax.numpy as jnp
from jax import lax
from jax.sharding import PartitionSpec as P

DH = 128
BLOCK = 64


def shifted(value, axis, steps):
    count = lax.axis_size(axis)
    first, last = (max(0, -steps), min(count, count - steps))
    return lax.ppermute(value, axis, [(source, source + steps) for source in range(first, last)])


def attend_forward(shifted_queries, neighbour_kv, head_count):
    block_count = neighbour_kv.shape[0]
    local_width = shifted_queries.shape[1]
    score_scale = DH ** (-0.5)
    queries_four = shifted_queries.reshape(block_count, BLOCK, head_count, DH)
    keys_four = neighbour_kv[:, :, :local_width].reshape(block_count, -1, head_count, DH)
    values_four = neighbour_kv[:, :, local_width:].reshape(block_count, -1, head_count, DH)
    scores = (
        jnp.einsum("cqhd,ckhd->chqk", queries_four, keys_four, preferred_element_type=jnp.float32)
        * score_scale
    )
    row_max = jnp.max(scores, axis=-1, keepdims=True)
    weights = jnp.exp(scores - row_max)
    probabilities = weights / jnp.sum(weights, axis=-1, keepdims=True)
    probs_low = probabilities.astype(jnp.bfloat16)
    shifted_context = jnp.einsum(
        "chqk,ckhd->cqhd", probs_low, values_four, preferred_element_type=jnp.float32
    )
    shifted_context = shifted_context.astype(jnp.bfloat16).reshape(block_count * BLOCK, local_width)
    return (shifted_context, probabilities, keys_four, values_four)


def attend_backward(shifted_grads, probabilities, keys_four, values_four, head_count):
    block_count = keys_four.shape[0]
    local_width = shifted_grads.shape[1]
    score_scale = DH ** (-0.5)
    grads_four = shifted_grads.reshape(block_count, BLOCK, head_count, DH)
    prob_grad = jnp.einsum(
        "cqhd,ckhd->chqk", grads_four, values_four, preferred_element_type=jnp.float32
    )
    row_delta = jnp.sum(probabilities * prob_grad, axis=-1, keepdims=True)
    dscore = (probabilities * (prob_grad - row_delta) * score_scale).astype(jnp.bfloat16)
    shifted_qgrad = jnp.einsum(
        "chqk,ckhd->cqhd", dscore, keys_four, preferred_element_type=jnp.float32
    )
    return shifted_qgrad.astype(jnp.bfloat16).reshape(block_count * BLOCK, local_width)


def project_rows(flat_rows, key_full, value_full):
    keys_rows = jnp.dot(flat_rows, key_full, preferred_element_type=jnp.float32).astype(
        jnp.bfloat16
    )
    values_rows = jnp.dot(flat_rows, value_full, preferred_element_type=jnp.float32).astype(
        jnp.bfloat16
    )
    return jnp.concatenate([keys_rows, values_rows], axis=1)


def body(queries, context_grad, database, neighbour_ids, owner_map, key_weight, value_weight):
    margin = BLOCK - 1
    local_width = queries.shape[1]
    head_count = local_width // DH
    next_queries, next_grads = shifted((queries[:margin], context_grad[:margin]), "seq", -1)
    shifted_queries = jnp.concatenate([queries[margin:], next_queries], axis=0)
    shifted_grads = jnp.concatenate([context_grad[margin:], next_grads], axis=0)
    key_full, value_full = (
        lax.all_gather(key_weight, "seq", axis=0, tiled=True),
        lax.all_gather(value_weight, "seq", axis=0, tiled=True),
    )
    seq_count = lax.axis_size("seq")
    local_rows = database.shape[0]
    neigh_tokens = database.shape[1]
    enc_width = database.shape[2]
    request_ids = neighbour_ids.reshape(-1)
    ask_total = request_ids.shape[0]
    capacity = (ask_total + seq_count - 1) // seq_count
    row_labels = jnp.arange(owner_map.shape[0], dtype=jnp.int32)
    stored = jnp.sum(
        jnp.where(request_ids[:, None] == row_labels[None, :], owner_map[None, :], 0),
        axis=1,
        dtype=jnp.int32,
    )
    owner_index = stored // local_rows
    local_row = stored % local_rows
    positions = jnp.arange(ask_total, dtype=jnp.int32)
    same_owner = (owner_index[:, None] == owner_index[None, :]) & (
        positions[:, None] > positions[None, :]
    )
    slot_rank = jnp.sum(same_owner.astype(jnp.int32), axis=1, dtype=jnp.int32)
    slot_index = owner_index * capacity + slot_rank
    slot_labels = jnp.arange(seq_count * capacity, dtype=jnp.int32)
    asked_rows = jnp.sum(
        jnp.where(slot_index[:, None] == slot_labels[None, :], local_row[:, None], 0),
        axis=0,
        dtype=jnp.int32,
    )
    wanted = lax.all_to_all(
        asked_rows.reshape(seq_count, capacity), "seq", split_axis=0, concat_axis=0, tiled=True
    ).reshape(-1)
    projected = project_rows(database.reshape(-1, enc_width), key_full, value_full)
    projected = projected.reshape(local_rows, neigh_tokens, 2 * local_width)
    outgoing = projected[wanted].reshape(seq_count, capacity, neigh_tokens, 2 * local_width)
    incoming = lax.all_to_all(outgoing, "seq", split_axis=0, concat_axis=0, tiled=True)
    neighbour_kv = incoming.reshape(seq_count * capacity, neigh_tokens, 2 * local_width)[slot_index]
    block_count = queries.shape[0] // BLOCK
    neighbour_kv = neighbour_kv.reshape(block_count, -1, 2 * local_width)
    shifted_context, probabilities, keys_four, values_four = attend_forward(
        shifted_queries, neighbour_kv, head_count
    )
    shifted_qgrad = attend_backward(
        shifted_grads, probabilities, keys_four, values_four, head_count
    )
    prev_context, prev_qgrad = shifted(
        (shifted_context[-margin:], shifted_qgrad[-margin:]), "seq", 1
    )
    context = jnp.concatenate([prev_context, shifted_context[:-margin]], axis=0)
    query_grad = jnp.concatenate([prev_qgrad, shifted_qgrad[:-margin]], axis=0)
    return (context, query_grad)


def solution(mesh):
    return jax.shard_map(
        body,
        mesh=mesh,
        in_specs=(
            P("seq", "head"),
            P("seq", "head"),
            P("seq", None, None),
            P("seq", None),
            P(),
            P("seq", "head"),
            P("seq", "head"),
        ),
        out_specs=(P("seq", "head"), P("seq", "head")),
        check_vma=False,
    )
```

profile of v0, /device:TPU:24, one launch (start us, length us, event | category | flops | bytes accessed | tf_op | source)
XLA Modules:
  0.0 624.9 jit_solution(12890810908819356217)
XLA Ops:
  0.6 0.8 copy.50
  1.5 0.9 select_reduce_fusion
  2.7 0.7 copy.51
  3.4 18.7 %all-to-all-start = ((s32[64,1,1]{2,1,0:T(1,128)}), s32[64,1,1]{2,1,0:T(1,128)S(1)}, u32[]{:S(2)}, u32[]{:S(2)}) async-start(s32[64,1,1]{2,1,0:T(1,128)} %copy.51), calls=%async_computation | async-start | bytes 65536 | tf_op jit(solution)/shard_map/all_to_all | solution.py:102
  22.1 99.7 %all_gather.7 = bf16[1024,256]{1,0:T(8,128)(2,1)S(1)} all-gather(bf16[16,256]{1,0:T(8,128)(2,1)} %param.13), channel_id=1, replica_groups=mesh['seq'=64,'head'=8] {'seq'}, dimensions={0}, use_global_device_ids=true | all-gather | bytes 532480 | tf_op jit(solution)/shard_map/all_gather | solution.py:73
  121.8 135.6 %all_gather.6 = bf16[1024,256]{1,0:T(8,128)(2,1)S(1)} all-gather(bf16[16,256]{1,0:T(8,128)(2,1)} %param.12), channel_id=1, replica_groups=mesh['seq'=64,'head'=8] {'seq'}, dimensions={0}, use_global_device_ids=true | all-gather | bytes 532480 | tf_op jit(solution)/shard_map/all_gather | solution.py:72
  257.4 3.6 convolution_convert_fusion
  261.0 1.3 convolution_convert_fusion.1
  262.3 1.5 pad_maximum_fusion
  263.8 2.9 copy.68
  266.7 1.2 reduce
  267.9 5.5 gather_fusion
  273.4 6.1 all-to-all-start.1
  279.5 4.9 collective-permute-start
  284.4 3.5 collective-permute-start.2
  288.2 269.8 %collective-permute-done = bf16[63,256]{1,0:T(8,128)(2,1)S(1)} collective-permute-done((bf16[63,256]{1,0:T(8,128)(2,1)S(1)}, bf16[63,256]{1,0:T(8,128)(2,1)S(1)}, u32[]{:S(2)}, u32[]{:S(2)}) %collective-permute-start) | collective-permute-done | bytes 32288 | tf_op jit(solution)/shard_map/ppermute | solution.py:13
  558.2 0.6 collective-permute-done.2
  559.0 3.3 all-to-all-done.1
  562.2 6.2 gather_fusion.1
  568.4 3.9 fusion.33
  572.3 2.4 copy.70
  574.6 2.0 fusion.21
  576.7 2.0 fusion.34
  578.7 3.9 copy.69
  582.6 3.3 fusion.19
  585.9 15.3 %fusion.13 = bf16[16,64,2,128]{3,1,2,0:T(8,128)(2,1)S(1)} fusion(bf16[16,256,2,128]{1,3,2,0:T(8,128)(2,1)} %bitcast.58, f32[16,2,64,256]{3,2,1,0:T(8,128)} %fusion.19, f32[16,2,64,256]{3,2,1,0:T(8,128)} %get-tuple-element.7, f32[16,2,64]{2,1,0:T(2,128)S(1)} %get-tuple-element.6), kind=kOutput, calls=%fused_computation.17 | convolution fusion | flops 138152192 | bytes 6823936 | tf_op jit(solution)/shard_map/chqk,ckhd->cqhd/dot_general | solution.py:48
  601.9 8.2 %collective-permute-start.3 = (bf16[63,256]{1,0:T(8,128)(2,1)S(1)}, bf16[63,256]{1,0:T(8,128)(2,1)S(1)}, u32[]{:S(2)}, u32[]{:S(2)}) collective-permute-start(bf16[63,256]{1,0:T(8,128)(2,1)S(1)} %slice.48), channel_id=1, source_target_pairs={{0,8},{8,16},{16,24},{24,32},{32,40},{40,48},{48,56},{56,64},{64,7... | collective-permute-start | bytes 96776 | tf_op jit(solution)/shard_map/ppermute | solution.py:13
  610.0 5.2 fusion.12
  616.0 1.9 collective-permute-start.1
  618.0 0.9 pad_maximum_fusion.4
  618.9 5.1 collective-permute-done.1
  624.0 0.9 pad_maximum_fusion.2
  (33 shorter events, 2.4 us)
Async XLA Ops:
  3.4 263.3 %all-to-all-start = ((s32[64,1,1]{2,1,0:T(1,128)}), s32[64,1,1]{2,1,0:T(1,128)S(1)}, u32[]{:S(2)}, u32[]{:S(2)}) async-start(s32[64,1,1]{2,1,0:T(1,128)} %copy.51), calls=%async_computation | async-start | bytes 65536 | tf_op jit(solution)/shard_map/all_to_all | solution.py:102
  257.4 3.6 copy-start.2
  273.4 6.1 copy-start
  273.4 11.0 %copy-start.1 = (bf16[1024,256]{1,0:T(8,128)(2,1)S(1)}, bf16[1024,256]{1,0:T(8,128)(2,1)}, u32[]{:S(2)}) copy-start(bf16[1024,256]{1,0:T(8,128)(2,1)} %param.8) | copy-start | bytes 1572868
  273.4 288.8 %all-to-all-start.1 = ((bf16[64,1,128,512]{3,2,1,0:T(8,128)(2,1)}), bf16[64,1,128,512]{3,2,1,0:T(8,128)(2,1)}, u32[]{:S(2)}, u32[]{:S(2)}) async-start(bf16[64,1,128,512]{3,2,1,0:T(8,128)(2,1)} %bitcast.53), calls=%async_computation.1 | async-start | bytes 16777216 | tf_op jit(solution)/shard_map/all_to_all | solution.py:108
  279.5 278.5 %collective-permute-start = (bf16[63,256]{1,0:T(8,128)(2,1)S(1)}, bf16[63,256]{1,0:T(8,128)(2,1)S(1)}, u32[]{:S(2)}, u32[]{:S(2)}) collective-permute-start(bf16[63,256]{1,0:T(8,128)(2,1)S(1)} %slice.32), channel_id=1, source_target_pairs={{8,0},{16,8},{24,16},{32,24},{40,32},{48,40},{56,48},{64,56},{72,6... | collective-permute-start | bytes 96776 | tf_op jit(solution)/shard_map/ppermute | solution.py:13
  284.4 274.4 %collective-permute-start.2 = (bf16[63,256]{1,0:T(8,128)(2,1)S(1)}, bf16[63,256]{1,0:T(8,128)(2,1)S(1)}, u32[]{:S(2)}, u32[]{:S(2)}) collective-permute-start(bf16[63,256]{1,0:T(8,128)(2,1)S(1)} %slice.37), channel_id=1, source_target_pairs={{8,0},{16,8},{24,16},{32,24},{40,32},{48,40},{56,48},{64,56},{72,6... | collective-permute-start | bytes 96776 | tf_op jit(solution)/shard_map/ppermute | solution.py:13
  601.9 16.1 %collective-permute-start.3 = (bf16[63,256]{1,0:T(8,128)(2,1)S(1)}, bf16[63,256]{1,0:T(8,128)(2,1)S(1)}, u32[]{:S(2)}, u32[]{:S(2)}) collective-permute-start(bf16[63,256]{1,0:T(8,128)(2,1)S(1)} %slice.48), channel_id=1, source_target_pairs={{0,8},{8,16},{16,24},{24,32},{32,40},{40,48},{48,56},{56,64},{64,7... | collective-permute-start | bytes 96776 | tf_op jit(solution)/shard_map/ppermute | solution.py:13
  616.0 7.9 %collective-permute-start.1 = (bf16[63,256]{1,0:T(8,128)(2,1)S(1)}, bf16[63,256]{1,0:T(8,128)(2,1)S(1)}, u32[]{:S(2)}, u32[]{:S(2)}) collective-permute-start(bf16[63,256]{1,0:T(8,128)(2,1)S(1)} %slice.46), channel_id=1, source_target_pairs={{0,8},{8,16},{16,24},{24,32},{32,40},{40,48},{48,56},{56,64},{64,7... | collective-permute-start | bytes 96776 | tf_op jit(solution)/shard_map/ppermute | solution.py:13
where the time goes:
time: 626 us; the launch traced here: 625 us
  waiting for transfers between devices  279 us (45%)
  blocking collectives  235 us (38%)
  starting transfers between devices  43.3 us (7%)
  matrix products  30.8 us (5%)
  local copies, waits for them, and re-layouts  28.1 us (4%)
  other arithmetic  7.83 us (1%)
    ppermute x4, waiting for transfers between devices, shifted(): lax.ppermute(value, axis, [(source, source + steps) for source in range(f...  275 us
    all_gather x1, blocking collectives, body(): lax.all_gather(key_weight, 'seq', axis=0, tiled=True)  136 us
    all_gather x1, blocking collectives, body(): lax.all_gather(value_weight, 'seq', axis=0, tiled=True)  99.7 us
    all_to_all x1, starting transfers between devices, body(): lax.all_to_all(asked_rows.reshape(seq_count, capacity), 'seq', split_axis...  18.7 us
    ppermute x4, starting transfers between devices, shifted(): lax.ppermute(value, axis, [(source, source + steps) for source in range(f...  18.5 us
    dot_general x1, matrix products, attend_backward(): jnp.einsum('chqk,ckhd->cqhd', dscore, keys_four, preferred_element_type=j...  15.3 us
  transfers between devices with their start and end apart: 6, of which 4 were waited for; matrix products, arithmetic and copies ran while one was open for 3% of the time, Pallas kernels for 0%

commit v1 on v0

v1 whole, which is shorter than its diff:
```python
import jax
import jax.numpy as jnp
from jax import lax
from jax.experimental import pallas as pl
from jax.experimental.pallas import tpu as pltpu
from jax.sharding import PartitionSpec as P

DH = 128
BLOCK = 64
Z = 16
PIECES = (512, 512)
GROUP = 4


def shifted(value, axis, steps):
    count = lax.axis_size(axis)
    first, last = (max(0, -steps), min(count, count - steps))
    return lax.ppermute(value, axis, [(source, source + steps) for source in range(first, last)])


def attend(query, grad, key, value):
    scale = DH ** (-0.5)
    last = (((1,), (1,)), ((), ()))
    scores = lax.dot_general(query, key, last, preferred_element_type=jnp.float32) * scale
    prob_grad = lax.dot_general(grad, value, last, preferred_element_type=jnp.float32)
    weights = jnp.exp(scores - jnp.max(scores, axis=-1, keepdims=True))
    probabilities = weights / jnp.sum(weights, axis=-1, keepdims=True)
    context = jnp.dot(
        probabilities.astype(jnp.bfloat16), value, preferred_element_type=jnp.float32
    )
    delta = jnp.sum(probabilities * prob_grad, axis=-1, keepdims=True)
    dscore = (probabilities * (prob_grad - delta) * scale).astype(jnp.bfloat16)
    qgrad = jnp.dot(dscore, key, preferred_element_type=jnp.float32)
    return context, qgrad


def project(piece_refs, weight_ref, kv_ref):
    total = None
    start = 0
    for piece_ref in piece_refs:
        width = piece_ref.shape[-1]
        rows = piece_ref[...].reshape(-1, width)
        term = jnp.dot(
            rows, weight_ref[start : start + width, :], preferred_element_type=jnp.float32
        )
        total = term if total is None else total + term
        start += width
    kv_ref[...] = total.astype(jnp.bfloat16).reshape(kv_ref.shape)


def attend_block(at, query_ref, grad_ref, kv_ref):
    width = query_ref.shape[1]
    rows = pl.ds(at * BLOCK, BLOCK)
    contexts, qgrads = [], []
    for head in range(width // DH):
        own = slice(head * DH, (head + 1) * DH)
        theirs = slice(width + head * DH, width + (head + 1) * DH)
        key = kv_ref[:, at, :, own].reshape(-1, DH)
        value = kv_ref[:, at, :, theirs].reshape(-1, DH)
        context, qgrad = attend(query_ref[rows, own], grad_ref[rows, own], key, value)
        contexts.append(pltpu.roll(context, BLOCK - 1, 0))
        qgrads.append(pltpu.roll(qgrad, BLOCK - 1, 0))
    return jnp.concatenate(contexts, axis=1), jnp.concatenate(qgrads, axis=1)


def halo_kernel(query_ref, grad_ref, *refs):
    *piece_refs, weight_ref, halo_ref, kv_ref = refs
    project(piece_refs, weight_ref, kv_ref)
    context, qgrad = attend_block(0, query_ref, grad_ref, kv_ref)
    halo_ref[:BLOCK, :] = context.astype(jnp.bfloat16)
    halo_ref[BLOCK:, :] = qgrad.astype(jnp.bfloat16)


def main_kernel(query_ref, grad_ref, *refs):
    *piece_refs, weight_ref, context_ref, qgrad_ref, kv_ref, carry_ref = refs

    @pl.when(pl.program_id(0) == 0)
    def _():
        carry_ref[...] = jnp.zeros_like(carry_ref)

    project(piece_refs, weight_ref, kv_ref)
    row = lax.broadcasted_iota(jnp.int32, (BLOCK, query_ref.shape[1]), 0)
    before = carry_ref[0], carry_ref[1]
    for at in range(kv_ref.shape[1]):
        now = attend_block(at, query_ref, grad_ref, kv_ref)
        for out_ref, old, new in zip((context_ref, qgrad_ref), before, now):
            tile = jnp.where(row < BLOCK - 1, old, new)
            out_ref[at * BLOCK : (at + 1) * BLOCK, :] = tile.astype(jnp.bfloat16)
        before = now
    carry_ref[0], carry_ref[1] = before


def first_rows_kernel(halo_ref, context_ref, qgrad_ref, context_out, qgrad_out):
    row = lax.broadcasted_iota(jnp.int32, context_ref.shape, 0)
    for at, (old, out) in enumerate(((context_ref, context_out), (qgrad_ref, qgrad_out))):
        new = halo_ref[at * BLOCK : (at + 1) * BLOCK, :].astype(jnp.float32)
        tile = jnp.where(row < BLOCK - 1, new, old[...].astype(jnp.float32))
        out[...] = tile.astype(jnp.bfloat16)


def attention(shifted_queries, shifted_grads, pieces, weight):
    tokens, width = shifted_queries.shape
    parts, blocks, part_tokens, _ = pieces[0].shape
    enc_width = weight.shape[0]
    params = pltpu.CompilerParams(vmem_limit_bytes=48 * 1024 * 1024)

    def operands(group, first):
        place = pl.BlockSpec((group * BLOCK, width), lambda i: (i + first, 0))
        return [place, place] + [
            pl.BlockSpec((parts, group, part_tokens, p.shape[-1]), lambda i: (0, i + first, 0, 0))
            for p in pieces
        ] + [pl.BlockSpec((enc_width, 2 * width), lambda i: (0, 0))]

    def cost(count):
        keys = parts * part_tokens
        return pl.CostEstimate(
            flops=count * 2 * keys * 2 * width * (enc_width + 2 * BLOCK),
            bytes_accessed=count * 2 * (keys * enc_width + 4 * BLOCK * width)
            + 4 * enc_width * width,
            transcendentals=count * keys * BLOCK * width // DH,
        )

    def kv_scratch(group):
        return pltpu.VMEM((parts, group, part_tokens, 2 * width), jnp.bfloat16)

    inputs = (shifted_queries, shifted_grads, *pieces, weight)
    halo = pl.pallas_call(
        halo_kernel,
        grid=(1,),
        out_shape=jax.ShapeDtypeStruct((2 * BLOCK, width), jnp.bfloat16),
        in_specs=operands(1, blocks - 1),
        out_specs=pl.BlockSpec((2 * BLOCK, width), lambda i: (0, 0)),
        scratch_shapes=[kv_scratch(1)],
        compiler_params=params,
        cost_estimate=cost(1),
        name="last_block",
    )(*inputs)
    halo = shifted(halo, "seq", 1)
    out = jax.ShapeDtypeStruct((tokens, width), jnp.bfloat16)
    place = pl.BlockSpec((GROUP * BLOCK, width), lambda i: (i, 0))
    context, query_grad = pl.pallas_call(
        main_kernel,
        grid=(blocks // GROUP,),
        out_shape=(out, out),
        in_specs=operands(GROUP, 0),
        out_specs=(place, place),
        scratch_shapes=[kv_scratch(GROUP), pltpu.VMEM((2, BLOCK, width), jnp.float32)],
        compiler_params=params,
        cost_estimate=cost(blocks),
        name="blocks",
    )(*inputs)
    place = pl.BlockSpec((BLOCK, width), lambda i: (0, 0))
    return pl.pallas_call(
        first_rows_kernel,
        grid=(1,),
        out_shape=(out, out),
        in_specs=[pl.BlockSpec((2 * BLOCK, width), lambda i: (0, 0)), place, place],
        out_specs=(place, place),
        input_output_aliases={1: 0, 2: 1},
        name="first_rows",
    )(halo, context, query_grad)


def body(queries, context_grad, database, neighbour_ids, owner_map, key_weight, value_weight):
    margin = BLOCK - 1
    seq_count = lax.axis_size("seq")
    head_devices = lax.axis_size("head")
    y_count = seq_count // Z
    local_rows, neigh_tokens, enc_width = database.shape
    part_tokens = neigh_tokens // head_devices
    my_head = lax.axis_index("head")

    request_ids = neighbour_ids.reshape(-1)
    row_labels = jnp.arange(owner_map.shape[0], dtype=jnp.int32)
    stored = jnp.sum(
        jnp.where(request_ids[:, None] == row_labels[None, :], owner_map[None, :], 0),
        axis=1,
        dtype=jnp.int32,
    )
    owner_index = stored // local_rows
    local_row = stored % local_rows
    slot_labels = jnp.arange(seq_count, dtype=jnp.int32)
    asked_rows = jnp.sum(
        jnp.where(owner_index[:, None] == slot_labels[None, :], local_row[:, None], 0),
        axis=0,
        dtype=jnp.int32,
    )
    wanted = lax.all_to_all(
        asked_rows.reshape(seq_count, 1), "seq", split_axis=0, concat_axis=0, tiled=True
    ).reshape(-1)

    weight = jnp.concatenate([key_weight, value_weight], axis=1)
    along_z = [[y * Z + z for z in range(Z)] for y in range(y_count)]
    along_y = [[y * Z + z for y in range(y_count)] for z in range(Z)]
    weight = lax.all_gather(weight, "seq", axis=0, tiled=True, axis_index_groups=along_z)
    first_rows = shifted(
        jnp.concatenate([queries[:margin], context_grad[:margin]], axis=1), "seq", -1
    )

    parts = database.reshape(local_rows, head_devices, part_tokens, enc_width)
    mine = lax.dynamic_index_in_dim(parts, my_head, axis=1, keepdims=False)
    wanted, weight, first_rows = lax.optimization_barrier((wanted, weight, first_rows))
    weight = lax.all_gather(weight, "seq", axis=0, tiled=True, axis_index_groups=along_y)
    pieces = []
    start = 0
    for width in PIECES:
        outgoing = mine[:, :, start : start + width][wanted]
        incoming = lax.all_to_all(outgoing, "seq", split_axis=0, concat_axis=0, tiled=True)
        asked = incoming[owner_index]
        rows = lax.all_gather(asked, "head", axis=0, tiled=False)
        pieces.append(rows.reshape(head_devices, -1, 2 * part_tokens, width))
        start += width

    width = queries.shape[1]
    shifted_queries = jnp.concatenate([queries[margin:], first_rows[:, :width]], axis=0)
    shifted_grads = jnp.concatenate([context_grad[margin:], first_rows[:, width:]], axis=0)
    return attention(shifted_queries, shifted_grads, pieces, weight)


def solution(mesh):
    return jax.shard_map(
        body,
        mesh=mesh,
        in_specs=(
            P("seq", "head"),
            P("seq", "head"),
            P("seq", None, None),
            P("seq", None),
            P(),
            P("seq", "head"),
            P("seq", "head"),
        ),
        out_specs=(P("seq", "head"), P("seq", "head")),
        check_vma=False,
    )
```

time: 626 us -> 254 us (0.41)
  waiting for transfers between devices: 279 us -> 77.5 us
  blocking collectives: 235 us -> 84.8 us
  matrix products: 30.8 us -> 0 us
  Pallas kernels: 0 us -> 22.1 us
  local copies, waits for them, and re-layouts: 28.1 us -> 11.3 us
  between operations: 0.9 us -> 13.9 us
    ppermute x4 -> x2, waiting for transfers between devices: 275 us -> 0.01 us  [shifted(): lax.ppermute(value, axis, [(source, source + steps) for source in range(f...]
    all_gather x2 -> x1, blocking collectives: 235 us -> 31.6 us  [body(): lax.all_gather(weight, 'seq', axis=0, tiled=True, axis_index_groups=along_z)]
    all_to_all x0 -> x1, blocking collectives: none -> 53.1 us  [body(): lax.all_to_all(outgoing, 'seq', split_axis=0, concat_axis=0, tiled=True)]
    all_to_all x1, waiting for transfers between devices: 3.25 us -> 43.7 us  [body(): lax.all_to_all(outgoing, 'seq', split_axis=0, concat_axis=0, tiled=True)]
    all_gather x0 -> x3, waiting for transfers between devices: none -> 33.1 us  [the longest x2 33.1 us: body(): rows = lax.all_gather(asked, 'head', axis=0, tiled=False)]
    dot_general x6 -> x0, matrix products: 30.8 us -> none  [the longest x1 15.3 us: attend_backward(): jnp.einsum('chqk,ckhd->cqhd', dscore, keys_four, preferred_element_type=j...]
    pallas_call x0 -> x3, Pallas kernels: none -> 22.1 us  [the longest x1 18.3 us: attention(): pl.pallas_call(main_kernel, grid=(blocks // GROUP,), out_shape=(out, out)...]
    ppermute x4 -> x2, starting transfers between devices: 18.5 us -> 8.33 us  [shifted(): lax.ppermute(value, axis, [(source, source + steps) for source in range(f...]
  transfers between devices with their start and end apart: 6 -> 7, of which waited for: 4 -> 2; matrix products, arithmetic and copies ran while one was open for 3% -> 3% of each run, Pallas kernels for 0% -> 7%
where the time goes in v1:
time: 254 us; the launch traced here: 252 us
  blocking collectives  84.8 us (33%)
  waiting for transfers between devices  77.5 us (31%)
  starting transfers between devices  39.6 us (16%)
  Pallas kernels  22.1 us (9%)
  between operations  13.9 us (5%)
  local copies, waits for them, and re-layouts  11.3 us (4%)
  other arithmetic  3.1 us (1%)
    all_to_all x1, blocking collectives, body(): lax.all_to_all(outgoing, 'seq', split_axis=0, concat_axis=0, tiled=True)  53.1 us
    all_to_all x1, waiting for transfers between devices, body(): lax.all_to_all(outgoing, 'seq', split_axis=0, concat_axis=0, tiled=True)  43.7 us
    all_gather x2, waiting for transfers between devices, body(): rows = lax.all_gather(asked, 'head', axis=0, tiled=False)  33.1 us
    all_gather x1, blocking collectives, body(): lax.all_gather(weight, 'seq', axis=0, tiled=True, axis_index_groups=along_z)  31.6 us
    all_to_all x1, starting transfers between devices, body(): lax.all_to_all(asked_rows.reshape(seq_count, 1), 'seq', split_axis=0, con...  18.7 us
    pallas_call x1, Pallas kernels, attention(): pl.pallas_call(main_kernel, grid=(blocks // GROUP,), out_shape=(out, out)...  18.3 us
    all_to_all x1, starting transfers between devices, body(): lax.all_to_all(outgoing, 'seq', split_axis=0, concat_axis=0, tiled=True)  12.4 us
    ppermute x2, starting transfers between devices, shifted(): lax.ppermute(value, axis, [(source, source + steps) for source in range(f...  8.33 us
  transfers between devices with their start and end apart: 7, of which 2 were waited for; matrix products, arithmetic and copies ran while one was open for 3% of the time, Pallas kernels for 7%

profile of v1, /device:TPU:24, one launch (start us, length us, event | category | flops | bytes accessed | tf_op | source)
XLA Modules:
  0.0 252.3 jit_solution(8101377507552918659)
XLA Ops:
  7.2 0.8 copy.17
  7.9 0.1 eq.30
  8.0 0.9 select_reduce_fusion
  8.9 0.1 select_reduce_fusion.1
  9.0 0.7 copy.18
  9.7 18.7 %all-to-all-start = ((s32[64,1,1]{2,1,0:T(1,128)}), s32[64,1,1]{2,1,0:T(1,128)S(1)}, u32[]{:S(2)}, u32[]{:S(2)}) async-start(s32[64,1,1]{2,1,0:T(1,128)} %copy.18), calls=%async_computation | async-start | bytes 65536 | tf_op jit(solution)/shard_map/all_to_all | solution.py:188
  28.4 0.8 slice.25
  29.2 0.8 slice.26
  30.0 4.9 %collective-permute-start = (bf16[63,512]{1,0:T(8,128)(2,1)S(1)}, bf16[63,512]{1,0:T(8,128)(2,1)S(1)}, u32[]{:S(2)}, u32[]{:S(2)}) collective-permute-start(bf16[63,512]{1,0:T(8,128)(2,1)S(1)} %pad_maximum_fusion.2), channel_id=1, source_target_pairs={{8,0},{16,8},{24,16},{32,24},{40,32},{48,40},{56,48},{64,56},{72,6... | collective-permute-start | bytes 193544 | tf_op jit(solution)/shard_map/ppermute | solution.py:18
  34.8 1.1 dynamic-slice_bitcast_fusion
  35.9 0.1 fusion.1
  36.0 0.7 pad_maximum_fusion.3
  36.7 31.6 %all_gather.18 = bf16[256,512]{1,0:T(8,128)(2,1)} all-gather(bf16[16,512]{1,0:T(8,128)(2,1)S(1)} %pad_maximum_fusion.3), channel_id=1, replica_groups={{0,8,16,24,32,40,48,56,64,72,80,88,96,104,112,120},{128,136,144,152,160..., dimensions={0}, use_global_device_ids=true | all-gather | bytes 278528 | tf_op jit(solution)/shard_map/all_gather | solution.py:195
  68.4 1.2 reduce
  69.6 1.6 gather_fusion
  71.2 12.4 %all-to-all-start.1 = ((bf16[64,16,512]{2,1,0:T(8,128)(2,1)}), bf16[64,16,512]{2,1,0:T(8,128)(2,1)S(1)}, u32[]{:S(2)}, u32[]{:S(2)}) async-start(bf16[64,16,512]{2,1,0:T(8,128)(2,1)} %gather_fusion), calls=%async_computation.1 | async-start | bytes 2097152 | tf_op jit(solution)/shard_map/all_to_all | solution.py:208
  83.7 0.7 all-gather.6.cloned.1.call-update
  84.5 43.7 %all-to-all-done.1 = bf16[64,16,512]{2,1,0:T(8,128)(2,1)S(1)} async-done(((bf16[64,16,512]{2,1,0:T(8,128)(2,1)}), bf16[64,16,512]{2,1,0:T(8,128)(2,1)S(1)}, u32[]{:S(2)}, u32[]{:S(2)}) %all-to-all-start.1) | async-done | bytes 1048608 | tf_op jit(solution)/shard_map/all_to_all | solution.py:208
  128.1 1.4 gather_fusion.1
  129.6 0.6 gather_fusion.2
  130.2 53.1 %all_to_all.19 = bf16[64,16,512]{2,1,0:T(8,128)(2,1)S(1)} all-to-all(bf16[64,16,512]{2,1,0:T(8,128)(2,1)S(1)} %gather_fusion.2), channel_id=1, replica_groups=mesh['seq'=64,'head'=8] {'seq'}, dimensions={0} | all-to-all | bytes 2097152 | tf_op jit(solution)/shard_map/all_to_all | solution.py:208
  183.3 1.4 gather_fusion.3
  184.7 0.1 slice.24
  184.9 0.1 slice.28
  185.0 0.1 pad_maximum_fusion
  185.2 33.1 %all-gather.10.cloned.1.call-done = bf16[256,16,512]{2,1,0:T(8,128)(2,1)} async-done(((bf16[32,16,512]{2,1,0:T(8,128)(2,1)}), bf16[256,16,512]{2,1,0:T(8,128)(2,1)}) %all-gather.10.cloned.1.call-update) | async-done | bytes 4194320 | tf_op jit(solution)/shard_map/all_gather | solution.py:210
  218.3 1.2 copy-done
  219.5 2.3 last_block.1
  221.9 3.5 %collective-permute-start.1 = (bf16[128,256]{1,0:T(8,128)(2,1)S(1)}, bf16[128,256]{1,0:T(8,128)(2,1)S(1)}, u32[]{:S(2)}, u32[]{:S(2)}) collective-permute-start(bf16[128,256]{1,0:T(8,128)(2,1)S(1)} %last_block.1), channel_id=1, source_target_pairs={{0,8},{8,16},{16,24},{24,32},{32,40},{40,48},{48,56},{56,64},{64,7... | collective-permute-start | bytes 196616 | tf_op jit(solution)/shard_map/ppermute | solution.py:18
  225.3 18.3 %blocks.1 = (bf16[1024,256]{1,0:T(8,128)(2,1)}, bf16[1024,256]{1,0:T(8,128)(2,1)}) custom-call(bf16[1024,256]{1,0:T(8,128)(2,1)S(1)} %get-tuple-element.18.query_ref, bf16[1024,256]{1,0:T(8,128)(2,1)S(1)} %get-tuple-element.19.grad_ref, bf16[8,16,32,512]{3,2,1,0:T(8,128)(2,1)} %bitcast.19, bf16[8,16,32,512]{3,2,1,0:T(8,128)(2,1)} %bitcast.21, ...), custom_call_target="tpu_custom_call" | custom-call | flops 4831838208 | bytes 11534336 | tf_op jit(solution)/shard_map/blocks/pallas_call | solution.py:141
  243.7 0.6 copy-done.3
  244.3 1.5 first_rows.1
  (23 shorter events, 0.3 us)
Async XLA Ops:
  9.7 58.6 %all-to-all-start = ((s32[64,1,1]{2,1,0:T(1,128)}), s32[64,1,1]{2,1,0:T(1,128)S(1)}, u32[]{:S(2)}, u32[]{:S(2)}) async-start(s32[64,1,1]{2,1,0:T(1,128)} %copy.18), calls=%async_computation | async-start | bytes 65536 | tf_op jit(solution)/shard_map/all_to_all | solution.py:188
  30.0 39.6 %collective-permute-start = (bf16[63,512]{1,0:T(8,128)(2,1)S(1)}, bf16[63,512]{1,0:T(8,128)(2,1)S(1)}, u32[]{:S(2)}, u32[]{:S(2)}) collective-permute-start(bf16[63,512]{1,0:T(8,128)(2,1)S(1)} %pad_maximum_fusion.2), channel_id=1, source_target_pairs={{8,0},{16,8},{24,16},{32,24},{40,32},{48,40},{56,48},{64,56},{72,6... | collective-permute-start | bytes 193544 | tf_op jit(solution)/shard_map/ppermute | solution.py:18
  71.2 56.9 %all-to-all-start.1 = ((bf16[64,16,512]{2,1,0:T(8,128)(2,1)}), bf16[64,16,512]{2,1,0:T(8,128)(2,1)S(1)}, u32[]{:S(2)}, u32[]{:S(2)}) async-start(bf16[64,16,512]{2,1,0:T(8,128)(2,1)} %gather_fusion), calls=%async_computation.1 | async-start | bytes 2097152 | tf_op jit(solution)/shard_map/all_to_all | solution.py:208
  83.6 101.1 %copy-start.1 = (bf16[1024,256]{1,0:T(8,128)(2,1)S(1)}, bf16[1024,256]{1,0:T(8,128)(2,1)}, u32[]{:S(2)}) copy-start(bf16[1024,256]{1,0:T(8,128)(2,1)} %param.7) | copy-start | bytes 1572868
  83.6 101.5 %all-gather.6.cloned.1.call-start = ((), (), s32[]{:S(2)}) async-start(), calls=%async_computation.3 | async-start | bytes 1310720 | tf_op jit(solution)/shard_map/all_gather | solution.py:203
  84.4 100.5 %copy-start.2 = (bf16[1024,256]{1,0:T(8,128)(2,1)S(1)}, bf16[1024,256]{1,0:T(8,128)(2,1)}, u32[]{:S(2)}) copy-start(bf16[1024,256]{1,0:T(8,128)(2,1)} %param.8) | copy-start | bytes 1572868
  84.4 100.8 %all-gather.8.cloned.1.call-start = ((), (), s32[]{:S(2)}) async-start(), calls=%async_computation.4 | async-start | bytes 4718592 | tf_op jit(solution)/shard_map/all_gather | solution.py:210
  129.5 88.8 %all-gather.10.cloned.1.call-start = ((), (), s32[]{:S(2)}) async-start(), calls=%async_computation.5 | async-start | bytes 4718592 | tf_op jit(solution)/shard_map/all_gather | solution.py:210
  218.3 1.2 copy-start
  221.9 21.8 %collective-permute-start.1 = (bf16[128,256]{1,0:T(8,128)(2,1)S(1)}, bf16[128,256]{1,0:T(8,128)(2,1)S(1)}, u32[]{:S(2)}, u32[]{:S(2)}) collective-permute-start(bf16[128,256]{1,0:T(8,128)(2,1)S(1)} %last_block.1), channel_id=1, source_target_pairs={{0,8},{8,16},{16,24},{24,32},{32,40},{40,48},{48,56},{56,64},{64,7... | collective-permute-start | bytes 196616 | tf_op jit(solution)/shard_map/ppermute | solution.py:18
  243.7 0.6 copy-start.3
Sparse Core Ops, SparseCore 0:
  86.6 33.7 all-gather.5
  129.7 34.0 all-gather.7
  184.9 33.4 all-gather.9

commit v2 on v0

v2 whole, which is shorter than its diff:
```python
import jax
import jax.numpy as jnp
from jax import lax
from jax.experimental import pallas as pl
from jax.experimental.pallas import tpu as pltpu
from jax.sharding import PartitionSpec as P

DH = 128
BLOCK = 64


def shifted(value, axis, steps):
    count = lax.axis_size(axis)
    first, last = (max(0, -steps), min(count, count - steps))
    return lax.ppermute(value, axis, [(source, source + steps) for source in range(first, last)])


def attend(query, grad, key, value):
    scale = DH ** (-0.5)
    last = (((1,), (1,)), ((), ()))
    scores = lax.dot_general(query, key, last, preferred_element_type=jnp.float32) * scale
    prob_grad = lax.dot_general(grad, value, last, preferred_element_type=jnp.float32)
    weights = jnp.exp(scores - jnp.max(scores, axis=-1, keepdims=True))
    probabilities = weights / jnp.sum(weights, axis=-1, keepdims=True)
    context = jnp.dot(
        probabilities.astype(jnp.bfloat16), value, preferred_element_type=jnp.float32
    )
    delta = jnp.sum(probabilities * prob_grad, axis=-1, keepdims=True)
    dscore = (probabilities * (prob_grad - delta) * scale).astype(jnp.bfloat16)
    qgrad = jnp.dot(dscore, key, preferred_element_type=jnp.float32)
    return context.astype(jnp.bfloat16), qgrad.astype(jnp.bfloat16)


def attend_kernel(tokens_ref, rows_ref, weight_ref, out_ref, kv_ref):
    width = tokens_ref.shape[2] // 2
    rows = rows_ref[...].reshape(-1, rows_ref.shape[-1])
    kv = jnp.dot(rows, weight_ref[0], preferred_element_type=jnp.float32)
    kv_ref[...] = kv.astype(jnp.bfloat16).reshape(kv_ref.shape)
    for at in range(rows_ref.shape[1]):
        place = slice(at * BLOCK, (at + 1) * BLOCK)
        for head in range(width // DH):
            own = slice(head * DH, (head + 1) * DH)
            other = slice(width + head * DH, width + (head + 1) * DH)
            key = kv_ref[:, at, :, own].reshape(-1, DH)
            value = kv_ref[:, at, :, other].reshape(-1, DH)
            context, qgrad = attend(
                tokens_ref[0, place, own], tokens_ref[0, place, other], key, value
            )
            out_ref[0, place, own] = context
            out_ref[0, place, other] = qgrad


def attention(tokens, rows, weights):
    parts, count, double = tokens.shape
    row_parts, blocks, part_tokens, enc_width = rows.shape
    keys = row_parts * part_tokens
    place = pl.BlockSpec((1, count, double), lambda i: (i, 0, 0))
    return pl.pallas_call(
        attend_kernel,
        grid=(parts,),
        out_shape=jax.ShapeDtypeStruct(tokens.shape, jnp.bfloat16),
        in_specs=[
            place,
            pl.BlockSpec(rows.shape, lambda i: (0, 0, 0, 0)),
            pl.BlockSpec((1, enc_width, double), lambda i: (i, 0, 0)),
        ],
        out_specs=place,
        scratch_shapes=[pltpu.VMEM((row_parts, blocks, part_tokens, double), jnp.bfloat16)],
        compiler_params=pltpu.CompilerParams(vmem_limit_bytes=56 * 1024 * 1024),
        cost_estimate=pl.CostEstimate(
            flops=2 * parts * blocks * keys * double * (enc_width + 2 * BLOCK),
            bytes_accessed=2 * (2 * tokens.size + rows.size + weights.size),
            transcendentals=parts * blocks * keys * BLOCK * double // (2 * DH),
        ),
        name="blocks",
    )(tokens, rows, weights)


def body(queries, context_grad, database, neighbour_ids, owner_map, key_weight, value_weight):
    margin = BLOCK - 1
    width = queries.shape[1]
    seq_count = lax.axis_size("seq")
    head_devices = lax.axis_size("head")
    local_rows, neigh_tokens, enc_width = database.shape
    part_tokens = neigh_tokens // head_devices
    my_head = lax.axis_index("head")

    weight = jnp.concatenate([key_weight, value_weight], axis=1)
    weight = lax.all_gather(weight, "seq", axis=0, tiled=True)
    weights = lax.all_gather(weight, "head", axis=0, tiled=False)

    request_ids = neighbour_ids.reshape(-1)
    row_labels = jnp.arange(owner_map.shape[0], dtype=jnp.int32)
    stored = jnp.sum(
        jnp.where(request_ids[:, None] == row_labels[None, :], owner_map[None, :], 0),
        axis=1,
        dtype=jnp.int32,
    )
    owner_index = stored // local_rows
    local_row = stored % local_rows
    slot_labels = jnp.arange(seq_count, dtype=jnp.int32)
    asked_rows = jnp.sum(
        jnp.where(owner_index[:, None] == slot_labels[None, :], local_row[:, None], 0),
        axis=0,
        dtype=jnp.int32,
    )
    wanted = lax.all_to_all(
        asked_rows.reshape(seq_count, 1), "seq", split_axis=0, concat_axis=0, tiled=True
    ).reshape(-1)

    tokens = jnp.concatenate([queries, context_grad], axis=1)
    tokens = jnp.concatenate([tokens[margin:], shifted(tokens[:margin], "seq", -1)], axis=0)
    tokens = lax.all_to_all(
        tokens.reshape(head_devices, -1, 2 * width), "head", split_axis=0, concat_axis=0, tiled=True
    )

    parts = database.reshape(local_rows, head_devices, part_tokens, enc_width)
    mine = lax.dynamic_index_in_dim(parts, my_head, axis=1, keepdims=False)
    wanted, tokens = lax.optimization_barrier((wanted, tokens))
    outgoing = mine[wanted]
    incoming = lax.all_to_all(outgoing, "seq", split_axis=0, concat_axis=0, tiled=True)
    asked = incoming[owner_index]
    rows = lax.all_to_all(
        asked.reshape(head_devices, -1, part_tokens, enc_width),
        "head",
        split_axis=0,
        concat_axis=0,
        tiled=True,
    )
    blocks = rows.shape[1] // 2
    rows = rows.reshape(head_devices, blocks, 2 * part_tokens, enc_width)

    out = attention(tokens, rows, weights)
    out = lax.all_to_all(out, "head", split_axis=0, concat_axis=0, tiled=True)
    out = out.reshape(-1, 2 * width)
    first = shifted(out[-margin:], "seq", 1)
    context = jnp.concatenate([first[:, :width], out[:-margin, :width]], axis=0)
    query_grad = jnp.concatenate([first[:, width:], out[:-margin, width:]], axis=0)
    return context, query_grad


def solution(mesh):
    return jax.shard_map(
        body,
        mesh=mesh,
        in_specs=(
            P("seq", "head"),
            P("seq", "head"),
            P("seq", None, None),
            P("seq", None),
            P(),
            P("seq", "head"),
            P("seq", "head"),
        ),
        out_specs=(P("seq", "head"), P("seq", "head")),
        check_vma=False,
    )
```

time: 626 us -> 397 us (0.63)
  blocking collectives: 235 us -> 38.8 us
  matrix products: 30.8 us -> 0 us
  local copies, waits for them, and re-layouts: 28.1 us -> 6.09 us
  Pallas kernels: 0 us -> 19.9 us
  between operations: 0.9 us -> 14.2 us
  starting transfers between devices: 43.3 us -> 30.2 us
    ppermute x4 -> x2, waiting for transfers between devices: 275 us -> 3.74 us  [shifted(): lax.ppermute(value, axis, [(source, source + steps) for source in range(f...]
    all_gather x2 -> x0, blocking collectives: 235 us -> none  [the longest x1 136 us: body(): lax.all_gather(key_weight, 'seq', axis=0, tiled=True)]
    all_gather x0 -> x2, waiting for transfers between devices: none -> 145 us  [the longest x1 145 us: body(): weight = lax.all_gather(weight, 'seq', axis=0, tiled=True)]
    all_to_all x1, waiting for transfers between devices: 3.25 us -> 97.1 us  [body(): lax.all_to_all(outgoing, 'seq', split_axis=0, concat_axis=0, tiled=True)]
    all_to_all x0 -> x2, blocking collectives: none -> 38.8 us  [the longest x1 19.6 us: body(): out = lax.all_to_all(out, 'head', split_axis=0, concat_axis=0, tiled=True)]
    all_to_all x1 -> x2, waiting for transfers between devices: 0.01 us -> 36.3 us  [the longest x1 25.2 us: body(): lax.all_to_all(tokens.reshape(head_devices, -1, 2 * width), 'head', split...]
    dot_general x6 -> x0, matrix products: 30.8 us -> none  [the longest x1 15.3 us: attend_backward(): jnp.einsum('chqk,ckhd->cqhd', dscore, keys_four, preferred_element_type=j...]
    pallas_call x0 -> x1, Pallas kernels: none -> 19.9 us  [attention(): pl.pallas_call(attend_kernel, grid=(parts,), out_shape=jax.ShapeDtypeStru...]
  transfers between devices with their start and end apart: 6 -> 7, of which waited for: 4 -> 5; matrix products, arithmetic and copies ran while one was open for 3% -> 2% of each run, Pallas kernels for 0% -> 0%
where the time goes in v2:
time: 397 us
  waiting for transfers between devices  282 us (71%)
  blocking collectives  38.8 us (10%)
  starting transfers between devices  30.2 us (8%)
  Pallas kernels  19.9 us (5%)
  between operations  14.2 us (4%)
  local copies, waits for them, and re-layouts  6.09 us (2%)
  other arithmetic  5.26 us (1%)
    all_gather x1, waiting for transfers between devices, body(): weight = lax.all_gather(weight, 'seq', axis=0, tiled=True)  145 us
    all_to_all x1, waiting for transfers between devices, body(): lax.all_to_all(outgoing, 'seq', split_axis=0, concat_axis=0, tiled=True)  97.1 us
    all_to_all x1, waiting for transfers between devices, body(): lax.all_to_all(tokens.reshape(head_devices, -1, 2 * width), 'head', split...  25.2 us
    pallas_call x1, Pallas kernels, attention(): pl.pallas_call(attend_kernel, grid=(parts,), out_shape=jax.ShapeDtypeStru...  19.9 us
    all_to_all x1, blocking collectives, body(): out = lax.all_to_all(out, 'head', split_axis=0, concat_axis=0, tiled=True)  19.6 us
    all_to_all x1, blocking collectives, body(): lax.all_to_all(asked.reshape(head_devices, -1, part_tokens, enc_width), '...  19.2 us
    all_to_all x1, waiting for transfers between devices, body(): lax.all_to_all(asked_rows.reshape(seq_count, 1), 'seq', split_axis=0, con...  11.1 us
    all_to_all x1, starting transfers between devices, body(): lax.all_to_all(asked_rows.reshape(seq_count, 1), 'seq', split_axis=0, con...  10.1 us
  transfers between devices with their start and end apart: 7, of which 5 were waited for; matrix products, arithmetic and copies ran while one was open for 2% of the time, Pallas kernels for 0%

profile of v2, /device:TPU:24, one launch (start us, length us, event | category | flops | bytes accessed | tf_op | source)
XLA Modules:
  0.0 396.7 jit_solution(10757053533643627944)
XLA Ops:
  7.2 0.0 all-gather.4.cloned.1.call-start
  7.2 1.4 pad_maximum_fusion.3
  8.6 0.0 all-gather.4.cloned.1.call-update
  8.6 0.0 all-gather.6.cloned.1.call-start
  8.7 145.0 %all-gather.4.cloned.1.call-done = bf16[1024,512]{1,0:T(8,128)(2,1)} async-done(((bf16[16,512]{1,0:T(8,128)(2,1)}), bf16[1024,512]{1,0:T(8,128)(2,1)}) %all-gather.4.cloned.1.call-update) | async-done | bytes 1048592 | tf_op jit(solution)/shard_map/all_gather | solution.py:89
  153.7 0.0 all-gather.6.cloned.1.call-update
  153.7 1.1 constant_dynamic-update-slice_fusion.1
  154.9 4.7 %collective-permute-start = (bf16[63,512]{1,0:T(8,128)(2,1)S(1)}, bf16[63,512]{1,0:T(8,128)(2,1)S(1)}, u32[]{:S(2)}, u32[]{:S(2)}) collective-permute-start(bf16[63,512]{1,0:T(8,128)(2,1)S(1)} %slice.33), channel_id=1, source_target_pairs={{8,0},{16,8},{24,16},{32,24},{40,32},{48,40},{56,48},{64,56},{72,6... | collective-permute-start | bytes 193544 | tf_op jit(solution)/shard_map/ppermute | solution.py:15
  159.6 0.1 copy.15
  159.7 0.1 eq.30
  159.8 0.2 select_reduce_fusion
  160.0 0.1 select_reduce_fusion.1
  160.1 0.7 copy.16
  160.8 10.1 %all-to-all-start = ((s32[64,1,1]{2,1,0:T(1,128)}), s32[64,1,1]{2,1,0:T(1,128)S(1)}, u32[]{:S(2)}, u32[]{:S(2)}) async-start(s32[64,1,1]{2,1,0:T(1,128)} %copy.16), calls=%async_computation | async-start | bytes 65536 | tf_op jit(solution)/shard_map/all_to_all | solution.py:107
  170.9 0.2 slice.32
  171.2 1.1 pad_maximum_fusion
  172.3 11.1 %all-to-all-done = s32[64,1,1]{2,1,0:T(1,128)S(1)} async-done(((s32[64,1,1]{2,1,0:T(1,128)}), s32[64,1,1]{2,1,0:T(1,128)S(1)}, u32[]{:S(2)}, u32[]{:S(2)}) %all-to-all-start) | async-done | bytes 288 | tf_op jit(solution)/shard_map/all_to_all | solution.py:107
  183.4 4.3 %all-to-all-start.1 = ((bf16[8,128,512]{2,1,0:T(8,128)(2,1)}), bf16[8,128,512]{2,1,0:T(8,128)(2,1)S(1)}, u32[]{:S(2)}, u32[]{:S(2)}) async-start(bf16[8,128,512]{2,1,0:T(8,128)(2,1)} %bitcast.1), calls=%async_computation.1 | async-start | bytes 2097152 | tf_op jit(solution)/shard_map/all_to_all | solution.py:113
  187.6 1.1 dynamic-slice_bitcast_fusion
  188.7 1.2 reduce
  190.0 25.2 %all-to-all-done.1.tokens_ref = bf16[8,128,512]{2,1,0:T(8,128)(2,1)S(1)} async-done(((bf16[8,128,512]{2,1,0:T(8,128)(2,1)}), bf16[8,128,512]{2,1,0:T(8,128)(2,1)S(1)}, u32[]{:S(2)}, u32[]{:S(2)}) %all-to-all-start.1) | async-done | bytes 1048608 | tf_op jit(solution)/shard_map/all_to_all | solution.py:113
  215.2 2.0 gather_fusion
  217.2 6.6 %all-to-all-start.2 = ((bf16[64,16,1024]{2,1,0:T(8,128)(2,1)}), bf16[64,16,1024]{2,1,0:T(8,128)(2,1)S(1)}, u32[]{:S(2)}, u32[]{:S(2)}) async-start(bf16[64,16,1024]{2,1,0:T(8,128)(2,1)} %gather_fusion), calls=%async_computation.2 | async-start | bytes 4194304 | tf_op jit(solution)/shard_map/all_to_all | solution.py:121
  223.9 97.1 %all-to-all-done.2 = bf16[64,16,1024]{2,1,0:T(8,128)(2,1)S(1)} async-done(((bf16[64,16,1024]{2,1,0:T(8,128)(2,1)}), bf16[64,16,1024]{2,1,0:T(8,128)(2,1)S(1)}, u32[]{:S(2)}, u32[]{:S(2)}) %all-to-all-start.2) | async-done | bytes 2097184 | tf_op jit(solution)/shard_map/all_to_all | solution.py:121
  321.0 0.6 gather_fusion.1
  321.6 19.2 %all_to_all.29 = bf16[8,4,16,1024]{3,2,1,0:T(8,128)(2,1)} all-to-all(bf16[8,4,16,1024]{3,2,1,0:T(8,128)(2,1)S(1)} %bitcast.23), channel_id=1, replica_groups=mesh['seq'=64,'head'=8] {'head'}, dimensions={0} | all-to-all | bytes 2097152 | tf_op jit(solution)/shard_map/all_to_all | solution.py:123
  340.8 19.9 %blocks.1 = bf16[8,128,512]{2,1,0:T(8,128)(2,1)} custom-call(bf16[8,128,512]{2,1,0:T(8,128)(2,1)} %copy-done, bf16[8,2,32,1024]{3,2,1,0:T(8,128)(2,1)} %bitcast.24, bf16[8,1024,512]{2,1,0:T(8,128)(2,1)} %bitcast.27), custom_call_target="tpu_custom_call" | custom-call | flops 4831838208 | bytes 11534336 | tf_op jit(solution)/shard_map/blocks/pallas_call | solution.py:58
  360.8 19.6 %all_to_all.30 = bf16[8,128,512]{2,1,0:T(8,128)(2,1)S(1)} all-to-all(bf16[8,128,512]{2,1,0:T(8,128)(2,1)} %blocks.1), channel_id=1, replica_groups=mesh['seq'=64,'head'=8] {'head'}, dimensions={0} | all-to-all | bytes 2097152 | tf_op jit(solution)/shard_map/all_to_all | solution.py:134
  380.4 4.4 %collective-permute-start.1 = (bf16[63,512]{1,0:T(8,128)(2,1)S(1)}, bf16[63,512]{1,0:T(8,128)(2,1)S(1)}, u32[]{:S(2)}, u32[]{:S(2)}) collective-permute-start(bf16[63,512]{1,0:T(8,128)(2,1)S(1)} %slice.34), channel_id=1, source_target_pairs={{0,8},{8,16},{16,24},{24,32},{32,40},{40,48},{48,56},{56,64},{64,7... | collective-permute-start | bytes 193544 | tf_op jit(solution)/shard_map/ppermute | solution.py:15
  384.8 0.1 fusion.1
  384.9 3.7 collective-permute-done.1
  388.6 1.2 pad_maximum_fusion.1
  (19 shorter events, 0.1 us)
Async XLA Ops:
  7.2 147.6 %copy-start.1 = (bf16[1024,256]{1,0:T(8,128)(2,1)S(1)}, bf16[1024,256]{1,0:T(8,128)(2,1)}, u32[]{:S(2)}) copy-start(bf16[1024,256]{1,0:T(8,128)(2,1)} %param.8) | copy-start | bytes 1572868
  7.2 152.4 %copy-start.3 = (s32[16,2]{0,1:T(2,128)S(1)}, s32[16,2]{0,1:T(2,128)}, u32[]{:S(2)}) copy-start(s32[16,2]{0,1:T(2,128)} %param.10) | copy-start | bytes 388
  7.2 152.6 %copy-start.2 = (s32[1024]{0:T(1024)S(1)}, s32[1024]{0:T(1024)}, u32[]{:S(2)}) copy-start(s32[1024]{0:T(1024)} %param.11) | copy-start | bytes 12292
  7.2 146.5 %all-gather.4.cloned.1.call-start = ((), (), s32[]{:S(2)}) async-start(), calls=%async_computation.5 | async-start | bytes 1064960 | tf_op jit(solution)/shard_map/all_gather | solution.py:89
  8.6 332.2 %all-gather.6.cloned.1.call-start = ((), (), s32[]{:S(2)}) async-start(), calls=%async_computation.6 | async-start | bytes 9437184 | tf_op jit(solution)/shard_map/all_gather | solution.py:90
  154.9 16.3 %collective-permute-start = (bf16[63,512]{1,0:T(8,128)(2,1)S(1)}, bf16[63,512]{1,0:T(8,128)(2,1)S(1)}, u32[]{:S(2)}, u32[]{:S(2)}) collective-permute-start(bf16[63,512]{1,0:T(8,128)(2,1)S(1)} %slice.33), channel_id=1, source_target_pairs={{8,0},{16,8},{24,16},{32,24},{40,32},{48,40},{56,48},{64,56},{72,6... | collective-permute-start | bytes 193544 | tf_op jit(solution)/shard_map/ppermute | solution.py:15
  160.8 22.6 %all-to-all-start = ((s32[64,1,1]{2,1,0:T(1,128)}), s32[64,1,1]{2,1,0:T(1,128)S(1)}, u32[]{:S(2)}, u32[]{:S(2)}) async-start(s32[64,1,1]{2,1,0:T(1,128)} %copy.16), calls=%async_computation | async-start | bytes 65536 | tf_op jit(solution)/shard_map/all_to_all | solution.py:107
  183.4 31.8 %all-to-all-start.1 = ((bf16[8,128,512]{2,1,0:T(8,128)(2,1)}), bf16[8,128,512]{2,1,0:T(8,128)(2,1)S(1)}, u32[]{:S(2)}, u32[]{:S(2)}) async-start(bf16[8,128,512]{2,1,0:T(8,128)(2,1)} %bitcast.1), calls=%async_computation.1 | async-start | bytes 2097152 | tf_op jit(solution)/shard_map/all_to_all | solution.py:113
  215.2 2.1 copy-start
  217.2 103.8 %all-to-all-start.2 = ((bf16[64,16,1024]{2,1,0:T(8,128)(2,1)}), bf16[64,16,1024]{2,1,0:T(8,128)(2,1)S(1)}, u32[]{:S(2)}, u32[]{:S(2)}) async-start(bf16[64,16,1024]{2,1,0:T(8,128)(2,1)} %gather_fusion), calls=%async_computation.2 | async-start | bytes 4194304 | tf_op jit(solution)/shard_map/all_to_all | solution.py:121
  380.4 8.3 %collective-permute-start.1 = (bf16[63,512]{1,0:T(8,128)(2,1)S(1)}, bf16[63,512]{1,0:T(8,128)(2,1)S(1)}, u32[]{:S(2)}, u32[]{:S(2)}) collective-permute-start(bf16[63,512]{1,0:T(8,128)(2,1)S(1)} %slice.34), channel_id=1, source_target_pairs={{0,8},{8,16},{16,24},{24,32},{32,40},{40,48},{48,56},{56,64},{64,7... | collective-permute-start | bytes 193544 | tf_op jit(solution)/shard_map/ppermute | solution.py:15
Sparse Core Ops, SparseCore 0:
  11.6 142.0 all-gather.3
  155.8 65.7 all-gather.5

commit v3 on v2

v3 whole, which is shorter than its diff:
```python
import functools

import jax
import jax.numpy as jnp
from jax import lax
from jax.experimental import pallas as pl
from jax.experimental.pallas import tpu as pltpu
from jax.sharding import PartitionSpec as P

DH = 128
BLOCK = 64
FEATURES = 1024
Z = 16
GROUP = 4


def shifted(value, axis, steps):
    count = lax.axis_size(axis)
    first, last = (max(0, -steps), min(count, count - steps))
    return lax.ppermute(value, axis, [(source, source + steps) for source in range(first, last)])


def scores_of(left, right):
    last = (((1,), (1,)), ((), ()))
    return lax.dot_general(left, right, last, preferred_element_type=jnp.float32)


def grouped(refs):
    groups = []
    for ref in refs:
        if groups and groups[-1][0].shape[-1] < FEATURES and len(groups[-1]) == 1:
            groups[-1].append(ref)
        else:
            groups.append([ref])
    return groups


def project(piece_refs, weight_ref, kv_ref):
    rows = []
    for group in grouped(piece_refs):
        parts = [ref[...].reshape(-1, ref.shape[-1]) for ref in group]
        rows.append(parts[0] if len(parts) == 1 else jnp.concatenate(parts, axis=1))
    kv = jnp.dot(
        jnp.concatenate(rows, axis=0), weight_ref[...], preferred_element_type=jnp.float32
    )
    kv_ref[...] = kv.astype(jnp.bfloat16).reshape(kv_ref.shape)


def attend(queries, grads, kv_ref):
    scale = DH ** (-0.5)
    width = queries[0].shape[1]
    pairs = [(at, head) for at in range(len(queries)) for head in range(width // DH)]
    keys, values, scores, prob_grad = [], [], [], []
    for at, head in pairs:
        own = slice(head * DH, (head + 1) * DH)
        other = slice(width + head * DH, width + (head + 1) * DH)
        keys.append(kv_ref[:, at, :, own].reshape(-1, DH))
        values.append(kv_ref[:, at, :, other].reshape(-1, DH))
        scores.append(scores_of(queries[at][:, own], keys[-1]))
        prob_grad.append(scores_of(grads[at][:, own], values[-1]))
    scores = jnp.concatenate(scores, axis=0) * scale
    prob_grad = jnp.concatenate(prob_grad, axis=0)
    weights = jnp.exp(scores - jnp.max(scores, axis=-1, keepdims=True))
    probabilities = weights / jnp.sum(weights, axis=-1, keepdims=True)
    delta = jnp.sum(probabilities * prob_grad, axis=-1, keepdims=True)
    probs_low = probabilities.astype(jnp.bfloat16)
    dscore = (probabilities * (prob_grad - delta) * scale).astype(jnp.bfloat16)
    blocks = [([], []) for _ in queries]
    for i, (at, head) in enumerate(pairs):
        rows = slice(i * BLOCK, (i + 1) * BLOCK)
        blocks[at][0].append(jnp.dot(probs_low[rows], values[i], preferred_element_type=jnp.float32))
        blocks[at][1].append(jnp.dot(dscore[rows], keys[i], preferred_element_type=jnp.float32))
    return [tuple(jnp.concatenate(heads, axis=1) for heads in block) for block in blocks]


def block_rows(ref, next_ref, at, count, last_row):
    here = ref[at * BLOCK : (at + 1) * BLOCK, :]
    there = next_ref[...] if at + 1 == count else ref[(at + 1) * BLOCK : (at + 2) * BLOCK, :]
    rows = jnp.where(last_row, here.astype(jnp.float32), there.astype(jnp.float32))
    return rows.astype(jnp.bfloat16)


def main_kernel(pieces_count, place_ref, query_ref, next_query_ref, grad_ref, next_grad_ref, *refs):
    piece_refs, refs = refs[:pieces_count], refs[pieces_count:]
    before_refs, refs = refs[:pieces_count], refs[pieces_count:]
    *held_refs, context_ref, qgrad_ref, weight_ref, kv_ref, before_kv_ref, carry_ref = refs

    @pl.when(pl.program_id(0) == 0)
    def _():
        rows = held_refs[0].shape[1]
        for step, held_ref in enumerate(held_refs):
            y = lax.rem(place_ref[0] + len(held_refs) - step, len(held_refs))
            for m in range(Z):
                at = (m & 3) * 4 + (m >> 2 & 1) * 2 + (m >> 3)
                start = (y * Z + (place_ref[1] ^ m)) * rows
                weight_ref[pl.ds(pl.multiple_of(start, 16), rows), :] = held_ref[at]
        project(before_refs, weight_ref, before_kv_ref)
        ((context, qgrad),) = attend([query_ref[:BLOCK, :]], [grad_ref[:BLOCK, :]], before_kv_ref)
        carry_ref[0] = context
        carry_ref[1] = qgrad

    project(piece_refs, weight_ref, kv_ref)
    count = kv_ref.shape[1]
    row = lax.broadcasted_iota(jnp.int32, (BLOCK, query_ref.shape[1]), 0)
    last_row = row == BLOCK - 1
    queries = [block_rows(query_ref, next_query_ref, at, count, last_row) for at in range(count)]
    grads = [block_rows(grad_ref, next_grad_ref, at, count, last_row) for at in range(count)]
    before = carry_ref[0], carry_ref[1]
    for at, now in enumerate(attend(queries, grads, kv_ref)):
        for out_ref, old, new in zip((context_ref, qgrad_ref), before, now):
            tile = jnp.where(last_row, new, old)
            out_ref[at * BLOCK : (at + 1) * BLOCK, :] = tile.astype(jnp.bfloat16)
        before = now
    carry_ref[0], carry_ref[1] = before


def attention(place, queries, grads, pieces, held):
    tokens, width = queries.shape
    blocks = tokens // BLOCK
    part_tokens = pieces[0].shape[1]
    parts = sum(p.shape[-1] for p in pieces) // FEATURES
    keys = parts * part_tokens
    tile = pl.BlockSpec((GROUP * BLOCK, width), lambda i: (i, 0))
    next_tile = pl.BlockSpec(
        (BLOCK, width), lambda i: (jnp.minimum((i + 1) * GROUP, blocks - 1), 0)
    )

    def whole(value):
        return pl.BlockSpec(value.shape, lambda i: (0,) * value.ndim)

    def kv_scratch(group):
        return pltpu.VMEM((parts, group, part_tokens, 2 * width), jnp.bfloat16)

    out = jax.ShapeDtypeStruct((tokens, width), jnp.bfloat16)
    return pl.pallas_call(
        functools.partial(main_kernel, len(pieces)),
        grid=(blocks // GROUP,),
        out_shape=(out, out),
        in_specs=[pl.BlockSpec(memory_space=pltpu.SMEM), tile, next_tile, tile, next_tile]
        + [pl.BlockSpec((GROUP,) + p.shape[1:], lambda i: (i, 0, 0)) for p in pieces]
        + [pl.BlockSpec((1,) + p.shape[1:], lambda i: (blocks, 0, 0)) for p in pieces]
        + [whole(h) for h in held],
        out_specs=(tile, tile),
        scratch_shapes=[
            pltpu.VMEM((FEATURES, 2 * width), jnp.bfloat16),
            kv_scratch(GROUP),
            kv_scratch(1),
            pltpu.VMEM((2, BLOCK, width), jnp.float32),
        ],
        compiler_params=pltpu.CompilerParams(vmem_limit_bytes=32 * 1024 * 1024),
        cost_estimate=pl.CostEstimate(
            flops=2 * (blocks + 1) * keys * 2 * width * (FEATURES + 2 * BLOCK),
            bytes_accessed=2 * (blocks * keys * FEATURES + 4 * tokens * width),
            transcendentals=blocks * keys * BLOCK * width // DH,
        ),
        name="blocks",
    )(place, queries, queries, grads, grads, *pieces, *pieces, *held)


def body(queries, context_grad, database, neighbour_ids, owner_map, key_weight, value_weight):
    seq_count = lax.axis_size("seq")
    head_devices = lax.axis_size("head")
    y_count = seq_count // Z
    local_rows, neigh_tokens, enc_width = database.shape
    part_tokens = neigh_tokens // head_devices
    my_head = lax.axis_index("head")

    request_ids = neighbour_ids.reshape(-1)
    row_labels = jnp.arange(owner_map.shape[0], dtype=jnp.int32)
    stored = jnp.sum(
        jnp.where(request_ids[:, None] == row_labels[None, :], owner_map[None, :], 0),
        axis=1,
        dtype=jnp.int32,
    )
    owner_index = stored // local_rows
    local_row = stored % local_rows
    slot_labels = jnp.arange(seq_count, dtype=jnp.int32)
    asked_rows = jnp.sum(
        jnp.where(owner_index[:, None] == slot_labels[None, :], local_row[:, None], 0),
        axis=0,
        dtype=jnp.int32,
    )
    wanted = lax.all_to_all(
        asked_rows.reshape(seq_count, 1), "seq", split_axis=0, concat_axis=0, tiled=True
    ).reshape(-1)

    def from_z(value, step):
        return lax.ppermute(value, "seq", [(i, i ^ step) for i in range(seq_count)])

    weight = jnp.concatenate([key_weight, value_weight], axis=1)[None]
    for step in (8, 4):
        weight = jnp.concatenate([weight, from_z(weight, step)], axis=0)

    parts = database.reshape(local_rows, head_devices, part_tokens, enc_width)
    mine = lax.dynamic_index_in_dim(parts, my_head, axis=1, keepdims=False)
    wanted, weight = lax.optimization_barrier((wanted, weight))
    outgoing = mine[wanted]
    outgoing, weight = lax.optimization_barrier((outgoing, weight))
    incoming = lax.all_to_all(outgoing, "seq", split_axis=0, concat_axis=0, tiled=True)
    weight = jnp.concatenate([weight] + [from_z(weight, step) for step in (1, 2, 3)], axis=0)
    asked = incoming[owner_index]
    weight, asked = lax.optimization_barrier((weight, asked))
    asked = jnp.concatenate([asked, shifted(asked[-2:], "seq", 1)], axis=0)

    def along_x(value, steps):
        return lax.ppermute(
            value, "head", [(i, (i + 2 * steps) % head_devices) for i in range(head_devices)]
        )

    def other_core(value):
        return lax.ppermute(value, "head", [(i, i ^ 1) for i in range(head_devices)])

    half = enc_width // 2
    before, after = along_x(asked, 1), along_x(asked, -1)
    across = along_x(before[:, :, :half], 1), along_x(after[:, :, half:], -1)
    pieces = [asked, before, after, *across]
    pieces += [other_core(piece) for piece in pieces]
    pieces = [piece.reshape(-1, 2 * part_tokens, piece.shape[-1]) for piece in pieces]

    held = [weight]
    for step in range(1, y_count):
        pairs = [(i, (i + step * Z) % seq_count) for i in range(seq_count)]
        held.append(lax.ppermute(weight, "seq", pairs))
    my_seq = lax.axis_index("seq")
    place = jnp.stack([my_seq // Z, my_seq % Z]).astype(jnp.int32)
    return attention(place, queries, context_grad, pieces, held)


def solution(mesh):
    return jax.shard_map(
        body,
        mesh=mesh,
        in_specs=(
            P("seq", "head"),
            P("seq", "head"),
            P("seq", None, None),
            P("seq", None),
            P(),
            P("seq", "head"),
            P("seq", "head"),
        ),
        out_specs=(P("seq", "head"), P("seq", "head")),
        check_vma=False,
    )
```

time: 397 us -> 237 us (0.60)
  waiting for transfers between devices: 282 us -> 117 us
  starting transfers between devices: 30.2 us -> 88.2 us
  blocking collectives: 38.8 us -> 0 us
  between operations: 14.2 us -> 1.01 us
  Pallas kernels: 19.9 us -> 11.9 us
  local copies, waits for them, and re-layouts: 6.09 us -> 13.4 us
    all_gather x2 -> x0, waiting for transfers between devices: 145 us -> none  [the longest x1 145 us: body(): weight = lax.all_gather(weight, 'seq', axis=0, tiled=True)]
    ppermute x0 -> x17, waiting for transfers between devices: none -> 106 us  [the longest x5 85.2 us: from_z(): return lax.ppermute(value, 'seq', [(i, i ^ step) for i in range(seq_count)])]
    all_to_all x1, waiting for transfers between devices: 97.1 us -> 0.13 us  [body(): lax.all_to_all(outgoing, 'seq', split_axis=0, concat_axis=0, tiled=True)]
    ppermute x0 -> x17, starting transfers between devices: none -> 65.4 us  [the longest x5 33.1 us: from_z(): return lax.ppermute(value, 'seq', [(i, i ^ step) for i in range(seq_count)])]
    all_to_all x2 -> x0, blocking collectives: 38.8 us -> none  [the longest x1 19.6 us: body(): out = lax.all_to_all(out, 'head', split_axis=0, concat_axis=0, tiled=True)]
    all_to_all x1 -> x0, waiting for transfers between devices: 25.2 us -> none  [body(): lax.all_to_all(tokens.reshape(head_devices, -1, 2 * width), 'head', split...]
    pallas_call x1, Pallas kernels: 19.9 us -> 11.9 us  [attention(): pl.pallas_call(functools.partial(main_kernel, len(pieces)), grid=(blocks...]
    unnamed x10 -> x22, local copies, waits for them, and re-layouts: 1.18 us -> 8.8 us
  transfers between devices with their start and end apart: 7 -> 20, of which waited for: 5 -> 10; matrix products, arithmetic and copies ran while one was open for 2% -> 2% of each run, Pallas kernels for 0% -> 0%
where the time goes in v3:
time: 237 us; the launch traced here: 236 us
  waiting for transfers between devices  117 us (49%)
  starting transfers between devices  88.2 us (37%)
  local copies, waits for them, and re-layouts  13.4 us (6%)
  Pallas kernels  11.9 us (5%)
  other arithmetic  3.78 us (2%)
    ppermute x5, waiting for transfers between devices, from_z(): return lax.ppermute(value, 'seq', [(i, i ^ step) for i in range(seq_count)])  85.2 us
    ppermute x5, starting transfers between devices, from_z(): return lax.ppermute(value, 'seq', [(i, i ^ step) for i in range(seq_count)])  33.1 us
    ppermute x4, waiting for transfers between devices, along_x(): lax.ppermute(value, 'head', [(i, (i + 2 * steps) % head_devices) for i in...  18.7 us
    ppermute x4, starting transfers between devices, along_x(): lax.ppermute(value, 'head', [(i, (i + 2 * steps) % head_devices) for i in...  12.4 us
    all_to_all x1, starting transfers between devices, body(): lax.all_to_all(outgoing, 'seq', split_axis=0, concat_axis=0, tiled=True)  12.2 us
    pallas_call x1, Pallas kernels, attention(): pl.pallas_call(functools.partial(main_kernel, len(pieces)), grid=(blocks...  11.9 us
    ppermute x5, starting transfers between devices, other_core(): lax.ppermute(value, 'head', [(i, i ^ 1) for i in range(head_devices)])  10 us
    ppermute x3, starting transfers between devices, body(): held.append(lax.ppermute(weight, 'seq', pairs))  9.79 us
  transfers between devices with their start and end apart: 20, of which 10 were waited for; matrix products, arithmetic and copies ran while one was open for 2% of the time, Pallas kernels for 0%

profile of v3, /device:TPU:24, one launch (start us, length us, event | category | flops | bytes accessed | tf_op | source)
XLA Modules:
  0.0 235.8 jit_solution(6353744026381949537)
XLA Ops:
  1.3 15.7 %collective-permute-start = (bf16[1,16,512]{2,1,0:T(8,128)(2,1)S(1)}, bf16[1,16,512]{2,1,0:T(8,128)(2,1)S(1)}, u32[]{:S(2)}, u32[]{:S(2)}) collective-permute-start(bf16[1,16,512]{2,1,0:T(8,128)(2,1)S(1)} %maximum_bitcast_fusion), channel_id=1, source_target_pairs={{0,64},{8,72},{16,80},{24,88},{32,96},{40,104},{48,112},{56,120},{... | collective-permute-start | bytes 49160 | tf_op jit(solution)/shard_map/ppermute | solution.py:188
  19.6 8.6 %all-to-all-start = ((s32[64,1,1]{2,1,0:T(1,128)}), s32[64,1,1]{2,1,0:T(1,128)S(1)}, u32[]{:S(2)}, u32[]{:S(2)}) async-start(s32[64,1,1]{2,1,0:T(1,128)} %copy.16), calls=%async_computation | async-start | bytes 65536 | tf_op jit(solution)/shard_map/all_to_all | solution.py:183
  28.3 7.3 %collective-permute-start.1 = (bf16[2,16,512]{2,1,0:T(8,128)(2,1)S(1)}, bf16[2,16,512]{2,1,0:T(8,128)(2,1)S(1)}, u32[]{:S(2)}, u32[]{:S(2)}) collective-permute-start(bf16[2,16,512]{2,1,0:T(8,128)(2,1)S(1)} %pad_maximum_fusion.2), channel_id=1, source_target_pairs={{0,32},{8,40},{16,48},{24,56},{32,0},{40,8},{48,16},{56,24},{64,96... | collective-permute-start | bytes 98312 | tf_op jit(solution)/shard_map/ppermute | solution.py:188
  36.7 4.1 %all-to-all-done = s32[64,1,1]{2,1,0:T(1,128)S(1)} async-done(((s32[64,1,1]{2,1,0:T(1,128)}), s32[64,1,1]{2,1,0:T(1,128)S(1)}, u32[]{:S(2)}, u32[]{:S(2)}) %all-to-all-start) | async-done | bytes 288 | tf_op jit(solution)/shard_map/all_to_all | solution.py:183
  40.8 1.2 reduce
  42.1 2.0 gather_fusion
  44.1 12.2 %all-to-all-start.1 = ((bf16[64,16,1024]{2,1,0:T(8,128)(2,1)}), bf16[64,16,1024]{2,1,0:T(8,128)(2,1)S(1)}, u32[]{:S(2)}, u32[]{:S(2)}) async-start(bf16[64,16,1024]{2,1,0:T(8,128)(2,1)} %gather_fusion), calls=%async_computation.1 | async-start | bytes 4194304 | tf_op jit(solution)/shard_map/all_to_all | solution.py:199
  56.3 5.2 %collective-permute-start.4 = (bf16[4,16,512]{2,1,0:T(8,128)(2,1)S(1)}, bf16[4,16,512]{2,1,0:T(8,128)(2,1)S(1)}, u32[]{:S(2)}, u32[]{:S(2)}) collective-permute-start(bf16[4,16,512]{2,1,0:T(8,128)(2,1)S(1)} %pad_maximum_fusion.1), channel_id=1, source_target_pairs={{0,24},{8,16},{16,8},{24,0},{32,56},{40,48},{48,40},{56,32},{64,88... | collective-permute-start | bytes 196616 | tf_op jit(solution)/shard_map/ppermute | solution.py:188
  61.5 1.9 collective-permute-start.3
  63.4 3.0 %collective-permute-start.2 = (bf16[4,16,512]{2,1,0:T(8,128)(2,1)S(1)}, bf16[4,16,512]{2,1,0:T(8,128)(2,1)S(1)}, u32[]{:S(2)}, u32[]{:S(2)}) collective-permute-start(bf16[4,16,512]{2,1,0:T(8,128)(2,1)S(1)} %pad_maximum_fusion.1), channel_id=1, source_target_pairs={{0,8},{8,0},{16,24},{24,16},{32,40},{40,32},{48,56},{56,48},{64,72... | collective-permute-start | bytes 196616 | tf_op jit(solution)/shard_map/ppermute | solution.py:188
  66.4 81.6 %collective-permute-done.4 = bf16[4,16,512]{2,1,0:T(8,128)(2,1)S(1)} collective-permute-done((bf16[4,16,512]{2,1,0:T(8,128)(2,1)S(1)}, bf16[4,16,512]{2,1,0:T(8,128)(2,1)S(1)}, u32[]{:S(2)}, u32[]{:S(2)}) %collective-permute-start.4) | collective-permute-done | bytes 65568 | tf_op jit(solution)/shard_map/ppermute | solution.py:188
  148.0 3.6 %collective-permute-done.3 = bf16[4,16,512]{2,1,0:T(8,128)(2,1)S(1)} collective-permute-done((bf16[4,16,512]{2,1,0:T(8,128)(2,1)S(1)}, bf16[4,16,512]{2,1,0:T(8,128)(2,1)S(1)}, u32[]{:S(2)}, u32[]{:S(2)}) %collective-permute-start.3) | collective-permute-done | bytes 65568 | tf_op jit(solution)/shard_map/ppermute | solution.py:188
  153.2 2.1 collective-permute-start.5
  155.3 7.1 %collective-permute-done.5 = bf16[2,16,1024]{2,1,0:T(8,128)(2,1)S(1)} collective-permute-done((bf16[2,16,1024]{2,1,0:T(8,128)(2,1)S(1)}, bf16[2,16,1024]{2,1,0:T(8,128)(2,1)S(1)}, u32[]{:S(2)}, u32[]{:S(2)}) %collective-permute-start.5) | collective-permute-done | bytes 65568 | tf_op jit(solution)/shard_map/ppermute | solution.py:20
  162.4 4.7 %collective-permute-start.7 = (bf16[34,16,1024]{2,1,0:T(8,128)(2,1)S(1)}, bf16[34,16,1024]{2,1,0:T(8,128)(2,1)S(1)}, u32[]{:S(2)}, u32[]{:S(2)}) collective-permute-start(bf16[34,16,1024]{2,1,0:T(8,128)(2,1)S(1)} %constant_dynamic-update-slice_fusion), channel_id=1, source_target_pairs={{0,6},{1,7},{2,0},{3,1},{4,2},{5,3},{6,4},{7,5},{8,14},{9,15},{10,... | collective-permute-start | bytes 3342344 | tf_op jit(solution)/shard_map/ppermute | solution.py:206
  167.1 1.9 collective-permute-start.6
  169.0 2.7 %collective-permute-start.17 = (bf16[16,16,512]{2,1,0:T(8,128)(2,1)S(1)}, bf16[16,16,512]{2,1,0:T(8,128)(2,1)S(1)}, u32[]{:S(2)}, u32[]{:S(2)}) collective-permute-start(bf16[16,16,512]{2,1,0:T(8,128)(2,1)S(1)} %copy-done.2), channel_id=1, source_target_pairs={{0,384},{8,392},{16,400},{24,408},{32,416},{40,424},{48,432},{56,4... | collective-permute-start | bytes 786440 | tf_op jit(solution)/shard_map/ppermute | solution.py:223
  171.7 2.6 %collective-permute-start.16 = (bf16[16,16,512]{2,1,0:T(8,128)(2,1)S(1)}, bf16[16,16,512]{2,1,0:T(8,128)(2,1)S(1)}, u32[]{:S(2)}, u32[]{:S(2)}) collective-permute-start(bf16[16,16,512]{2,1,0:T(8,128)(2,1)S(1)} %copy-done.2), channel_id=1, source_target_pairs={{0,256},{8,264},{16,272},{24,280},{32,288},{40,296},{48,304},{56,3... | collective-permute-start | bytes 786440 | tf_op jit(solution)/shard_map/ppermute | solution.py:223
  174.3 4.5 %collective-permute-start.15 = (bf16[16,16,512]{2,1,0:T(8,128)(2,1)S(1)}, bf16[16,16,512]{2,1,0:T(8,128)(2,1)S(1)}, u32[]{:S(2)}, u32[]{:S(2)}) collective-permute-start(bf16[16,16,512]{2,1,0:T(8,128)(2,1)S(1)} %copy-done.2), channel_id=1, source_target_pairs={{0,128},{8,136},{16,144},{24,152},{32,160},{40,168},{48,176},{56,1... | collective-permute-start | bytes 786440 | tf_op jit(solution)/shard_map/ppermute | solution.py:223
  178.9 8.6 %collective-permute-done.7 = bf16[34,16,1024]{2,1,0:T(8,128)(2,1)S(1)} collective-permute-done((bf16[34,16,1024]{2,1,0:T(8,128)(2,1)S(1)}, bf16[34,16,1024]{2,1,0:T(8,128)(2,1)S(1)}, u32[]{:S(2)}, u32[]{:S(2)}) %collective-permute-start.7) | collective-permute-done | bytes 1114144 | tf_op jit(solution)/shard_map/ppermute | solution.py:206
  187.5 1.9 collective-permute-start.10
  189.4 3.4 %collective-permute-done.6 = bf16[34,16,1024]{2,1,0:T(8,128)(2,1)S(1)} collective-permute-done((bf16[34,16,1024]{2,1,0:T(8,128)(2,1)S(1)}, bf16[34,16,1024]{2,1,0:T(8,128)(2,1)S(1)}, u32[]{:S(2)}, u32[]{:S(2)}) %collective-permute-start.6) | collective-permute-done | bytes 1114144 | tf_op jit(solution)/shard_map/ppermute | solution.py:206
  192.8 2.2 collective-permute-start.9
  195.8 3.6 %collective-permute-start.8 = (bf16[34,16,512]{2,1,0:T(8,128)(2,1)S(1)}, bf16[34,16,512]{2,1,0:T(8,128)(2,1)}, u32[]{:S(2)}, u32[]{:S(2)}) collective-permute-start(bf16[34,16,512]{2,1,0:T(8,128)(2,1)S(1)} %slice.16), channel_id=1, source_target_pairs={{0,2},{1,3},{2,4},{3,5},{4,6},{5,7},{6,0},{7,1},{8,10},{9,11},{10,... | collective-permute-start | bytes 1671176 | tf_op jit(solution)/shard_map/ppermute | solution.py:206
  200.1 1.9 collective-permute-start.12
  202.8 2.4 %collective-permute-start.11 = (bf16[34,16,1024]{2,1,0:T(8,128)(2,1)S(1)}, bf16[34,16,1024]{2,1,0:T(8,128)(2,1)}, u32[]{:S(2)}, u32[]{:S(2)}) collective-permute-start(bf16[34,16,1024]{2,1,0:T(8,128)(2,1)S(1)} %collective-permute-done.6), channel_id=1, source_target_pairs={{0,1},{1,0},{2,3},{3,2},{4,5},{5,4},{6,7},{7,6},{8,9},{9,8},{10,11... | collective-permute-start | bytes 3342344 | tf_op jit(solution)/shard_map/ppermute | solution.py:211
  205.2 2.4 %collective-permute-done.9 = bf16[34,16,512]{2,1,0:T(8,128)(2,1)} collective-permute-done((bf16[34,16,512]{2,1,0:T(8,128)(2,1)S(1)}, bf16[34,16,512]{2,1,0:T(8,128)(2,1)}, u32[]{:S(2)}, u32[]{:S(2)}) %collective-permute-start.9) | collective-permute-done | bytes 557088 | tf_op jit(solution)/shard_map/ppermute | solution.py:206
  207.6 1.9 collective-permute-start.14
  209.5 4.3 %collective-permute-done.8 = bf16[34,16,512]{2,1,0:T(8,128)(2,1)} collective-permute-done((bf16[34,16,512]{2,1,0:T(8,128)(2,1)S(1)}, bf16[34,16,512]{2,1,0:T(8,128)(2,1)}, u32[]{:S(2)}, u32[]{:S(2)}) %collective-permute-start.8) | collective-permute-done | bytes 557088 | tf_op jit(solution)/shard_map/ppermute | solution.py:206
  213.8 1.9 collective-permute-start.13
  215.8 2.2 collective-permute-done.13
  223.9 11.9 %blocks.1 = (bf16[1024,256]{1,0:T(8,128)(2,1)}, bf16[1024,256]{1,0:T(8,128)(2,1)}) custom-call(s32[2]{0:T(128)S(1)} %pad_add_fusion.place_ref, bf16[1024,256]{1,0:T(8,128)(2,1)S(1)} %copy-done, bf16[1024,256]{1,0:T(8,128)(2,1)S(1)} %copy-done, bf16[1024,256]{1,0:T(8,128)(2,1)S(1)} %copy-done.1, bf16[1024,256]{1,0:T(8,128)(2,1)S(1)} %copy-done.1, ...), custom_call_target="tpu_custom_call" | custom-call | flops 5133828096 | bytes 10485760 | tf_op jit(solution)/shard_map/blocks/pallas_call | solution.py:135
  (53 shorter events, 14.1 us)
Async XLA Ops:
  1.3 26.9 %collective-permute-start = (bf16[1,16,512]{2,1,0:T(8,128)(2,1)S(1)}, bf16[1,16,512]{2,1,0:T(8,128)(2,1)S(1)}, u32[]{:S(2)}, u32[]{:S(2)}) collective-permute-start(bf16[1,16,512]{2,1,0:T(8,128)(2,1)S(1)} %maximum_bitcast_fusion), channel_id=1, source_target_pairs={{0,64},{8,72},{16,80},{24,88},{32,96},{40,104},{48,112},{56,120},{... | collective-permute-start | bytes 49160 | tf_op jit(solution)/shard_map/ppermute | solution.py:188
  19.6 21.2 %all-to-all-start = ((s32[64,1,1]{2,1,0:T(1,128)}), s32[64,1,1]{2,1,0:T(1,128)S(1)}, u32[]{:S(2)}, u32[]{:S(2)}) async-start(s32[64,1,1]{2,1,0:T(1,128)} %copy.16), calls=%async_computation | async-start | bytes 65536 | tf_op jit(solution)/shard_map/all_to_all | solution.py:183
  28.3 13.7 %collective-permute-start.1 = (bf16[2,16,512]{2,1,0:T(8,128)(2,1)S(1)}, bf16[2,16,512]{2,1,0:T(8,128)(2,1)S(1)}, u32[]{:S(2)}, u32[]{:S(2)}) collective-permute-start(bf16[2,16,512]{2,1,0:T(8,128)(2,1)S(1)} %pad_maximum_fusion.2), channel_id=1, source_target_pairs={{0,32},{8,40},{16,48},{24,56},{32,0},{40,8},{48,16},{56,24},{64,96... | collective-permute-start | bytes 98312 | tf_op jit(solution)/shard_map/ppermute | solution.py:188
  44.1 108.4 %all-to-all-start.1 = ((bf16[64,16,1024]{2,1,0:T(8,128)(2,1)}), bf16[64,16,1024]{2,1,0:T(8,128)(2,1)S(1)}, u32[]{:S(2)}, u32[]{:S(2)}) async-start(bf16[64,16,1024]{2,1,0:T(8,128)(2,1)} %gather_fusion), calls=%async_computation.1 | async-start | bytes 4194304 | tf_op jit(solution)/shard_map/all_to_all | solution.py:199
  56.3 91.7 %collective-permute-start.4 = (bf16[4,16,512]{2,1,0:T(8,128)(2,1)S(1)}, bf16[4,16,512]{2,1,0:T(8,128)(2,1)S(1)}, u32[]{:S(2)}, u32[]{:S(2)}) collective-permute-start(bf16[4,16,512]{2,1,0:T(8,128)(2,1)S(1)} %pad_maximum_fusion.1), channel_id=1, source_target_pairs={{0,24},{8,16},{16,8},{24,0},{32,56},{40,48},{48,40},{56,32},{64,88... | collective-permute-start | bytes 196616 | tf_op jit(solution)/shard_map/ppermute | solution.py:188
  61.5 90.2 %collective-permute-start.3 = (bf16[4,16,512]{2,1,0:T(8,128)(2,1)S(1)}, bf16[4,16,512]{2,1,0:T(8,128)(2,1)S(1)}, u32[]{:S(2)}, u32[]{:S(2)}) collective-permute-start(bf16[4,16,512]{2,1,0:T(8,128)(2,1)S(1)} %pad_maximum_fusion.1), channel_id=1, source_target_pairs={{0,16},{8,24},{16,0},{24,8},{32,48},{40,56},{48,32},{56,40},{64,80... | collective-permute-start | bytes 196616 | tf_op jit(solution)/shard_map/ppermute | solution.py:188
  63.4 88.2 %collective-permute-start.2 = (bf16[4,16,512]{2,1,0:T(8,128)(2,1)S(1)}, bf16[4,16,512]{2,1,0:T(8,128)(2,1)S(1)}, u32[]{:S(2)}, u32[]{:S(2)}) collective-permute-start(bf16[4,16,512]{2,1,0:T(8,128)(2,1)S(1)} %pad_maximum_fusion.1), channel_id=1, source_target_pairs={{0,8},{8,0},{16,24},{24,16},{32,40},{40,32},{48,56},{56,48},{64,72... | collective-permute-start | bytes 196616 | tf_op jit(solution)/shard_map/ppermute | solution.py:188
  153.2 15.9 %copy-start.2 = (bf16[16,16,512]{2,1,0:T(8,128)(2,1)S(1)}, bf16[16,16,512]{2,1,0:T(8,128)(2,1)}, u32[]{:S(2)}) copy-start(bf16[16,16,512]{2,1,0:T(8,128)(2,1)} %pad_maximum_fusion.refs_20_) | copy-start | bytes 786436
  153.2 9.3 %collective-permute-start.5 = (bf16[2,16,1024]{2,1,0:T(8,128)(2,1)S(1)}, bf16[2,16,1024]{2,1,0:T(8,128)(2,1)S(1)}, u32[]{:S(2)}, u32[]{:S(2)}) collective-permute-start(bf16[2,16,1024]{2,1,0:T(8,128)(2,1)S(1)} %slice.9), channel_id=1, source_target_pairs={{0,8},{8,16},{16,24},{24,32},{32,40},{40,48},{48,56},{56,64},{64,7... | collective-permute-start | bytes 196616 | tf_op jit(solution)/shard_map/ppermute | solution.py:20
  162.4 25.0 %collective-permute-start.7 = (bf16[34,16,1024]{2,1,0:T(8,128)(2,1)S(1)}, bf16[34,16,1024]{2,1,0:T(8,128)(2,1)S(1)}, u32[]{:S(2)}, u32[]{:S(2)}) collective-permute-start(bf16[34,16,1024]{2,1,0:T(8,128)(2,1)S(1)} %constant_dynamic-update-slice_fusion), channel_id=1, source_target_pairs={{0,6},{1,7},{2,0},{3,1},{4,2},{5,3},{6,4},{7,5},{8,14},{9,15},{10,... | collective-permute-start | bytes 3342344 | tf_op jit(solution)/shard_map/ppermute | solution.py:206
  167.1 25.7 %collective-permute-start.6 = (bf16[34,16,1024]{2,1,0:T(8,128)(2,1)S(1)}, bf16[34,16,1024]{2,1,0:T(8,128)(2,1)S(1)}, u32[]{:S(2)}, u32[]{:S(2)}) collective-permute-start(bf16[34,16,1024]{2,1,0:T(8,128)(2,1)S(1)} %constant_dynamic-update-slice_fusion), channel_id=1, source_target_pairs={{0,2},{1,3},{2,4},{3,5},{4,6},{5,7},{6,0},{7,1},{8,10},{9,11},{10,... | collective-permute-start | bytes 3342344 | tf_op jit(solution)/shard_map/ppermute | solution.py:206
  169.0 26.1 %collective-permute-start.17 = (bf16[16,16,512]{2,1,0:T(8,128)(2,1)S(1)}, bf16[16,16,512]{2,1,0:T(8,128)(2,1)S(1)}, u32[]{:S(2)}, u32[]{:S(2)}) collective-permute-start(bf16[16,16,512]{2,1,0:T(8,128)(2,1)S(1)} %copy-done.2), channel_id=1, source_target_pairs={{0,384},{8,392},{16,400},{24,408},{32,416},{40,424},{48,432},{56,4... | collective-permute-start | bytes 786440 | tf_op jit(solution)/shard_map/ppermute | solution.py:223
  171.7 27.7 %collective-permute-start.16 = (bf16[16,16,512]{2,1,0:T(8,128)(2,1)S(1)}, bf16[16,16,512]{2,1,0:T(8,128)(2,1)S(1)}, u32[]{:S(2)}, u32[]{:S(2)}) collective-permute-start(bf16[16,16,512]{2,1,0:T(8,128)(2,1)S(1)} %copy-done.2), channel_id=1, source_target_pairs={{0,256},{8,264},{16,272},{24,280},{32,288},{40,296},{48,304},{56,3... | collective-permute-start | bytes 786440 | tf_op jit(solution)/shard_map/ppermute | solution.py:223
  174.3 27.7 %collective-permute-start.15 = (bf16[16,16,512]{2,1,0:T(8,128)(2,1)S(1)}, bf16[16,16,512]{2,1,0:T(8,128)(2,1)S(1)}, u32[]{:S(2)}, u32[]{:S(2)}) collective-permute-start(bf16[16,16,512]{2,1,0:T(8,128)(2,1)S(1)} %copy-done.2), channel_id=1, source_target_pairs={{0,128},{8,136},{16,144},{24,152},{32,160},{40,168},{48,176},{56,1... | collective-permute-start | bytes 786440 | tf_op jit(solution)/shard_map/ppermute | solution.py:223
  187.5 28.3 %collective-permute-start.10 = (bf16[34,16,1024]{2,1,0:T(8,128)(2,1)S(1)}, bf16[34,16,1024]{2,1,0:T(8,128)(2,1)}, u32[]{:S(2)}, u32[]{:S(2)}) collective-permute-start(bf16[34,16,1024]{2,1,0:T(8,128)(2,1)S(1)} %constant_dynamic-update-slice_fusion), channel_id=1, source_target_pairs={{0,1},{1,0},{2,3},{3,2},{4,5},{5,4},{6,7},{7,6},{8,9},{9,8},{10,11... | collective-permute-start | bytes 3342344 | tf_op jit(solution)/shard_map/ppermute | solution.py:211
  192.8 14.8 %collective-permute-start.9 = (bf16[34,16,512]{2,1,0:T(8,128)(2,1)S(1)}, bf16[34,16,512]{2,1,0:T(8,128)(2,1)}, u32[]{:S(2)}, u32[]{:S(2)}) collective-permute-start(bf16[34,16,512]{2,1,0:T(8,128)(2,1)S(1)} %slice.17), channel_id=1, source_target_pairs={{0,6},{1,7},{2,0},{3,1},{4,2},{5,3},{6,4},{7,5},{8,14},{9,15},{10,... | collective-permute-start | bytes 1671176 | tf_op jit(solution)/shard_map/ppermute | solution.py:206
  195.1 0.7 copy-start.4
  195.8 17.9 %collective-permute-start.8 = (bf16[34,16,512]{2,1,0:T(8,128)(2,1)S(1)}, bf16[34,16,512]{2,1,0:T(8,128)(2,1)}, u32[]{:S(2)}, u32[]{:S(2)}) collective-permute-start(bf16[34,16,512]{2,1,0:T(8,128)(2,1)S(1)} %slice.16), channel_id=1, source_target_pairs={{0,2},{1,3},{2,4},{3,5},{4,6},{5,7},{6,0},{7,1},{8,10},{9,11},{10,... | collective-permute-start | bytes 1671176 | tf_op jit(solution)/shard_map/ppermute | solution.py:206
  199.4 0.7 copy-start.6
  200.1 15.7 %collective-permute-start.12 = (bf16[34,16,1024]{2,1,0:T(8,128)(2,1)S(1)}, bf16[34,16,1024]{2,1,0:T(8,128)(2,1)}, u32[]{:S(2)}, u32[]{:S(2)}) collective-permute-start(bf16[34,16,1024]{2,1,0:T(8,128)(2,1)S(1)} %collective-permute-done.7), channel_id=1, source_target_pairs={{0,1},{1,0},{2,3},{3,2},{4,5},{5,4},{6,7},{7,6},{8,9},{9,8},{10,11... | collective-permute-start | bytes 3342344 | tf_op jit(solution)/shard_map/ppermute | solution.py:211
  202.0 0.7 copy-start.8
  202.8 15.2 %collective-permute-start.11 = (bf16[34,16,1024]{2,1,0:T(8,128)(2,1)S(1)}, bf16[34,16,1024]{2,1,0:T(8,128)(2,1)}, u32[]{:S(2)}, u32[]{:S(2)}) collective-permute-start(bf16[34,16,1024]{2,1,0:T(8,128)(2,1)S(1)} %collective-permute-done.6), channel_id=1, source_target_pairs={{0,1},{1,0},{2,3},{3,2},{4,5},{5,4},{6,7},{7,6},{8,9},{9,8},{10,11... | collective-permute-start | bytes 3342344 | tf_op jit(solution)/shard_map/ppermute | solution.py:211
  207.6 8.2 %collective-permute-start.14 = (bf16[34,16,512]{2,1,0:T(8,128)(2,1)}, bf16[34,16,512]{2,1,0:T(8,128)(2,1)}, u32[]{:S(2)}, u32[]{:S(2)}) collective-permute-start(bf16[34,16,512]{2,1,0:T(8,128)(2,1)} %collective-permute-done.9), channel_id=1, source_target_pairs={{0,1},{1,0},{2,3},{3,2},{4,5},{5,4},{6,7},{7,6},{8,9},{9,8},{10,11... | collective-permute-start | bytes 1671176 | tf_op jit(solution)/shard_map/ppermute | solution.py:211
  213.8 4.2 %collective-permute-start.13 = (bf16[34,16,512]{2,1,0:T(8,128)(2,1)}, bf16[34,16,512]{2,1,0:T(8,128)(2,1)}, u32[]{:S(2)}, u32[]{:S(2)}) collective-permute-start(bf16[34,16,512]{2,1,0:T(8,128)(2,1)} %collective-permute-done.8), channel_id=1, source_target_pairs={{0,1},{1,0},{2,3},{3,2},{4,5},{5,4},{6,7},{7,6},{8,9},{9,8},{10,11... | collective-permute-start | bytes 1671176 | tf_op jit(solution)/shard_map/ppermute | solution.py:211
  218.0 1.0 copy-start
  219.0 1.0 copy-start.1
  220.1 0.9 copy-start.3
  221.0 0.9 copy-start.5
  222.0 0.9 copy-start.7
  222.9 0.9 copy-start.9

commit v4 on v3

--- a/solution.py
+++ b/solution.py
@@ -1,5 +1,3 @@
-import functools
-
 import jax
 import jax.numpy as jnp
 from jax import lax
@@ -10,6 +8,7 @@
 DH = 128
 BLOCK = 64
 FEATURES = 1024
+FIRST, SECOND = 640, 384
 Z = 16
 GROUP = 4
 
@@ -25,24 +24,9 @@
     return lax.dot_general(left, right, last, preferred_element_type=jnp.float32)
 
 
-def grouped(refs):
-    groups = []
-    for ref in refs:
-        if groups and groups[-1][0].shape[-1] < FEATURES and len(groups[-1]) == 1:
-            groups[-1].append(ref)
-        else:
-            groups.append([ref])
-    return groups
-
-
-def project(piece_refs, weight_ref, kv_ref):
-    rows = []
-    for group in grouped(piece_refs):
-        parts = [ref[...].reshape(-1, ref.shape[-1]) for ref in group]
-        rows.append(parts[0] if len(parts) == 1 else jnp.concatenate(parts, axis=1))
-    kv = jnp.dot(
-        jnp.concatenate(rows, axis=0), weight_ref[...], preferred_element_type=jnp.float32
-    )
+def project(rows, weight_ref, kv_ref):
+    rows = jnp.concatenate([part.reshape(-1, part.shape[-1]) for part in rows], axis=1)
+    kv = jnp.dot(rows, weight_ref[...], preferred_element_type=jnp.float32)
     kv_ref[...] = kv.astype(jnp.bfloat16).reshape(kv_ref.shape)
 
 
@@ -80,9 +64,19 @@
     return rows.astype(jnp.bfloat16)
 
 
-def main_kernel(pieces_count, place_ref, query_ref, next_query_ref, grad_ref, next_grad_ref, *refs):
-    piece_refs, refs = refs[:pieces_count], refs[pieces_count:]
-    before_refs, refs = refs[:pieces_count], refs[pieces_count:]
+def main_kernel(
+    place_ref,
+    query_ref,
+    next_query_ref,
+    grad_ref,
+    next_grad_ref,
+    first_ref,
+    second_ref,
+    before_second_ref,
+    before_low_ref,
+    before_high_ref,
+    *refs,
+):
     *held_refs, context_ref, qgrad_ref, weight_ref, kv_ref, before_kv_ref, carry_ref = refs
 
     @pl.when(pl.program_id(0) == 0)
@@ -94,12 +88,14 @@
                 at = (m & 3) * 4 + (m >> 2 & 1) * 2 + (m >> 3)
                 start = (y * Z + (place_ref[1] ^ m)) * rows
                 weight_ref[pl.ds(pl.multiple_of(start, 16), rows), :] = held_ref[at]
-        project(before_refs, weight_ref, before_kv_ref)
+        high = before_high_ref[:, :, :, : FIRST - SECOND]
+        rows = [before_low_ref[...], high, before_second_ref[...]]
+        project(rows, weight_ref, before_kv_ref)
         ((context, qgrad),) = attend([query_ref[:BLOCK, :]], [grad_ref[:BLOCK, :]], before_kv_ref)
         carry_ref[0] = context
         carry_ref[1] = qgrad
 
-    project(piece_refs, weight_ref, kv_ref)
+    project([first_ref[...], second_ref[...]], weight_ref, kv_ref)
     count = kv_ref.shape[1]
     row = lax.broadcasted_iota(jnp.int32, (BLOCK, query_ref.shape[1]), 0)
     last_row = row == BLOCK - 1
@@ -114,17 +110,22 @@
     carry_ref[0], carry_ref[1] = before
 
 
-def attention(place, queries, grads, pieces, held):
+def attention(place, queries, grads, first, second, held):
     tokens, width = queries.shape
     blocks = tokens // BLOCK
-    part_tokens = pieces[0].shape[1]
-    parts = sum(p.shape[-1] for p in pieces) // FEATURES
+    parts, _, part_tokens, _ = first.shape
     keys = parts * part_tokens
     tile = pl.BlockSpec((GROUP * BLOCK, width), lambda i: (i, 0))
     next_tile = pl.BlockSpec(
         (BLOCK, width), lambda i: (jnp.minimum((i + 1) * GROUP, blocks - 1), 0)
     )
 
+    def group_of(value):
+        return pl.BlockSpec((parts, GROUP, part_tokens, value.shape[-1]), lambda i: (0, i, 0, 0))
+
+    def one_of(value, at):
+        return pl.BlockSpec((parts, 1, part_tokens, value.shape[-1]), lambda i: (0, at, 0, 0))
+
     def whole(value):
         return pl.BlockSpec(value.shape, lambda i: (0,) * value.ndim)
 
@@ -133,12 +134,12 @@
 
     out = jax.ShapeDtypeStruct((tokens, width), jnp.bfloat16)
     return pl.pallas_call(
-        functools.partial(main_kernel, len(pieces)),
+        main_kernel,
         grid=(blocks // GROUP,),
         out_shape=(out, out),
         in_specs=[pl.BlockSpec(memory_space=pltpu.SMEM), tile, next_tile, tile, next_tile]
-        + [pl.BlockSpec((GROUP,) + p.shape[1:], lambda i: (i, 0, 0)) for p in pieces]
-        + [pl.BlockSpec((1,) + p.shape[1:], lambda i: (blocks, 0, 0)) for p in pieces]
+        + [group_of(first), group_of(second)]
+        + [one_of(second, blocks + k) for k in range(3)]
         + [whole(h) for h in held],
         out_specs=(tile, tile),
         scratch_shapes=[
@@ -147,14 +148,16 @@
             kv_scratch(1),
             pltpu.VMEM((2, BLOCK, width), jnp.float32),
         ],
-        compiler_params=pltpu.CompilerParams(vmem_limit_bytes=32 * 1024 * 1024),
+        compiler_params=pltpu.CompilerParams(vmem_limit_bytes=56 * 1024 * 1024),
         cost_estimate=pl.CostEstimate(
             flops=2 * (blocks + 1) * keys * 2 * width * (FEATURES + 2 * BLOCK),
             bytes_accessed=2 * (blocks * keys * FEATURES + 4 * tokens * width),
             transcendentals=blocks * keys * BLOCK * width // DH,
         ),
         name="blocks",
-    )(place, queries, queries, grads, grads, *pieces, *pieces, *held)
+    )(
+        place, queries, queries, grads, grads, first, second, second, second, second, *held
+    )
 
 
 def body(queries, context_grad, database, neighbour_ids, owner_map, key_weight, value_weight):
@@ -194,28 +197,28 @@
     parts = database.reshape(local_rows, head_devices, part_tokens, enc_width)
     mine = lax.dynamic_index_in_dim(parts, my_head, axis=1, keepdims=False)
     wanted, weight = lax.optimization_barrier((wanted, weight))
-    outgoing = mine[wanted]
-    outgoing, weight = lax.optimization_barrier((outgoing, weight))
-    incoming = lax.all_to_all(outgoing, "seq", split_axis=0, concat_axis=0, tiled=True)
+
+    def exchanged(start, stop, wanted):
+        outgoing = mine[:, :, start:stop][wanted]
+        incoming = lax.all_to_all(outgoing, "seq", split_axis=0, concat_axis=0, tiled=True)
+        return incoming[owner_index]
+
+    def all_parts(rows):
+        rows = lax.all_gather(rows, "head", axis=0, tiled=False)
+        return rows.reshape(head_devices, -1, 2 * part_tokens, rows.shape[-1])
+
+    asked_first = exchanged(0, FIRST, wanted)
     weight = jnp.concatenate([weight] + [from_z(weight, step) for step in (1, 2, 3)], axis=0)
-    asked = incoming[owner_index]
-    weight, asked = lax.optimization_barrier((weight, asked))
-    asked = jnp.concatenate([asked, shifted(asked[-2:], "seq", 1)], axis=0)
-
-    def along_x(value, steps):
-        return lax.ppermute(
-            value, "head", [(i, (i + 2 * steps) % head_devices) for i in range(head_devices)]
-        )
-
-    def other_core(value):
-        return lax.ppermute(value, "head", [(i, i ^ 1) for i in range(head_devices)])
-
-    half = enc_width // 2
-    before, after = along_x(asked, 1), along_x(asked, -1)
-    across = along_x(before[:, :, :half], 1), along_x(after[:, :, half:], -1)
-    pieces = [asked, before, after, *across]
-    pieces += [other_core(piece) for piece in pieces]
-    pieces = [piece.reshape(-1, 2 * part_tokens, piece.shape[-1]) for piece in pieces]
+    first = all_parts(asked_first)
+    asked_first, wanted = lax.optimization_barrier((asked_first, wanted))
+    asked_second = exchanged(FIRST, FEATURES, wanted)
+    weight, asked_second, first = lax.optimization_barrier((weight, asked_second, first))
+    last = jnp.concatenate([asked_first[-2:], asked_second[-2:]], axis=-1)
+    last = shifted(last, "seq", 1)
+    high = jnp.pad(last[:, :, SECOND:FIRST], ((0, 0), (0, 0), (0, 2 * SECOND - FIRST)))
+    second = all_parts(
+        jnp.concatenate([asked_second, last[:, :, FIRST:], last[:, :, :SECOND], high], axis=0)
+    )
 
     held = [weight]
     for step in range(1, y_count):
@@ -223,7 +226,7 @@
         held.append(lax.ppermute(weight, "seq", pairs))
     my_seq = lax.axis_index("seq")
     place = jnp.stack([my_seq // Z, my_seq % Z]).astype(jnp.int32)
-    return attention(place, queries, context_grad, pieces, held)
+    return attention(place, queries, context_grad, first, second, held)
 
 
 def solution(mesh):

time: 237 us -> 244 us (1.030)
  starting transfers between devices: 88.2 us -> 73 us
  between operations: 1.01 us -> 14.3 us
  waiting for transfers between devices: 117 us -> 128 us
  local copies, waits for them, and re-layouts: 13.4 us -> 9.05 us
    all_to_all x1 -> x2, waiting for transfers between devices: 0.13 us -> 64.5 us  [exchanged(): lax.all_to_all(outgoing, 'seq', split_axis=0, concat_axis=0, tiled=True)]
    ppermute x5, waiting for transfers between devices: 85.2 us -> 29.2 us  [from_z(): return lax.ppermute(value, 'seq', [(i, i ^ step) for i in range(seq_count)])]
    ppermute x9 -> x0, starting transfers between devices: 22.4 us -> none  [the longest x4 12.4 us: along_x(): lax.ppermute(value, 'head', [(i, (i + 2 * steps) % head_devices) for i in...]
    ppermute x9 -> x0, waiting for transfers between devices: 20.9 us -> none  [the longest x4 18.7 us: along_x(): lax.ppermute(value, 'head', [(i, (i + 2 * steps) % head_devices) for i in...]
    all_gather x0 -> x2, waiting for transfers between devices: none -> 19.6 us  [all_parts(): rows = lax.all_gather(rows, 'head', axis=0, tiled=False)]
    unnamed x22 -> x9, local copies, waits for them, and re-layouts: 8.8 us -> 0.77 us
    all_to_all x1 -> x2, starting transfers between devices: 12.2 us -> 19.3 us  [exchanged(): lax.all_to_all(outgoing, 'seq', split_axis=0, concat_axis=0, tiled=True)]
    ppermute x3, waiting for transfers between devices: 0.01 us -> 4.78 us  [body(): held.append(lax.ppermute(weight, 'seq', pairs))]
  transfers between devices with their start and end apart: 20 -> 14, of which waited for: 10 -> 9; matrix products, arithmetic and copies ran while one was open for 2% -> 4% of each run, Pallas kernels for 0% -> 0%
where the time goes in v4:
time: 244 us; the launch traced here: 242 us
  waiting for transfers between devices  128 us (52%)
  starting transfers between devices  73 us (30%)
  between operations  14.3 us (6%)
  Pallas kernels  12.7 us (5%)
  local copies, waits for them, and re-layouts  9.05 us (4%)
  other arithmetic  4.45 us (2%)
    all_to_all x2, waiting for transfers between devices, exchanged(): lax.all_to_all(outgoing, 'seq', split_axis=0, concat_axis=0, tiled=True)  64.5 us
    ppermute x5, starting transfers between devices, from_z(): return lax.ppermute(value, 'seq', [(i, i ^ step) for i in range(seq_count)])  33.1 us
    ppermute x5, waiting for transfers between devices, from_z(): return lax.ppermute(value, 'seq', [(i, i ^ step) for i in range(seq_count)])  29.2 us
    all_gather x2, waiting for transfers between devices, all_parts(): rows = lax.all_gather(rows, 'head', axis=0, tiled=False)  19.6 us
    all_to_all x2, starting transfers between devices, exchanged(): lax.all_to_all(outgoing, 'seq', split_axis=0, concat_axis=0, tiled=True)  19.3 us
    pallas_call x1, Pallas kernels, attention(): pl.pallas_call(main_kernel, grid=(blocks // GROUP,), out_shape=(out, out)...  12.7 us
    ppermute x3, starting transfers between devices, body(): held.append(lax.ppermute(weight, 'seq', pairs))  9.6 us
    all_to_all x1, starting transfers between devices, body(): lax.all_to_all(asked_rows.reshape(seq_count, 1), 'seq', split_axis=0, con...  8.64 us
  transfers between devices with their start and end apart: 14, of which 9 were waited for; matrix products, arithmetic and copies ran while one was open for 4% of the time, Pallas kernels for 0%

profile of v4, /device:TPU:24, one launch (start us, length us, event | category | flops | bytes accessed | tf_op | source)
XLA Modules:
  0.0 241.7 jit_solution(17358482083407608720)
XLA Ops:
  7.2 0.7 maximum_bitcast_fusion
  7.9 15.7 %collective-permute-start = (bf16[1,16,512]{2,1,0:T(8,128)(2,1)S(1)}, bf16[1,16,512]{2,1,0:T(8,128)(2,1)S(1)}, u32[]{:S(2)}, u32[]{:S(2)}) collective-permute-start(bf16[1,16,512]{2,1,0:T(8,128)(2,1)S(1)} %maximum_bitcast_fusion), channel_id=1, source_target_pairs={{0,64},{8,72},{16,80},{24,88},{32,96},{40,104},{48,112},{56,120},{... | collective-permute-start | bytes 49160 | tf_op jit(solution)/shard_map/ppermute | solution.py:191
  23.6 0.8 copy.15
  24.4 0.9 select_reduce_fusion
  26.2 8.6 %all-to-all-start = ((s32[64,1,1]{2,1,0:T(1,128)}), s32[64,1,1]{2,1,0:T(1,128)S(1)}, u32[]{:S(2)}, u32[]{:S(2)}) async-start(s32[64,1,1]{2,1,0:T(1,128)} %copy.16), calls=%async_computation | async-start | bytes 65536 | tf_op jit(solution)/shard_map/all_to_all | solution.py:186
  34.8 7.3 %collective-permute-start.1 = (bf16[2,16,512]{2,1,0:T(8,128)(2,1)S(1)}, bf16[2,16,512]{2,1,0:T(8,128)(2,1)S(1)}, u32[]{:S(2)}, u32[]{:S(2)}) collective-permute-start(bf16[2,16,512]{2,1,0:T(8,128)(2,1)S(1)} %pad_maximum_fusion.3), channel_id=1, source_target_pairs={{0,32},{8,40},{16,48},{24,56},{32,0},{40,8},{48,16},{56,24},{64,96... | collective-permute-start | bytes 98312 | tf_op jit(solution)/shard_map/ppermute | solution.py:191
  42.1 1.1 dynamic-slice_bitcast_fusion
  43.3 4.0 %all-to-all-done = s32[64,1,1]{2,1,0:T(1,128)S(1)} async-done(((s32[64,1,1]{2,1,0:T(1,128)}), s32[64,1,1]{2,1,0:T(1,128)S(1)}, u32[]{:S(2)}, u32[]{:S(2)}) %all-to-all-start) | async-done | bytes 288 | tf_op jit(solution)/shard_map/all_to_all | solution.py:186
  47.3 1.2 reduce
  48.6 1.8 gather_fusion
  50.4 12.2 %all-to-all-start.1 = ((bf16[64,16,640]{2,1,0:T(8,128)(2,1)}), bf16[64,16,640]{2,1,0:T(8,128)(2,1)S(1)}, u32[]{:S(2)}, u32[]{:S(2)}) async-start(bf16[64,16,640]{2,1,0:T(8,128)(2,1)} %gather_fusion), calls=%async_computation.1 | async-start | bytes 2621440 | tf_op jit(solution)/shard_map/all_to_all | solution.py:203
  62.7 62.6 %all-to-all-done.1 = bf16[64,16,640]{2,1,0:T(8,128)(2,1)S(1)} async-done(((bf16[64,16,640]{2,1,0:T(8,128)(2,1)}), bf16[64,16,640]{2,1,0:T(8,128)(2,1)S(1)}, u32[]{:S(2)}, u32[]{:S(2)}) %all-to-all-start.1) | async-done | bytes 1310752 | tf_op jit(solution)/shard_map/all_to_all | solution.py:203
  125.3 1.5 gather_fusion.1
  126.8 1.6 gather_fusion.2
  128.4 7.2 %all-to-all-start.2 = ((bf16[64,16,384]{2,1,0:T(8,128)(2,1)}), bf16[64,16,384]{2,1,0:T(8,128)(2,1)S(1)}, u32[]{:S(2)}, u32[]{:S(2)}) async-start(bf16[64,16,384]{2,1,0:T(8,128)(2,1)} %gather_fusion.2), calls=%async_computation.2 | async-start | bytes 1572864 | tf_op jit(solution)/shard_map/all_to_all | solution.py:203
  135.7 5.2 %collective-permute-start.4 = (bf16[4,16,512]{2,1,0:T(8,128)(2,1)S(1)}, bf16[4,16,512]{2,1,0:T(8,128)(2,1)S(1)}, u32[]{:S(2)}, u32[]{:S(2)}) collective-permute-start(bf16[4,16,512]{2,1,0:T(8,128)(2,1)S(1)} %pad_maximum_fusion.1), channel_id=1, source_target_pairs={{0,24},{8,16},{16,8},{24,0},{32,56},{40,48},{48,40},{56,32},{64,88... | collective-permute-start | bytes 196616 | tf_op jit(solution)/shard_map/ppermute | solution.py:191
  140.9 1.9 collective-permute-start.3
  142.8 3.0 %collective-permute-start.2 = (bf16[4,16,512]{2,1,0:T(8,128)(2,1)S(1)}, bf16[4,16,512]{2,1,0:T(8,128)(2,1)S(1)}, u32[]{:S(2)}, u32[]{:S(2)}) collective-permute-start(bf16[4,16,512]{2,1,0:T(8,128)(2,1)S(1)} %pad_maximum_fusion.1), channel_id=1, source_target_pairs={{0,8},{8,0},{16,24},{24,16},{32,40},{40,32},{48,56},{56,48},{64,72... | collective-permute-start | bytes 196616 | tf_op jit(solution)/shard_map/ppermute | solution.py:191
  145.8 26.3 %collective-permute-done.4 = bf16[4,16,512]{2,1,0:T(8,128)(2,1)S(1)} collective-permute-done((bf16[4,16,512]{2,1,0:T(8,128)(2,1)S(1)}, bf16[4,16,512]{2,1,0:T(8,128)(2,1)S(1)}, u32[]{:S(2)}, u32[]{:S(2)}) %collective-permute-start.4) | collective-permute-done | bytes 65568 | tf_op jit(solution)/shard_map/ppermute | solution.py:191
  172.1 3.0 %collective-permute-done.3 = bf16[4,16,512]{2,1,0:T(8,128)(2,1)S(1)} collective-permute-done((bf16[4,16,512]{2,1,0:T(8,128)(2,1)S(1)}, bf16[4,16,512]{2,1,0:T(8,128)(2,1)S(1)}, u32[]{:S(2)}, u32[]{:S(2)}) %collective-permute-start.3) | collective-permute-done | bytes 65568 | tf_op jit(solution)/shard_map/ppermute | solution.py:191
  175.1 0.8 slice.23
  175.9 1.9 all-to-all-done.2
  178.5 2.2 collective-permute-start.5
  180.6 6.1 %collective-permute-done.5 = bf16[2,16,1024]{2,1,0:T(8,128)(2,1)S(1)} collective-permute-done((bf16[2,16,1024]{2,1,0:T(8,128)(2,1)S(1)}, bf16[2,16,1024]{2,1,0:T(8,128)(2,1)S(1)}, u32[]{:S(2)}, u32[]{:S(2)}) %collective-permute-start.5) | collective-permute-done | bytes 65568 | tf_op jit(solution)/shard_map/ppermute | solution.py:19
  186.7 0.8 fusion.1
  187.6 2.7 %collective-permute-start.8 = (bf16[16,16,512]{2,1,0:T(8,128)(2,1)S(1)}, bf16[16,16,512]{2,1,0:T(8,128)(2,1)S(1)}, u32[]{:S(2)}, u32[]{:S(2)}) collective-permute-start(bf16[16,16,512]{2,1,0:T(8,128)(2,1)S(1)} %pad_maximum_fusion.refs_0_), channel_id=1, source_target_pairs={{0,384},{8,392},{16,400},{24,408},{32,416},{40,424},{48,432},{56,4... | collective-permute-start | bytes 786440 | tf_op jit(solution)/shard_map/ppermute | solution.py:226
  190.2 2.4 collective-permute-start.7
  192.7 4.5 %collective-permute-start.6 = (bf16[16,16,512]{2,1,0:T(8,128)(2,1)S(1)}, bf16[16,16,512]{2,1,0:T(8,128)(2,1)S(1)}, u32[]{:S(2)}, u32[]{:S(2)}) collective-permute-start(bf16[16,16,512]{2,1,0:T(8,128)(2,1)S(1)} %pad_maximum_fusion.refs_0_), channel_id=1, source_target_pairs={{0,128},{8,136},{16,144},{24,152},{32,160},{40,168},{48,176},{56,1... | collective-permute-start | bytes 786440 | tf_op jit(solution)/shard_map/ppermute | solution.py:226
  197.8 3.0 %collective-permute-done.8.refs_3_ = bf16[16,16,512]{2,1,0:T(8,128)(2,1)S(1)} collective-permute-done((bf16[16,16,512]{2,1,0:T(8,128)(2,1)S(1)}, bf16[16,16,512]{2,1,0:T(8,128)(2,1)S(1)}, u32[]{:S(2)}, u32[]{:S(2)}) %collective-permute-start.8) | collective-permute-done | bytes 262176 | tf_op jit(solution)/shard_map/ppermute | solution.py:226
  200.9 1.7 collective-permute-done.6.refs_1_
  202.6 19.5 %all-gather.7.cloned.1.call-done = bf16[304,16,384]{2,1,0:T(8,128)(2,1)} async-done(((bf16[38,16,384]{2,1,0:T(8,128)(2,1)}), bf16[304,16,384]{2,1,0:T(8,128)(2,1)}) %all-gather.7.cloned.1.call-update) | async-done | bytes 3735568 | tf_op jit(solution)/shard_map/all_gather | solution.py:207
  222.2 12.7 %blocks.1 = (bf16[1024,256]{1,0:T(8,128)(2,1)}, bf16[1024,256]{1,0:T(8,128)(2,1)}) custom-call(s32[2]{0:T(128)} %pad_add_fusion.place_ref, bf16[1024,256]{1,0:T(8,128)(2,1)} %next_query_ref.1, bf16[1024,256]{1,0:T(8,128)(2,1)} %next_query_ref.1, bf16[1024,256]{1,0:T(8,128)(2,1)} %next_grad_ref.1, bf16[1024,256]{1,0:T(8,128)(2,1)} %next_grad_ref.1, ...), custom_call_target="tpu_custom_call" | custom-call | flops 5133828096 | bytes 10485760 | tf_op jit(solution)/shard_map/blocks/pallas_call | solution.py:136
  (38 shorter events, 2.5 us)
Async XLA Ops:
  7.9 26.9 %collective-permute-start = (bf16[1,16,512]{2,1,0:T(8,128)(2,1)S(1)}, bf16[1,16,512]{2,1,0:T(8,128)(2,1)S(1)}, u32[]{:S(2)}, u32[]{:S(2)}) collective-permute-start(bf16[1,16,512]{2,1,0:T(8,128)(2,1)S(1)} %maximum_bitcast_fusion), channel_id=1, source_target_pairs={{0,64},{8,72},{16,80},{24,88},{32,96},{40,104},{48,112},{56,120},{... | collective-permute-start | bytes 49160 | tf_op jit(solution)/shard_map/ppermute | solution.py:191
  26.2 21.2 %all-to-all-start = ((s32[64,1,1]{2,1,0:T(1,128)}), s32[64,1,1]{2,1,0:T(1,128)S(1)}, u32[]{:S(2)}, u32[]{:S(2)}) async-start(s32[64,1,1]{2,1,0:T(1,128)} %copy.16), calls=%async_computation | async-start | bytes 65536 | tf_op jit(solution)/shard_map/all_to_all | solution.py:186
  34.8 13.7 %collective-permute-start.1 = (bf16[2,16,512]{2,1,0:T(8,128)(2,1)S(1)}, bf16[2,16,512]{2,1,0:T(8,128)(2,1)S(1)}, u32[]{:S(2)}, u32[]{:S(2)}) collective-permute-start(bf16[2,16,512]{2,1,0:T(8,128)(2,1)S(1)} %pad_maximum_fusion.3), channel_id=1, source_target_pairs={{0,32},{8,40},{16,48},{24,56},{32,0},{40,8},{48,16},{56,24},{64,96... | collective-permute-start | bytes 98312 | tf_op jit(solution)/shard_map/ppermute | solution.py:191
  50.4 74.9 %all-to-all-start.1 = ((bf16[64,16,640]{2,1,0:T(8,128)(2,1)}), bf16[64,16,640]{2,1,0:T(8,128)(2,1)S(1)}, u32[]{:S(2)}, u32[]{:S(2)}) async-start(bf16[64,16,640]{2,1,0:T(8,128)(2,1)} %gather_fusion), calls=%async_computation.1 | async-start | bytes 2621440 | tf_op jit(solution)/shard_map/all_to_all | solution.py:203
  62.6 115.8 %all-gather.5.cloned.1.call-start = ((), (), s32[]{:S(2)}) async-start(), calls=%async_computation.3 | async-start | bytes 5898240 | tf_op jit(solution)/shard_map/all_gather | solution.py:207
  128.4 49.3 %all-to-all-start.2 = ((bf16[64,16,384]{2,1,0:T(8,128)(2,1)}), bf16[64,16,384]{2,1,0:T(8,128)(2,1)S(1)}, u32[]{:S(2)}, u32[]{:S(2)}) async-start(bf16[64,16,384]{2,1,0:T(8,128)(2,1)} %gather_fusion.2), calls=%async_computation.2 | async-start | bytes 1572864 | tf_op jit(solution)/shard_map/all_to_all | solution.py:203
  135.6 86.6 %all-gather.7.cloned.1.call-start = ((), (), s32[]{:S(2)}) async-start(), calls=%async_computation.4 | async-start | bytes 4202496 | tf_op jit(solution)/shard_map/all_gather | solution.py:207
  135.7 36.4 %collective-permute-start.4 = (bf16[4,16,512]{2,1,0:T(8,128)(2,1)S(1)}, bf16[4,16,512]{2,1,0:T(8,128)(2,1)S(1)}, u32[]{:S(2)}, u32[]{:S(2)}) collective-permute-start(bf16[4,16,512]{2,1,0:T(8,128)(2,1)S(1)} %pad_maximum_fusion.1), channel_id=1, source_target_pairs={{0,24},{8,16},{16,8},{24,0},{32,56},{40,48},{48,40},{56,32},{64,88... | collective-permute-start | bytes 196616 | tf_op jit(solution)/shard_map/ppermute | solution.py:191
  140.9 34.2 %collective-permute-start.3 = (bf16[4,16,512]{2,1,0:T(8,128)(2,1)S(1)}, bf16[4,16,512]{2,1,0:T(8,128)(2,1)S(1)}, u32[]{:S(2)}, u32[]{:S(2)}) collective-permute-start(bf16[4,16,512]{2,1,0:T(8,128)(2,1)S(1)} %pad_maximum_fusion.1), channel_id=1, source_target_pairs={{0,16},{8,24},{16,0},{24,8},{32,48},{40,56},{48,32},{56,40},{64,80... | collective-permute-start | bytes 196616 | tf_op jit(solution)/shard_map/ppermute | solution.py:191
  142.8 32.2 %collective-permute-start.2 = (bf16[4,16,512]{2,1,0:T(8,128)(2,1)S(1)}, bf16[4,16,512]{2,1,0:T(8,128)(2,1)S(1)}, u32[]{:S(2)}, u32[]{:S(2)}) collective-permute-start(bf16[4,16,512]{2,1,0:T(8,128)(2,1)S(1)} %pad_maximum_fusion.1), channel_id=1, source_target_pairs={{0,8},{8,0},{16,24},{24,16},{32,40},{40,32},{48,56},{56,48},{64,72... | collective-permute-start | bytes 196616 | tf_op jit(solution)/shard_map/ppermute | solution.py:191
  175.1 22.1 %copy-start = (bf16[16,16,512]{2,1,0:T(8,128)(2,1)}, bf16[16,16,512]{2,1,0:T(8,128)(2,1)S(1)}, u32[]{:S(2)}) copy-start(bf16[16,16,512]{2,1,0:T(8,128)(2,1)S(1)} %pad_maximum_fusion.refs_0_) | copy-start | bytes 786436
  178.5 8.3 %collective-permute-start.5 = (bf16[2,16,1024]{2,1,0:T(8,128)(2,1)S(1)}, bf16[2,16,1024]{2,1,0:T(8,128)(2,1)S(1)}, u32[]{:S(2)}, u32[]{:S(2)}) collective-permute-start(bf16[2,16,1024]{2,1,0:T(8,128)(2,1)S(1)} %pad_maximum_fusion.2), channel_id=1, source_target_pairs={{0,8},{8,16},{16,24},{24,32},{32,40},{40,48},{48,56},{56,64},{64,7... | collective-permute-start | bytes 196616 | tf_op jit(solution)/shard_map/ppermute | solution.py:19
  187.6 13.3 %collective-permute-start.8 = (bf16[16,16,512]{2,1,0:T(8,128)(2,1)S(1)}, bf16[16,16,512]{2,1,0:T(8,128)(2,1)S(1)}, u32[]{:S(2)}, u32[]{:S(2)}) collective-permute-start(bf16[16,16,512]{2,1,0:T(8,128)(2,1)S(1)} %pad_maximum_fusion.refs_0_), channel_id=1, source_target_pairs={{0,384},{8,392},{16,400},{24,408},{32,416},{40,424},{48,432},{56,4... | collective-permute-start | bytes 786440 | tf_op jit(solution)/shard_map/ppermute | solution.py:226
  190.2 10.6 %collective-permute-start.7 = (bf16[16,16,512]{2,1,0:T(8,128)(2,1)S(1)}, bf16[16,16,512]{2,1,0:T(8,128)(2,1)S(1)}, u32[]{:S(2)}, u32[]{:S(2)}) collective-permute-start(bf16[16,16,512]{2,1,0:T(8,128)(2,1)S(1)} %pad_maximum_fusion.refs_0_), channel_id=1, source_target_pairs={{0,256},{8,264},{16,272},{24,280},{32,288},{40,296},{48,304},{56,3... | collective-permute-start | bytes 786440 | tf_op jit(solution)/shard_map/ppermute | solution.py:226
  192.7 10.0 %collective-permute-start.6 = (bf16[16,16,512]{2,1,0:T(8,128)(2,1)S(1)}, bf16[16,16,512]{2,1,0:T(8,128)(2,1)S(1)}, u32[]{:S(2)}, u32[]{:S(2)}) collective-permute-start(bf16[16,16,512]{2,1,0:T(8,128)(2,1)S(1)} %pad_maximum_fusion.refs_0_), channel_id=1, source_target_pairs={{0,128},{8,136},{16,144},{24,152},{32,160},{40,168},{48,176},{56,1... | collective-permute-start | bytes 786440 | tf_op jit(solution)/shard_map/ppermute | solution.py:226
  200.9 21.3 %copy-start.1 = (bf16[16,16,512]{2,1,0:T(8,128)(2,1)}, bf16[16,16,512]{2,1,0:T(8,128)(2,1)S(1)}, u32[]{:S(2)}) copy-start(bf16[16,16,512]{2,1,0:T(8,128)(2,1)S(1)} %collective-permute-done.8.refs_3_) | copy-start | bytes 786436
  200.9 21.3 %copy-start.2 = (bf16[16,16,512]{2,1,0:T(8,128)(2,1)}, bf16[16,16,512]{2,1,0:T(8,128)(2,1)S(1)}, u32[]{:S(2)}) copy-start(bf16[16,16,512]{2,1,0:T(8,128)(2,1)S(1)} %collective-permute-done.7.refs_2_) | copy-start | bytes 786436
  202.6 19.6 %copy-start.3 = (bf16[16,16,512]{2,1,0:T(8,128)(2,1)}, bf16[16,16,512]{2,1,0:T(8,128)(2,1)S(1)}, u32[]{:S(2)}) copy-start(bf16[16,16,512]{2,1,0:T(8,128)(2,1)S(1)} %collective-permute-done.6.refs_1_) | copy-start | bytes 786436
Sparse Core Ops, SparseCore 0:
  126.9 36.8 all-gather.4
  187.7 34.4 all-gather.6

commit v5 on v3

--- a/solution.py
+++ b/solution.py
@@ -117,8 +117,9 @@
 def attention(place, queries, grads, pieces, held):
     tokens, width = queries.shape
     blocks = tokens // BLOCK
-    part_tokens = pieces[0].shape[1]
-    parts = sum(p.shape[-1] for p in pieces) // FEATURES
+    arrays = [array for array, _, _ in pieces]
+    part_tokens = arrays[0].shape[1]
+    parts = sum(a.shape[-1] for a in arrays) // FEATURES
     keys = parts * part_tokens
     tile = pl.BlockSpec((GROUP * BLOCK, width), lambda i: (i, 0))
     next_tile = pl.BlockSpec(
@@ -127,6 +128,12 @@
 
     def whole(value):
         return pl.BlockSpec(value.shape, lambda i: (0,) * value.ndim)
+
+    def group_of(array, start, _):
+        return pl.BlockSpec((GROUP,) + array.shape[1:], lambda i: (start // GROUP + i, 0, 0))
+
+    def one_of(array, _, at):
+        return pl.BlockSpec((1,) + array.shape[1:], lambda i: (at, 0, 0))
 
     def kv_scratch(group):
         return pltpu.VMEM((parts, group, part_tokens, 2 * width), jnp.bfloat16)
@@ -137,8 +144,8 @@
         grid=(blocks // GROUP,),
         out_shape=(out, out),
         in_specs=[pl.BlockSpec(memory_space=pltpu.SMEM), tile, next_tile, tile, next_tile]
-        + [pl.BlockSpec((GROUP,) + p.shape[1:], lambda i: (i, 0, 0)) for p in pieces]
-        + [pl.BlockSpec((1,) + p.shape[1:], lambda i: (blocks, 0, 0)) for p in pieces]
+        + [group_of(*piece) for piece in pieces]
+        + [one_of(*piece) for piece in pieces]
         + [whole(h) for h in held],
         out_specs=(tile, tile),
         scratch_shapes=[
@@ -147,14 +154,14 @@
             kv_scratch(1),
             pltpu.VMEM((2, BLOCK, width), jnp.float32),
         ],
-        compiler_params=pltpu.CompilerParams(vmem_limit_bytes=32 * 1024 * 1024),
+        compiler_params=pltpu.CompilerParams(vmem_limit_bytes=56 * 1024 * 1024),
         cost_estimate=pl.CostEstimate(
             flops=2 * (blocks + 1) * keys * 2 * width * (FEATURES + 2 * BLOCK),
             bytes_accessed=2 * (blocks * keys * FEATURES + 4 * tokens * width),
             transcendentals=blocks * keys * BLOCK * width // DH,
         ),
         name="blocks",
-    )(place, queries, queries, grads, grads, *pieces, *pieces, *held)
+    )(place, queries, queries, grads, grads, *arrays, *arrays, *held)
 
 
 def body(queries, context_grad, database, neighbour_ids, owner_map, key_weight, value_weight):
@@ -180,6 +187,7 @@
         axis=0,
         dtype=jnp.int32,
     )
+    asked_rows, key_weight = lax.optimization_barrier((asked_rows, key_weight))
     wanted = lax.all_to_all(
         asked_rows.reshape(seq_count, 1), "seq", split_axis=0, concat_axis=0, tiled=True
     ).reshape(-1)
@@ -211,16 +219,30 @@
         return lax.ppermute(value, "head", [(i, i ^ 1) for i in range(head_devices)])
 
     half = enc_width // 2
-    before, after = along_x(asked, 1), along_x(asked, -1)
-    across = along_x(before[:, :, :half], 1), along_x(after[:, :, half:], -1)
-    pieces = [asked, before, after, *across]
-    pieces += [other_core(piece) for piece in pieces]
-    pieces = [piece.reshape(-1, 2 * part_tokens, piece.shape[-1]) for piece in pieces]
-
-    held = [weight]
+    def together(came, own):
+        return jnp.concatenate([came[:-2], own[:-2], came[-2:], own[-2:]], axis=0)
+
+    low, high = asked[:, :, :half], asked[:, :, half:]
+    before_low, after_high = along_x(low, 1), along_x(high, -1)
+    up, down = along_x(together(before_low, high), 1), along_x(together(after_high, low), -1)
+    held = []
     for step in range(1, y_count):
         pairs = [(i, (i + step * Z) % seq_count) for i in range(seq_count)]
         held.append(lax.ppermute(weight, "seq", pairs))
+    near = [asked, before_low, after_high]
+    swapped = [other_core(a) for a in near]
+    up, down, swapped, held = lax.optimization_barrier((up, down, swapped, held))
+    held = [weight, *held]
+    blocks = queries.shape[0] // BLOCK
+    pieces = []
+    for arrays in (near + [up, down], swapped + [other_core(up), other_core(down)]):
+        arrays = [a.reshape(-1, 2 * part_tokens, a.shape[-1]) for a in arrays]
+        asked, before_low, after_high, up, down = arrays
+        pieces += [(asked, 0, blocks)]
+        pieces += [(before_low, 0, blocks), (up, blocks, 2 * blocks + 1)]
+        pieces += [(down, blocks, 2 * blocks + 1), (after_high, 0, blocks)]
+        pieces += [(up, 0, 2 * blocks), (down, 0, 2 * blocks)]
+
     my_seq = lax.axis_index("seq")
     place = jnp.stack([my_seq // Z, my_seq % Z]).astype(jnp.int32)
     return attention(place, queries, context_grad, pieces, held)

time: 237 us -> 233 us (0.983)
  local copies, waits for them, and re-layouts: 13.4 us -> 6.73 us
    ppermute x4, waiting for transfers between devices: 18.7 us -> 4.26 us  [along_x(): lax.ppermute(value, 'head', [(i, (i + 2 * steps) % head_devices) for i in...]
    ppermute x3, waiting for transfers between devices: 0.01 us -> 12.8 us  [body(): held.append(lax.ppermute(weight, 'seq', pairs))]
    unnamed x22 -> x28, local copies, waits for them, and re-layouts: 8.8 us -> 1.86 us
    ppermute x3, starting transfers between devices: 9.79 us -> 6.98 us  [body(): held.append(lax.ppermute(weight, 'seq', pairs))]
where the time goes in v5:
time: 233 us; the launch traced here: 230 us
  waiting for transfers between devices  118 us (51%)
  starting transfers between devices  87 us (37%)
  Pallas kernels  13.3 us (6%)
  local copies, waits for them, and re-layouts  6.73 us (3%)
  other arithmetic  4.04 us (2%)
    ppermute x5, waiting for transfers between devices, from_z(): return lax.ppermute(value, 'seq', [(i, i ^ step) for i in range(seq_count)])  85.2 us
    ppermute x5, starting transfers between devices, from_z(): return lax.ppermute(value, 'seq', [(i, i ^ step) for i in range(seq_count)])  33.1 us
    ppermute x4, starting transfers between devices, along_x(): lax.ppermute(value, 'head', [(i, (i + 2 * steps) % head_devices) for i in...  14.1 us
    pallas_call x1, Pallas kernels, attention(): pl.pallas_call(functools.partial(main_kernel, len(pieces)), grid=(blocks...  13.3 us
    ppermute x3, waiting for transfers between devices, body(): held.append(lax.ppermute(weight, 'seq', pairs))  12.8 us
    all_to_all x1, starting transfers between devices, body(): lax.all_to_all(outgoing, 'seq', split_axis=0, concat_axis=0, tiled=True)  12.2 us
    ppermute x5, starting transfers between devices, other_core(): lax.ppermute(value, 'head', [(i, i ^ 1) for i in range(head_devices)])  10.1 us
    all_to_all x1, starting transfers between devices, body(): lax.all_to_all(asked_rows.reshape(seq_count, 1), 'seq', split_axis=0, con...  8.64 us
  transfers between devices with their start and end apart: 20, of which 10 were waited for; matrix products, arithmetic and copies ran while one was open for 2% of the time, Pallas kernels for 0%

profile of v5, /device:TPU:24, one launch (start us, length us, event | category | flops | bytes accessed | tf_op | source)
XLA Modules:
  0.0 230.2 jit_solution(16018184419060951492)
XLA Ops:
  3.2 15.7 %collective-permute-start = (bf16[1,16,512]{2,1,0:T(8,128)(2,1)S(1)}, bf16[1,16,512]{2,1,0:T(8,128)(2,1)S(1)}, u32[]{:S(2)}, u32[]{:S(2)}) collective-permute-start(bf16[1,16,512]{2,1,0:T(8,128)(2,1)S(1)} %maximum_bitcast_fusion), channel_id=1, source_target_pairs={{0,64},{8,72},{16,80},{24,88},{32,96},{40,104},{48,112},{56,120},{... | collective-permute-start | bytes 49160 | tf_op jit(solution)/shard_map/ppermute | solution.py:196
  19.6 8.6 %all-to-all-start = ((s32[64,1,1]{2,1,0:T(1,128)}), s32[64,1,1]{2,1,0:T(1,128)S(1)}, u32[]{:S(2)}, u32[]{:S(2)}) async-start(s32[64,1,1]{2,1,0:T(1,128)} %copy.16), calls=%async_computation | async-start | bytes 65536 | tf_op jit(solution)/shard_map/all_to_all | solution.py:191
  28.3 7.3 %collective-permute-start.1 = (bf16[2,16,512]{2,1,0:T(8,128)(2,1)S(1)}, bf16[2,16,512]{2,1,0:T(8,128)(2,1)S(1)}, u32[]{:S(2)}, u32[]{:S(2)}) collective-permute-start(bf16[2,16,512]{2,1,0:T(8,128)(2,1)S(1)} %pad_maximum_fusion.4), channel_id=1, source_target_pairs={{0,32},{8,40},{16,48},{24,56},{32,0},{40,8},{48,16},{56,24},{64,96... | collective-permute-start | bytes 98312 | tf_op jit(solution)/shard_map/ppermute | solution.py:196
  36.7 4.1 %all-to-all-done = s32[64,1,1]{2,1,0:T(1,128)S(1)} async-done(((s32[64,1,1]{2,1,0:T(1,128)}), s32[64,1,1]{2,1,0:T(1,128)S(1)}, u32[]{:S(2)}, u32[]{:S(2)}) %all-to-all-start) | async-done | bytes 288 | tf_op jit(solution)/shard_map/all_to_all | solution.py:191
  40.8 1.2 reduce
  42.1 2.0 gather_fusion
  44.1 12.2 %all-to-all-start.1 = ((bf16[64,16,1024]{2,1,0:T(8,128)(2,1)}), bf16[64,16,1024]{2,1,0:T(8,128)(2,1)S(1)}, u32[]{:S(2)}, u32[]{:S(2)}) async-start(bf16[64,16,1024]{2,1,0:T(8,128)(2,1)} %gather_fusion), calls=%async_computation.1 | async-start | bytes 4194304 | tf_op jit(solution)/shard_map/all_to_all | solution.py:207
  56.3 5.2 %collective-permute-start.4 = (bf16[4,16,512]{2,1,0:T(8,128)(2,1)S(1)}, bf16[4,16,512]{2,1,0:T(8,128)(2,1)S(1)}, u32[]{:S(2)}, u32[]{:S(2)}) collective-permute-start(bf16[4,16,512]{2,1,0:T(8,128)(2,1)S(1)} %pad_maximum_fusion.3), channel_id=1, source_target_pairs={{0,24},{8,16},{16,8},{24,0},{32,56},{40,48},{48,40},{56,32},{64,88... | collective-permute-start | bytes 196616 | tf_op jit(solution)/shard_map/ppermute | solution.py:196
  61.5 1.9 collective-permute-start.3
  63.4 3.0 %collective-permute-start.2 = (bf16[4,16,512]{2,1,0:T(8,128)(2,1)S(1)}, bf16[4,16,512]{2,1,0:T(8,128)(2,1)S(1)}, u32[]{:S(2)}, u32[]{:S(2)}) collective-permute-start(bf16[4,16,512]{2,1,0:T(8,128)(2,1)S(1)} %pad_maximum_fusion.3), channel_id=1, source_target_pairs={{0,8},{8,0},{16,24},{24,16},{32,40},{40,32},{48,56},{56,48},{64,72... | collective-permute-start | bytes 196616 | tf_op jit(solution)/shard_map/ppermute | solution.py:196
  66.4 81.6 %collective-permute-done.4 = bf16[4,16,512]{2,1,0:T(8,128)(2,1)S(1)} collective-permute-done((bf16[4,16,512]{2,1,0:T(8,128)(2,1)S(1)}, bf16[4,16,512]{2,1,0:T(8,128)(2,1)S(1)}, u32[]{:S(2)}, u32[]{:S(2)}) %collective-permute-start.4) | collective-permute-done | bytes 65568 | tf_op jit(solution)/shard_map/ppermute | solution.py:196
  148.0 3.6 %collective-permute-done.3 = bf16[4,16,512]{2,1,0:T(8,128)(2,1)S(1)} collective-permute-done((bf16[4,16,512]{2,1,0:T(8,128)(2,1)S(1)}, bf16[4,16,512]{2,1,0:T(8,128)(2,1)S(1)}, u32[]{:S(2)}, u32[]{:S(2)}) %collective-permute-start.3) | collective-permute-done | bytes 65568 | tf_op jit(solution)/shard_map/ppermute | solution.py:196
  153.2 1.9 collective-permute-start.5
  155.2 7.1 %collective-permute-done.5 = bf16[2,16,1024]{2,1,0:T(8,128)(2,1)S(1)} collective-permute-done((bf16[2,16,1024]{2,1,0:T(8,128)(2,1)S(1)}, bf16[2,16,1024]{2,1,0:T(8,128)(2,1)S(1)}, u32[]{:S(2)}, u32[]{:S(2)}) %collective-permute-start.5) | collective-permute-done | bytes 65568 | tf_op jit(solution)/shard_map/ppermute | solution.py:20
  162.5 3.4 %collective-permute-start.6 = (bf16[34,16,512]{2,1,0:T(8,128)(2,1)S(1)}, bf16[34,16,512]{2,1,0:T(8,128)(2,1)S(1)}, u32[]{:S(2)}, u32[]{:S(2)}) collective-permute-start(bf16[34,16,512]{2,1,0:T(8,128)(2,1)S(1)} %get-tuple-element.35), channel_id=1, source_target_pairs={{0,2},{1,3},{2,4},{3,5},{4,6},{5,7},{6,0},{7,1},{8,10},{9,11},{10,... | collective-permute-start | bytes 1671176 | tf_op jit(solution)/shard_map/ppermute | solution.py:214
  165.9 3.7 %collective-permute-start.8 = (bf16[34,16,512]{2,1,0:T(8,128)(2,1)S(1)}, bf16[34,16,512]{2,1,0:T(8,128)(2,1)S(1)}, u32[]{:S(2)}, u32[]{:S(2)}) collective-permute-start(bf16[34,16,512]{2,1,0:T(8,128)(2,1)S(1)} %get-tuple-element.34), channel_id=1, source_target_pairs={{0,6},{1,7},{2,0},{3,1},{4,2},{5,3},{6,4},{7,5},{8,14},{9,15},{10,... | collective-permute-start | bytes 1671176 | tf_op jit(solution)/shard_map/ppermute | solution.py:214
  169.6 1.9 collective-permute-start.10
  171.6 4.3 %collective-permute-done.6 = bf16[34,16,512]{2,1,0:T(8,128)(2,1)S(1)} collective-permute-done((bf16[34,16,512]{2,1,0:T(8,128)(2,1)S(1)}, bf16[34,16,512]{2,1,0:T(8,128)(2,1)S(1)}, u32[]{:S(2)}, u32[]{:S(2)}) %collective-permute-start.6) | collective-permute-done | bytes 557088 | tf_op jit(solution)/shard_map/ppermute | solution.py:214
  176.1 2.2 collective-permute-start.7
  178.5 4.9 %collective-permute-start.9 = (bf16[68,16,512]{2,1,0:T(8,128)(2,1)S(1)}, bf16[68,16,512]{2,1,0:T(8,128)(2,1)S(1)}, u32[]{:S(2)}, u32[]{:S(2)}) collective-permute-start(bf16[68,16,512]{2,1,0:T(8,128)(2,1)S(1)} %pad_maximum_fusion.1), channel_id=1, source_target_pairs={{0,6},{1,7},{2,0},{3,1},{4,2},{5,3},{6,4},{7,5},{8,14},{9,15},{10,... | collective-permute-start | bytes 3342344 | tf_op jit(solution)/shard_map/ppermute | solution.py:214
  183.4 2.7 %collective-permute-start.15 = (bf16[16,16,512]{2,1,0:T(8,128)(2,1)S(1)}, bf16[16,16,512]{2,1,0:T(8,128)(2,1)S(1)}, u32[]{:S(2)}, u32[]{:S(2)}) collective-permute-start(bf16[16,16,512]{2,1,0:T(8,128)(2,1)S(1)} %pad_maximum_fusion.2.refs_28_), channel_id=1, source_target_pairs={{0,384},{8,392},{16,400},{24,408},{32,416},{40,424},{48,432},{56,4... | collective-permute-start | bytes 786440 | tf_op jit(solution)/shard_map/ppermute | solution.py:231
  186.1 2.4 %collective-permute-start.14 = (bf16[16,16,512]{2,1,0:T(8,128)(2,1)S(1)}, bf16[16,16,512]{2,1,0:T(8,128)(2,1)S(1)}, u32[]{:S(2)}, u32[]{:S(2)}) collective-permute-start(bf16[16,16,512]{2,1,0:T(8,128)(2,1)S(1)} %pad_maximum_fusion.2.refs_28_), channel_id=1, source_target_pairs={{0,256},{8,264},{16,272},{24,280},{32,288},{40,296},{48,304},{56,3... | collective-permute-start | bytes 786440 | tf_op jit(solution)/shard_map/ppermute | solution.py:231
  188.5 8.5 %collective-permute-done.15.refs_31_ = bf16[16,16,512]{2,1,0:T(8,128)(2,1)S(1)} collective-permute-done((bf16[16,16,512]{2,1,0:T(8,128)(2,1)S(1)}, bf16[16,16,512]{2,1,0:T(8,128)(2,1)S(1)}, u32[]{:S(2)}, u32[]{:S(2)}) %collective-permute-start.15) | collective-permute-done | bytes 262176 | tf_op jit(solution)/shard_map/ppermute | solution.py:231
  197.0 1.9 collective-permute-start.13
  198.9 1.9 collective-permute-start.12
  200.8 4.4 %collective-permute-done.13.refs_29_ = bf16[16,16,512]{2,1,0:T(8,128)(2,1)S(1)} collective-permute-done((bf16[16,16,512]{2,1,0:T(8,128)(2,1)S(1)}, bf16[16,16,512]{2,1,0:T(8,128)(2,1)S(1)}, u32[]{:S(2)}, u32[]{:S(2)}) %collective-permute-start.13) | collective-permute-done | bytes 262176 | tf_op jit(solution)/shard_map/ppermute | solution.py:231
  205.2 1.9 collective-permute-start.11
  207.2 1.9 collective-permute-done.11
  210.1 2.0 collective-permute-start.16
  212.2 2.3 collective-permute-start.17
  215.1 1.8 collective-permute-done.17
  217.0 13.3 %blocks.1 = (bf16[1024,256]{1,0:T(8,128)(2,1)}, bf16[1024,256]{1,0:T(8,128)(2,1)}) custom-call(s32[2]{0:T(128)} %pad_add_fusion.place_ref, bf16[1024,256]{1,0:T(8,128)(2,1)} %next_query_ref.1, bf16[1024,256]{1,0:T(8,128)(2,1)} %next_query_ref.1, bf16[1024,256]{1,0:T(8,128)(2,1)} %next_grad_ref.1, bf16[1024,256]{1,0:T(8,128)(2,1)} %next_grad_ref.1, ...), custom_call_target="tpu_custom_call" | custom-call | flops 5133828096 | bytes 10485760 | tf_op jit(solution)/shard_map/blocks/pallas_call | solution.py:142
  (66 shorter events, 8.4 us)
Async XLA Ops:
  3.2 25.1 %collective-permute-start = (bf16[1,16,512]{2,1,0:T(8,128)(2,1)S(1)}, bf16[1,16,512]{2,1,0:T(8,128)(2,1)S(1)}, u32[]{:S(2)}, u32[]{:S(2)}) collective-permute-start(bf16[1,16,512]{2,1,0:T(8,128)(2,1)S(1)} %maximum_bitcast_fusion), channel_id=1, source_target_pairs={{0,64},{8,72},{16,80},{24,88},{32,96},{40,104},{48,112},{56,120},{... | collective-permute-start | bytes 49160 | tf_op jit(solution)/shard_map/ppermute | solution.py:196
  19.6 21.2 %all-to-all-start = ((s32[64,1,1]{2,1,0:T(1,128)}), s32[64,1,1]{2,1,0:T(1,128)S(1)}, u32[]{:S(2)}, u32[]{:S(2)}) async-start(s32[64,1,1]{2,1,0:T(1,128)} %copy.16), calls=%async_computation | async-start | bytes 65536 | tf_op jit(solution)/shard_map/all_to_all | solution.py:191
  28.3 13.7 %collective-permute-start.1 = (bf16[2,16,512]{2,1,0:T(8,128)(2,1)S(1)}, bf16[2,16,512]{2,1,0:T(8,128)(2,1)S(1)}, u32[]{:S(2)}, u32[]{:S(2)}) collective-permute-start(bf16[2,16,512]{2,1,0:T(8,128)(2,1)S(1)} %pad_maximum_fusion.4), channel_id=1, source_target_pairs={{0,32},{8,40},{16,48},{24,56},{32,0},{40,8},{48,16},{56,24},{64,96... | collective-permute-start | bytes 98312 | tf_op jit(solution)/shard_map/ppermute | solution.py:196
  44.1 108.4 %all-to-all-start.1 = ((bf16[64,16,1024]{2,1,0:T(8,128)(2,1)}), bf16[64,16,1024]{2,1,0:T(8,128)(2,1)S(1)}, u32[]{:S(2)}, u32[]{:S(2)}) async-start(bf16[64,16,1024]{2,1,0:T(8,128)(2,1)} %gather_fusion), calls=%async_computation.1 | async-start | bytes 4194304 | tf_op jit(solution)/shard_map/all_to_all | solution.py:207
  56.3 91.7 %collective-permute-start.4 = (bf16[4,16,512]{2,1,0:T(8,128)(2,1)S(1)}, bf16[4,16,512]{2,1,0:T(8,128)(2,1)S(1)}, u32[]{:S(2)}, u32[]{:S(2)}) collective-permute-start(bf16[4,16,512]{2,1,0:T(8,128)(2,1)S(1)} %pad_maximum_fusion.3), channel_id=1, source_target_pairs={{0,24},{8,16},{16,8},{24,0},{32,56},{40,48},{48,40},{56,32},{64,88... | collective-permute-start | bytes 196616 | tf_op jit(solution)/shard_map/ppermute | solution.py:196
  61.5 90.2 %collective-permute-start.3 = (bf16[4,16,512]{2,1,0:T(8,128)(2,1)S(1)}, bf16[4,16,512]{2,1,0:T(8,128)(2,1)S(1)}, u32[]{:S(2)}, u32[]{:S(2)}) collective-permute-start(bf16[4,16,512]{2,1,0:T(8,128)(2,1)S(1)} %pad_maximum_fusion.3), channel_id=1, source_target_pairs={{0,16},{8,24},{16,0},{24,8},{32,48},{40,56},{48,32},{56,40},{64,80... | collective-permute-start | bytes 196616 | tf_op jit(solution)/shard_map/ppermute | solution.py:196
  63.4 88.2 %collective-permute-start.2 = (bf16[4,16,512]{2,1,0:T(8,128)(2,1)S(1)}, bf16[4,16,512]{2,1,0:T(8,128)(2,1)S(1)}, u32[]{:S(2)}, u32[]{:S(2)}) collective-permute-start(bf16[4,16,512]{2,1,0:T(8,128)(2,1)S(1)} %pad_maximum_fusion.3), channel_id=1, source_target_pairs={{0,8},{8,0},{16,24},{24,16},{32,40},{40,32},{48,56},{56,48},{64,72... | collective-permute-start | bytes 196616 | tf_op jit(solution)/shard_map/ppermute | solution.py:196
  151.7 45.3 %copy-start.9 = (bf16[16,16,512]{2,1,0:T(8,128)(2,1)}, bf16[16,16,512]{2,1,0:T(8,128)(2,1)S(1)}, u32[]{:S(2)}) copy-start(bf16[16,16,512]{2,1,0:T(8,128)(2,1)S(1)} %pad_maximum_fusion.2.refs_28_) | copy-start | bytes 786436
  153.2 9.1 %collective-permute-start.5 = (bf16[2,16,1024]{2,1,0:T(8,128)(2,1)S(1)}, bf16[2,16,1024]{2,1,0:T(8,128)(2,1)S(1)}, u32[]{:S(2)}, u32[]{:S(2)}) collective-permute-start(bf16[2,16,1024]{2,1,0:T(8,128)(2,1)S(1)} %slice.41), channel_id=1, source_target_pairs={{0,8},{8,16},{16,24},{24,32},{32,40},{40,48},{48,56},{56,64},{64,7... | collective-permute-start | bytes 196616 | tf_op jit(solution)/shard_map/ppermute | solution.py:20
  162.3 7.3 %copy-start.3 = (bf16[34,16,1024]{2,1,0:T(8,128)(2,1)}, bf16[34,16,1024]{2,1,0:T(8,128)(2,1)S(1)}, u32[]{:S(2)}) copy-start(bf16[34,16,1024]{2,1,0:T(8,128)(2,1)S(1)} %constant_dynamic-update-slice_fusion) | copy-start | bytes 3342340
  162.5 13.4 %collective-permute-start.6 = (bf16[34,16,512]{2,1,0:T(8,128)(2,1)S(1)}, bf16[34,16,512]{2,1,0:T(8,128)(2,1)S(1)}, u32[]{:S(2)}, u32[]{:S(2)}) collective-permute-start(bf16[34,16,512]{2,1,0:T(8,128)(2,1)S(1)} %get-tuple-element.35), channel_id=1, source_target_pairs={{0,2},{1,3},{2,4},{3,5},{4,6},{5,7},{6,0},{7,1},{8,10},{9,11},{10,... | collective-permute-start | bytes 1671176 | tf_op jit(solution)/shard_map/ppermute | solution.py:214
  165.9 12.4 %collective-permute-start.8 = (bf16[34,16,512]{2,1,0:T(8,128)(2,1)S(1)}, bf16[34,16,512]{2,1,0:T(8,128)(2,1)S(1)}, u32[]{:S(2)}, u32[]{:S(2)}) collective-permute-start(bf16[34,16,512]{2,1,0:T(8,128)(2,1)S(1)} %get-tuple-element.34), channel_id=1, source_target_pairs={{0,6},{1,7},{2,0},{3,1},{4,2},{5,3},{6,4},{7,5},{8,14},{9,15},{10,... | collective-permute-start | bytes 1671176 | tf_op jit(solution)/shard_map/ppermute | solution.py:214
  169.6 39.4 %collective-permute-start.10 = (bf16[34,16,1024]{2,1,0:T(8,128)(2,1)S(1)}, bf16[34,16,1024]{2,1,0:T(8,128)(2,1)S(1)}, u32[]{:S(2)}, u32[]{:S(2)}) collective-permute-start(bf16[34,16,1024]{2,1,0:T(8,128)(2,1)S(1)} %constant_dynamic-update-slice_fusion), channel_id=1, source_target_pairs={{0,1},{1,0},{2,3},{3,2},{4,5},{5,4},{6,7},{7,6},{8,9},{9,8},{10,11... | collective-permute-start | bytes 3342344 | tf_op jit(solution)/shard_map/ppermute | solution.py:219
  175.8 29.4 %copy-start.4 = (bf16[34,16,512]{2,1,0:T(8,128)(2,1)}, bf16[34,16,512]{2,1,0:T(8,128)(2,1)S(1)}, u32[]{:S(2)}) copy-start(bf16[34,16,512]{2,1,0:T(8,128)(2,1)S(1)} %collective-permute-done.6) | copy-start | bytes 1671172
  176.1 33.0 %collective-permute-start.7 = (bf16[68,16,512]{2,1,0:T(8,128)(2,1)S(1)}, bf16[68,16,512]{2,1,0:T(8,128)(2,1)S(1)}, u32[]{:S(2)}, u32[]{:S(2)}) collective-permute-start(bf16[68,16,512]{2,1,0:T(8,128)(2,1)S(1)} %pad_maximum_fusion), channel_id=1, source_target_pairs={{0,2},{1,3},{2,4},{3,5},{4,6},{5,7},{6,0},{7,1},{8,10},{9,11},{10,... | collective-permute-start | bytes 3342344 | tf_op jit(solution)/shard_map/ppermute | solution.py:214
  178.3 20.6 %copy-start.5 = (bf16[34,16,512]{2,1,0:T(8,128)(2,1)}, bf16[34,16,512]{2,1,0:T(8,128)(2,1)S(1)}, u32[]{:S(2)}) copy-start(bf16[34,16,512]{2,1,0:T(8,128)(2,1)S(1)} %collective-permute-done.8) | copy-start | bytes 1671172
  178.5 30.6 %collective-permute-start.9 = (bf16[68,16,512]{2,1,0:T(8,128)(2,1)S(1)}, bf16[68,16,512]{2,1,0:T(8,128)(2,1)S(1)}, u32[]{:S(2)}, u32[]{:S(2)}) collective-permute-start(bf16[68,16,512]{2,1,0:T(8,128)(2,1)S(1)} %pad_maximum_fusion.1), channel_id=1, source_target_pairs={{0,6},{1,7},{2,0},{3,1},{4,2},{5,3},{6,4},{7,5},{8,14},{9,15},{10,... | collective-permute-start | bytes 3342344 | tf_op jit(solution)/shard_map/ppermute | solution.py:214
  183.4 13.5 %collective-permute-start.15 = (bf16[16,16,512]{2,1,0:T(8,128)(2,1)S(1)}, bf16[16,16,512]{2,1,0:T(8,128)(2,1)S(1)}, u32[]{:S(2)}, u32[]{:S(2)}) collective-permute-start(bf16[16,16,512]{2,1,0:T(8,128)(2,1)S(1)} %pad_maximum_fusion.2.refs_28_), channel_id=1, source_target_pairs={{0,384},{8,392},{16,400},{24,408},{32,416},{40,424},{48,432},{56,4... | collective-permute-start | bytes 786440 | tf_op jit(solution)/shard_map/ppermute | solution.py:231
  186.1 12.8 %collective-permute-start.14 = (bf16[16,16,512]{2,1,0:T(8,128)(2,1)S(1)}, bf16[16,16,512]{2,1,0:T(8,128)(2,1)S(1)}, u32[]{:S(2)}, u32[]{:S(2)}) collective-permute-start(bf16[16,16,512]{2,1,0:T(8,128)(2,1)S(1)} %pad_maximum_fusion.2.refs_28_), channel_id=1, source_target_pairs={{0,256},{8,264},{16,272},{24,280},{32,288},{40,296},{48,304},{56,3... | collective-permute-start | bytes 786440 | tf_op jit(solution)/shard_map/ppermute | solution.py:231
  197.0 12.1 %copy-start.10 = (bf16[16,16,512]{2,1,0:T(8,128)(2,1)}, bf16[16,16,512]{2,1,0:T(8,128)(2,1)S(1)}, u32[]{:S(2)}) copy-start(bf16[16,16,512]{2,1,0:T(8,128)(2,1)S(1)} %collective-permute-done.15.refs_31_) | copy-start | bytes 786436
  197.0 8.3 %collective-permute-start.13 = (bf16[16,16,512]{2,1,0:T(8,128)(2,1)S(1)}, bf16[16,16,512]{2,1,0:T(8,128)(2,1)S(1)}, u32[]{:S(2)}, u32[]{:S(2)}) collective-permute-start(bf16[16,16,512]{2,1,0:T(8,128)(2,1)S(1)} %pad_maximum_fusion.2.refs_28_), channel_id=1, source_target_pairs={{0,128},{8,136},{16,144},{24,152},{32,160},{40,168},{48,176},{56,1... | collective-permute-start | bytes 786440 | tf_op jit(solution)/shard_map/ppermute | solution.py:231
  198.9 10.2 %copy-start.11 = (bf16[16,16,512]{2,1,0:T(8,128)(2,1)}, bf16[16,16,512]{2,1,0:T(8,128)(2,1)S(1)}, u32[]{:S(2)}) copy-start(bf16[16,16,512]{2,1,0:T(8,128)(2,1)S(1)} %collective-permute-done.14.refs_30_) | copy-start | bytes 786436
  198.9 8.2 %collective-permute-start.12 = (bf16[34,16,512]{2,1,0:T(8,128)(2,1)S(1)}, bf16[34,16,512]{2,1,0:T(8,128)(2,1)S(1)}, u32[]{:S(2)}, u32[]{:S(2)}) collective-permute-start(bf16[34,16,512]{2,1,0:T(8,128)(2,1)S(1)} %collective-permute-done.8), channel_id=1, source_target_pairs={{0,1},{1,0},{2,3},{3,2},{4,5},{5,4},{6,7},{7,6},{8,9},{9,8},{10,11... | collective-permute-start | bytes 1671176 | tf_op jit(solution)/shard_map/ppermute | solution.py:219
  205.2 3.9 %copy-start.12 = (bf16[16,16,512]{2,1,0:T(8,128)(2,1)}, bf16[16,16,512]{2,1,0:T(8,128)(2,1)S(1)}, u32[]{:S(2)}) copy-start(bf16[16,16,512]{2,1,0:T(8,128)(2,1)S(1)} %collective-permute-done.13.refs_29_) | copy-start | bytes 786436
  205.2 3.8 %collective-permute-start.11 = (bf16[34,16,512]{2,1,0:T(8,128)(2,1)S(1)}, bf16[34,16,512]{2,1,0:T(8,128)(2,1)S(1)}, u32[]{:S(2)}, u32[]{:S(2)}) collective-permute-start(bf16[34,16,512]{2,1,0:T(8,128)(2,1)S(1)} %collective-permute-done.6), channel_id=1, source_target_pairs={{0,1},{1,0},{2,3},{3,2},{4,5},{5,4},{6,7},{7,6},{8,9},{9,8},{10,11... | collective-permute-start | bytes 1671176 | tf_op jit(solution)/shard_map/ppermute | solution.py:219
  207.1 5.0 %copy-start.7 = (bf16[34,16,512]{2,1,0:T(8,128)(2,1)}, bf16[34,16,512]{2,1,0:T(8,128)(2,1)S(1)}, u32[]{:S(2)}) copy-start(bf16[34,16,512]{2,1,0:T(8,128)(2,1)S(1)} %collective-permute-done.12) | copy-start | bytes 1671172
  209.1 3.1 %copy-start.8 = (bf16[34,16,512]{2,1,0:T(8,128)(2,1)}, bf16[34,16,512]{2,1,0:T(8,128)(2,1)S(1)}, u32[]{:S(2)}) copy-start(bf16[34,16,512]{2,1,0:T(8,128)(2,1)S(1)} %collective-permute-done.11) | copy-start | bytes 1671172
  209.1 7.8 %copy-start = (bf16[68,16,512]{2,1,0:T(8,128)(2,1)}, bf16[68,16,512]{2,1,0:T(8,128)(2,1)S(1)}, u32[]{:S(2)}) copy-start(bf16[68,16,512]{2,1,0:T(8,128)(2,1)S(1)} %collective-permute-done.7) | copy-start | bytes 3342340
  210.1 6.8 %copy-start.1 = (bf16[68,16,512]{2,1,0:T(8,128)(2,1)}, bf16[68,16,512]{2,1,0:T(8,128)(2,1)S(1)}, u32[]{:S(2)}) copy-start(bf16[68,16,512]{2,1,0:T(8,128)(2,1)S(1)} %collective-permute-done.9) | copy-start | bytes 3342340
  210.1 5.0 %collective-permute-start.16 = (bf16[68,16,512]{2,1,0:T(8,128)(2,1)S(1)}, bf16[68,16,512]{2,1,0:T(8,128)(2,1)S(1)}, u32[]{:S(2)}, u32[]{:S(2)}) collective-permute-start(bf16[68,16,512]{2,1,0:T(8,128)(2,1)S(1)} %collective-permute-done.7), channel_id=1, source_target_pairs={{0,1},{1,0},{2,3},{3,2},{4,5},{5,4},{6,7},{7,6},{8,9},{9,8},{10,11... | collective-permute-start | bytes 3342344 | tf_op jit(solution)/shard_map/ppermute | solution.py:219
  212.2 4.8 %collective-permute-start.17 = (bf16[68,16,512]{2,1,0:T(8,128)(2,1)S(1)}, bf16[68,16,512]{2,1,0:T(8,128)(2,1)}, u32[]{:S(2)}, u32[]{:S(2)}) collective-permute-start(bf16[68,16,512]{2,1,0:T(8,128)(2,1)S(1)} %collective-permute-done.9), channel_id=1, source_target_pairs={{0,1},{1,0},{2,3},{3,2},{4,5},{5,4},{6,7},{7,6},{8,9},{9,8},{10,11... | collective-permute-start | bytes 3342344 | tf_op jit(solution)/shard_map/ppermute | solution.py:219
  215.1 1.8 copy-start.2
  (1 other events, 1.0 us)

commit v6 on v5

--- a/solution.py
+++ b/solution.py
@@ -88,10 +88,11 @@
     @pl.when(pl.program_id(0) == 0)
     def _():
         rows = held_refs[0].shape[1]
-        for step, held_ref in enumerate(held_refs):
-            y = lax.rem(place_ref[0] + len(held_refs) - step, len(held_refs))
-            for m in range(Z):
-                at = (m & 3) * 4 + (m >> 2 & 1) * 2 + (m >> 3)
+        y_count = len(held_refs) // 2
+        for k, held_ref in enumerate(held_refs):
+            y = lax.rem(place_ref[0] + y_count - k // 2, y_count)
+            for at in range(held_ref.shape[0]):
+                m = (at & 1) * 8 + (at >> 1 & 1) * 4 + (at >> 2) * 2 + k % 2
                 start = (y * Z + (place_ref[1] ^ m)) * rows
                 weight_ref[pl.ds(pl.multiple_of(start, 16), rows), :] = held_ref[at]
         project(before_refs, weight_ref, before_kv_ref)
@@ -192,22 +193,26 @@
         asked_rows.reshape(seq_count, 1), "seq", split_axis=0, concat_axis=0, tiled=True
     ).reshape(-1)
 
-    def from_z(value, step):
-        return lax.ppermute(value, "seq", [(i, i ^ step) for i in range(seq_count)])
+    def moved(value, y_steps, z_flip):
+        pairs = [
+            (i, (i // Z + y_steps) % y_count * Z + (i % Z ^ z_flip)) for i in range(seq_count)
+        ]
+        return lax.ppermute(value, "seq", pairs)
 
     weight = jnp.concatenate([key_weight, value_weight], axis=1)[None]
     for step in (8, 4):
-        weight = jnp.concatenate([weight, from_z(weight, step)], axis=0)
+        weight = jnp.concatenate([weight, moved(weight, 0, step)], axis=0)
 
     parts = database.reshape(local_rows, head_devices, part_tokens, enc_width)
     mine = lax.dynamic_index_in_dim(parts, my_head, axis=1, keepdims=False)
     wanted, weight = lax.optimization_barrier((wanted, weight))
     outgoing = mine[wanted]
+    weight = jnp.concatenate([weight, moved(weight, 0, 2)], axis=0)
     outgoing, weight = lax.optimization_barrier((outgoing, weight))
     incoming = lax.all_to_all(outgoing, "seq", split_axis=0, concat_axis=0, tiled=True)
-    weight = jnp.concatenate([weight] + [from_z(weight, step) for step in (1, 2, 3)], axis=0)
+    held = [moved(weight, k // 2, k % 2) for k in range(1, 2 * y_count)]
     asked = incoming[owner_index]
-    weight, asked = lax.optimization_barrier((weight, asked))
+    asked, held = lax.optimization_barrier((asked, [weight, *held]))
     asked = jnp.concatenate([asked, shifted(asked[-2:], "seq", 1)], axis=0)
 
     def along_x(value, steps):
@@ -225,14 +230,9 @@
     low, high = asked[:, :, :half], asked[:, :, half:]
     before_low, after_high = along_x(low, 1), along_x(high, -1)
     up, down = along_x(together(before_low, high), 1), along_x(together(after_high, low), -1)
-    held = []
-    for step in range(1, y_count):
-        pairs = [(i, (i + step * Z) % seq_count) for i in range(seq_count)]
-        held.append(lax.ppermute(weight, "seq", pairs))
     near = [asked, before_low, after_high]
     swapped = [other_core(a) for a in near]
-    up, down, swapped, held = lax.optimization_barrier((up, down, swapped, held))
-    held = [weight, *held]
+    up, down, swapped = lax.optimization_barrier((up, down, swapped))
     blocks = queries.shape[0] // BLOCK
     pieces = []
     for arrays in (near + [up, down], swapped + [other_core(up), other_core(down)]):

time: 233 us -> 238 us (1.021)
  starting transfers between devices: 87 us -> 101 us
  waiting for transfers between devices: 118 us -> 109 us
    ppermute x8 -> x10, waiting for transfers between devices: 98 us -> 79.3 us  [moved(): return lax.ppermute(value, 'seq', pairs)]
    ppermute x4, waiting for transfers between devices: 4.26 us -> 18.3 us  [along_x(): lax.ppermute(value, 'head', [(i, (i + 2 * steps) % head_devices) for i in...]
    ppermute x8 -> x10, starting transfers between devices: 40.1 us -> 51.3 us  [moved(): return lax.ppermute(value, 'seq', pairs)]
    ppermute x1, waiting for transfers between devices: 7.12 us -> 4.06 us  [shifted(): lax.ppermute(value, axis, [(source, source + steps) for source in range(f...]
  transfers between devices with their start and end apart: 20 -> 22, of which waited for: 10 -> 10; matrix products, arithmetic and copies ran while one was open for 2% -> 3% of each run, Pallas kernels for 0% -> 0%
where the time goes in v6:
time: 238 us; the launch traced here: 234 us
  waiting for transfers between devices  109 us (46%)
  starting transfers between devices  101 us (42%)
  Pallas kernels  13.3 us (6%)
  local copies, waits for them, and re-layouts  6.43 us (3%)
  other arithmetic  4.01 us (2%)
    ppermute x10, waiting for transfers between devices, moved(): return lax.ppermute(value, 'seq', pairs)  79.3 us
    ppermute x10, starting transfers between devices, moved(): return lax.ppermute(value, 'seq', pairs)  51.3 us
    ppermute x4, waiting for transfers between devices, along_x(): lax.ppermute(value, 'head', [(i, (i + 2 * steps) % head_devices) for i in...  18.3 us
    ppermute x4, starting transfers between devices, along_x(): lax.ppermute(value, 'head', [(i, (i + 2 * steps) % head_devices) for i in...  14.1 us
    pallas_call x1, Pallas kernels, attention(): pl.pallas_call(functools.partial(main_kernel, len(pieces)), grid=(blocks...  13.3 us
    all_to_all x1, starting transfers between devices, body(): lax.all_to_all(outgoing, 'seq', split_axis=0, concat_axis=0, tiled=True)  11.8 us
    ppermute x5, starting transfers between devices, other_core(): lax.ppermute(value, 'head', [(i, i ^ 1) for i in range(head_devices)])  10.6 us
    all_to_all x1, starting transfers between devices, body(): lax.all_to_all(asked_rows.reshape(seq_count, 1), 'seq', split_axis=0, con...  8.64 us
  transfers between devices with their start and end apart: 22, of which 10 were waited for; matrix products, arithmetic and copies ran while one was open for 3% of the time, Pallas kernels for 0%

profile of v6, /device:TPU:24, one launch (start us, length us, event | category | flops | bytes accessed | tf_op | source)
XLA Modules:
  0.0 234.5 jit_solution(5966030754979499596)
XLA Ops:
  3.2 15.7 %collective-permute-start = (bf16[1,16,512]{2,1,0:T(8,128)(2,1)S(1)}, bf16[1,16,512]{2,1,0:T(8,128)(2,1)S(1)}, u32[]{:S(2)}, u32[]{:S(2)}) collective-permute-start(bf16[1,16,512]{2,1,0:T(8,128)(2,1)S(1)} %maximum_bitcast_fusion), channel_id=1, source_target_pairs={{0,64},{8,72},{16,80},{24,88},{32,96},{40,104},{48,112},{56,120},{... | collective-permute-start | bytes 49160 | tf_op jit(solution)/shard_map/ppermute | solution.py:200
  19.6 8.6 %all-to-all-start = ((s32[64,1,1]{2,1,0:T(1,128)}), s32[64,1,1]{2,1,0:T(1,128)S(1)}, u32[]{:S(2)}, u32[]{:S(2)}) async-start(s32[64,1,1]{2,1,0:T(1,128)} %copy.16), calls=%async_computation | async-start | bytes 65536 | tf_op jit(solution)/shard_map/all_to_all | solution.py:192
  28.3 7.3 %collective-permute-start.1 = (bf16[2,16,512]{2,1,0:T(8,128)(2,1)S(1)}, bf16[2,16,512]{2,1,0:T(8,128)(2,1)S(1)}, u32[]{:S(2)}, u32[]{:S(2)}) collective-permute-start(bf16[2,16,512]{2,1,0:T(8,128)(2,1)S(1)} %pad_maximum_fusion.4), channel_id=1, source_target_pairs={{0,32},{8,40},{16,48},{24,56},{32,0},{40,8},{48,16},{56,24},{64,96... | collective-permute-start | bytes 98312 | tf_op jit(solution)/shard_map/ppermute | solution.py:200
  36.7 4.1 %all-to-all-done = s32[64,1,1]{2,1,0:T(1,128)S(1)} async-done(((s32[64,1,1]{2,1,0:T(1,128)}), s32[64,1,1]{2,1,0:T(1,128)S(1)}, u32[]{:S(2)}, u32[]{:S(2)}) %all-to-all-start) | async-done | bytes 288 | tf_op jit(solution)/shard_map/all_to_all | solution.py:192
  42.0 2.5 %collective-permute-start.2 = (bf16[4,16,512]{2,1,0:T(8,128)(2,1)S(1)}, bf16[4,16,512]{2,1,0:T(8,128)(2,1)S(1)}, u32[]{:S(2)}, u32[]{:S(2)}) collective-permute-start(bf16[4,16,512]{2,1,0:T(8,128)(2,1)S(1)} %pad_maximum_fusion.3), channel_id=1, source_target_pairs={{0,16},{8,24},{16,0},{24,8},{32,48},{40,56},{48,32},{56,40},{64,80... | collective-permute-start | bytes 196616 | tf_op jit(solution)/shard_map/ppermute | solution.py:200
  44.6 2.0 gather_fusion
  46.6 3.2 %collective-permute-done.2 = bf16[4,16,512]{2,1,0:T(8,128)(2,1)S(1)} collective-permute-done((bf16[4,16,512]{2,1,0:T(8,128)(2,1)S(1)}, bf16[4,16,512]{2,1,0:T(8,128)(2,1)S(1)}, u32[]{:S(2)}, u32[]{:S(2)}) %collective-permute-start.2) | collective-permute-done | bytes 65568 | tf_op jit(solution)/shard_map/ppermute | solution.py:200
  49.8 11.8 %all-to-all-start.1 = ((bf16[64,16,1024]{2,1,0:T(8,128)(2,1)}), bf16[64,16,1024]{2,1,0:T(8,128)(2,1)S(1)}, u32[]{:S(2)}, u32[]{:S(2)}) async-start(bf16[64,16,1024]{2,1,0:T(8,128)(2,1)} %gather_fusion), calls=%async_computation.1 | async-start | bytes 4194304 | tf_op jit(solution)/shard_map/all_to_all | solution.py:212
  61.7 3.6 %collective-permute-start.9 = (bf16[8,16,512]{2,1,0:T(8,128)(2,1)S(1)}, bf16[8,16,512]{2,1,0:T(8,128)(2,1)S(1)}, u32[]{:S(2)}, u32[]{:S(2)}) collective-permute-start(bf16[8,16,512]{2,1,0:T(8,128)(2,1)S(1)} %pad_maximum_fusion.2.refs_28_), channel_id=1, source_target_pairs={{0,392},{8,384},{16,408},{24,400},{32,424},{40,416},{48,440},{56,4... | collective-permute-start | bytes 393224 | tf_op jit(solution)/shard_map/ppermute | solution.py:200
  65.3 2.4 %collective-permute-start.8 = (bf16[8,16,512]{2,1,0:T(8,128)(2,1)S(1)}, bf16[8,16,512]{2,1,0:T(8,128)(2,1)S(1)}, u32[]{:S(2)}, u32[]{:S(2)}) collective-permute-start(bf16[8,16,512]{2,1,0:T(8,128)(2,1)S(1)} %pad_maximum_fusion.2.refs_28_), channel_id=1, source_target_pairs={{0,384},{8,392},{16,400},{24,408},{32,416},{40,424},{48,432},{56,4... | collective-permute-start | bytes 393224 | tf_op jit(solution)/shard_map/ppermute | solution.py:200
  67.6 5.4 %collective-permute-start.7 = (bf16[8,16,512]{2,1,0:T(8,128)(2,1)S(1)}, bf16[8,16,512]{2,1,0:T(8,128)(2,1)}, u32[]{:S(2)}, u32[]{:S(2)}) collective-permute-start(bf16[8,16,512]{2,1,0:T(8,128)(2,1)S(1)} %pad_maximum_fusion.2.refs_28_), channel_id=1, source_target_pairs={{0,264},{8,256},{16,280},{24,272},{32,296},{40,288},{48,312},{56,3... | collective-permute-start | bytes 393224 | tf_op jit(solution)/shard_map/ppermute | solution.py:200
  73.0 2.0 collective-permute-start.6
  75.0 5.6 %collective-permute-start.5 = (bf16[8,16,512]{2,1,0:T(8,128)(2,1)S(1)}, bf16[8,16,512]{2,1,0:T(8,128)(2,1)}, u32[]{:S(2)}, u32[]{:S(2)}) collective-permute-start(bf16[8,16,512]{2,1,0:T(8,128)(2,1)S(1)} %pad_maximum_fusion.2.refs_28_), channel_id=1, source_target_pairs={{0,136},{8,128},{16,152},{24,144},{32,168},{40,160},{48,184},{56,1... | collective-permute-start | bytes 393224 | tf_op jit(solution)/shard_map/ppermute | solution.py:200
  80.6 73.4 %collective-permute-done.9.refs_35_ = bf16[8,16,512]{2,1,0:T(8,128)(2,1)S(1)} collective-permute-done((bf16[8,16,512]{2,1,0:T(8,128)(2,1)S(1)}, bf16[8,16,512]{2,1,0:T(8,128)(2,1)S(1)}, u32[]{:S(2)}, u32[]{:S(2)}) %collective-permute-start.9) | collective-permute-done | bytes 131104 | tf_op jit(solution)/shard_map/ppermute | solution.py:200
  154.0 3.4 %collective-permute-start.4 = (bf16[8,16,512]{2,1,0:T(8,128)(2,1)S(1)}, bf16[8,16,512]{2,1,0:T(8,128)(2,1)}, u32[]{:S(2)}, u32[]{:S(2)}) collective-permute-start(bf16[8,16,512]{2,1,0:T(8,128)(2,1)S(1)} %pad_maximum_fusion.2.refs_28_), channel_id=1, source_target_pairs={{0,128},{8,136},{16,144},{24,152},{32,160},{40,168},{48,176},{56,1... | collective-permute-start | bytes 393224 | tf_op jit(solution)/shard_map/ppermute | solution.py:200
  158.0 3.5 %collective-permute-start.3 = (bf16[8,16,512]{2,1,0:T(8,128)(2,1)S(1)}, bf16[8,16,512]{2,1,0:T(8,128)(2,1)}, u32[]{:S(2)}, u32[]{:S(2)}) collective-permute-start(bf16[8,16,512]{2,1,0:T(8,128)(2,1)S(1)} %pad_maximum_fusion.2.refs_28_), channel_id=1, source_target_pairs={{0,8},{8,0},{16,24},{24,16},{32,40},{40,32},{48,56},{56,48},{64,72... | collective-permute-start | bytes 393224 | tf_op jit(solution)/shard_map/ppermute | solution.py:200
  162.3 2.7 %collective-permute-done.3.refs_29_ = bf16[8,16,512]{2,1,0:T(8,128)(2,1)} collective-permute-done((bf16[8,16,512]{2,1,0:T(8,128)(2,1)S(1)}, bf16[8,16,512]{2,1,0:T(8,128)(2,1)}, u32[]{:S(2)}, u32[]{:S(2)}) %collective-permute-start.3) | collective-permute-done | bytes 131104 | tf_op jit(solution)/shard_map/ppermute | solution.py:200
  165.0 4.1 %collective-permute-start.10 = (bf16[2,16,1024]{2,1,0:T(8,128)(2,1)S(1)}, bf16[2,16,1024]{2,1,0:T(8,128)(2,1)S(1)}, u32[]{:S(2)}, u32[]{:S(2)}) collective-permute-start(bf16[2,16,1024]{2,1,0:T(8,128)(2,1)S(1)} %slice.41), channel_id=1, source_target_pairs={{0,8},{8,16},{16,24},{24,32},{32,40},{40,48},{48,56},{56,64},{64,7... | collective-permute-start | bytes 196616 | tf_op jit(solution)/shard_map/ppermute | solution.py:20
  169.2 4.1 %collective-permute-done.10 = bf16[2,16,1024]{2,1,0:T(8,128)(2,1)S(1)} collective-permute-done((bf16[2,16,1024]{2,1,0:T(8,128)(2,1)S(1)}, bf16[2,16,1024]{2,1,0:T(8,128)(2,1)S(1)}, u32[]{:S(2)}, u32[]{:S(2)}) %collective-permute-start.10) | collective-permute-done | bytes 65568 | tf_op jit(solution)/shard_map/ppermute | solution.py:20
  173.4 3.4 %collective-permute-start.11 = (bf16[34,16,512]{2,1,0:T(8,128)(2,1)S(1)}, bf16[34,16,512]{2,1,0:T(8,128)(2,1)S(1)}, u32[]{:S(2)}, u32[]{:S(2)}) collective-permute-start(bf16[34,16,512]{2,1,0:T(8,128)(2,1)S(1)} %get-tuple-element.43), channel_id=1, source_target_pairs={{0,2},{1,3},{2,4},{3,5},{4,6},{5,7},{6,0},{7,1},{8,10},{9,11},{10,... | collective-permute-start | bytes 1671176 | tf_op jit(solution)/shard_map/ppermute | solution.py:219
  176.8 3.7 %collective-permute-start.13 = (bf16[34,16,512]{2,1,0:T(8,128)(2,1)S(1)}, bf16[34,16,512]{2,1,0:T(8,128)(2,1)S(1)}, u32[]{:S(2)}, u32[]{:S(2)}) collective-permute-start(bf16[34,16,512]{2,1,0:T(8,128)(2,1)S(1)} %get-tuple-element.42), channel_id=1, source_target_pairs={{0,6},{1,7},{2,0},{3,1},{4,2},{5,3},{6,4},{7,5},{8,14},{9,15},{10,... | collective-permute-start | bytes 1671176 | tf_op jit(solution)/shard_map/ppermute | solution.py:219
  180.6 1.9 collective-permute-start.15
  182.6 3.5 %collective-permute-done.11 = bf16[34,16,512]{2,1,0:T(8,128)(2,1)S(1)} collective-permute-done((bf16[34,16,512]{2,1,0:T(8,128)(2,1)S(1)}, bf16[34,16,512]{2,1,0:T(8,128)(2,1)S(1)}, u32[]{:S(2)}, u32[]{:S(2)}) %collective-permute-start.11) | collective-permute-done | bytes 557088 | tf_op jit(solution)/shard_map/ppermute | solution.py:219
  186.3 2.2 collective-permute-start.12
  188.8 4.9 %collective-permute-start.14 = (bf16[68,16,512]{2,1,0:T(8,128)(2,1)S(1)}, bf16[68,16,512]{2,1,0:T(8,128)(2,1)S(1)}, u32[]{:S(2)}, u32[]{:S(2)}) collective-permute-start(bf16[68,16,512]{2,1,0:T(8,128)(2,1)S(1)} %pad_maximum_fusion.1), channel_id=1, source_target_pairs={{0,6},{1,7},{2,0},{3,1},{4,2},{5,3},{6,4},{7,5},{8,14},{9,15},{10,... | collective-permute-start | bytes 3342344 | tf_op jit(solution)/shard_map/ppermute | solution.py:219
  193.6 1.9 collective-permute-start.17
  195.6 2.4 %collective-permute-start.16 = (bf16[34,16,512]{2,1,0:T(8,128)(2,1)S(1)}, bf16[34,16,512]{2,1,0:T(8,128)(2,1)S(1)}, u32[]{:S(2)}, u32[]{:S(2)}) collective-permute-start(bf16[34,16,512]{2,1,0:T(8,128)(2,1)S(1)} %collective-permute-done.11), channel_id=1, source_target_pairs={{0,1},{1,0},{2,3},{3,2},{4,5},{5,4},{6,7},{7,6},{8,9},{9,8},{10,11... | collective-permute-start | bytes 1671176 | tf_op jit(solution)/shard_map/ppermute | solution.py:224
  199.6 13.4 %collective-permute-done.12 = bf16[68,16,512]{2,1,0:T(8,128)(2,1)S(1)} collective-permute-done((bf16[68,16,512]{2,1,0:T(8,128)(2,1)S(1)}, bf16[68,16,512]{2,1,0:T(8,128)(2,1)S(1)}, u32[]{:S(2)}, u32[]{:S(2)}) %collective-permute-start.12) | collective-permute-done | bytes 1114144 | tf_op jit(solution)/shard_map/ppermute | solution.py:219
  214.4 1.9 collective-permute-start.18
  216.3 2.4 %collective-permute-start.19 = (bf16[68,16,512]{2,1,0:T(8,128)(2,1)S(1)}, bf16[68,16,512]{2,1,0:T(8,128)(2,1)}, u32[]{:S(2)}, u32[]{:S(2)}) collective-permute-start(bf16[68,16,512]{2,1,0:T(8,128)(2,1)S(1)} %collective-permute-done.14), channel_id=1, source_target_pairs={{0,1},{1,0},{2,3},{3,2},{4,5},{5,4},{6,7},{7,6},{8,9},{9,8},{10,11... | collective-permute-start | bytes 3342344 | tf_op jit(solution)/shard_map/ppermute | solution.py:224
  219.4 1.8 collective-permute-done.19
  221.2 13.3 %blocks.1 = (bf16[1024,256]{1,0:T(8,128)(2,1)}, bf16[1024,256]{1,0:T(8,128)(2,1)}) custom-call(s32[2]{0:T(128)} %pad_add_fusion.place_ref, bf16[1024,256]{1,0:T(8,128)(2,1)} %next_query_ref.1, bf16[1024,256]{1,0:T(8,128)(2,1)} %next_query_ref.1, bf16[1024,256]{1,0:T(8,128)(2,1)} %next_grad_ref.1, bf16[1024,256]{1,0:T(8,128)(2,1)} %next_grad_ref.1, ...), custom_call_target="tpu_custom_call" | custom-call | flops 5133828096 | bytes 10485760 | tf_op jit(solution)/shard_map/blocks/pallas_call | solution.py:143
  (68 shorter events, 11.4 us)
Async XLA Ops:
  3.2 25.1 %collective-permute-start = (bf16[1,16,512]{2,1,0:T(8,128)(2,1)S(1)}, bf16[1,16,512]{2,1,0:T(8,128)(2,1)S(1)}, u32[]{:S(2)}, u32[]{:S(2)}) collective-permute-start(bf16[1,16,512]{2,1,0:T(8,128)(2,1)S(1)} %maximum_bitcast_fusion), channel_id=1, source_target_pairs={{0,64},{8,72},{16,80},{24,88},{32,96},{40,104},{48,112},{56,120},{... | collective-permute-start | bytes 49160 | tf_op jit(solution)/shard_map/ppermute | solution.py:200
  19.6 21.2 %all-to-all-start = ((s32[64,1,1]{2,1,0:T(1,128)}), s32[64,1,1]{2,1,0:T(1,128)S(1)}, u32[]{:S(2)}, u32[]{:S(2)}) async-start(s32[64,1,1]{2,1,0:T(1,128)} %copy.16), calls=%async_computation | async-start | bytes 65536 | tf_op jit(solution)/shard_map/all_to_all | solution.py:192
  28.3 13.7 %collective-permute-start.1 = (bf16[2,16,512]{2,1,0:T(8,128)(2,1)S(1)}, bf16[2,16,512]{2,1,0:T(8,128)(2,1)S(1)}, u32[]{:S(2)}, u32[]{:S(2)}) collective-permute-start(bf16[2,16,512]{2,1,0:T(8,128)(2,1)S(1)} %pad_maximum_fusion.4), channel_id=1, source_target_pairs={{0,32},{8,40},{16,48},{24,56},{32,0},{40,8},{48,16},{56,24},{64,96... | collective-permute-start | bytes 98312 | tf_op jit(solution)/shard_map/ppermute | solution.py:200
  42.0 7.8 %collective-permute-start.2 = (bf16[4,16,512]{2,1,0:T(8,128)(2,1)S(1)}, bf16[4,16,512]{2,1,0:T(8,128)(2,1)S(1)}, u32[]{:S(2)}, u32[]{:S(2)}) collective-permute-start(bf16[4,16,512]{2,1,0:T(8,128)(2,1)S(1)} %pad_maximum_fusion.3), channel_id=1, source_target_pairs={{0,16},{8,24},{16,0},{24,8},{32,48},{40,56},{48,32},{56,40},{64,80... | collective-permute-start | bytes 196616 | tf_op jit(solution)/shard_map/ppermute | solution.py:200
  49.8 107.5 %copy-start.9 = (bf16[8,16,512]{2,1,0:T(8,128)(2,1)}, bf16[8,16,512]{2,1,0:T(8,128)(2,1)S(1)}, u32[]{:S(2)}) copy-start(bf16[8,16,512]{2,1,0:T(8,128)(2,1)S(1)} %pad_maximum_fusion.2.refs_28_) | copy-start | bytes 393220
  49.8 111.8 %all-to-all-start.1 = ((bf16[64,16,1024]{2,1,0:T(8,128)(2,1)}), bf16[64,16,1024]{2,1,0:T(8,128)(2,1)S(1)}, u32[]{:S(2)}, u32[]{:S(2)}) async-start(bf16[64,16,1024]{2,1,0:T(8,128)(2,1)} %gather_fusion), calls=%async_computation.1 | async-start | bytes 4194304 | tf_op jit(solution)/shard_map/all_to_all | solution.py:212
  61.7 92.3 %collective-permute-start.9 = (bf16[8,16,512]{2,1,0:T(8,128)(2,1)S(1)}, bf16[8,16,512]{2,1,0:T(8,128)(2,1)S(1)}, u32[]{:S(2)}, u32[]{:S(2)}) collective-permute-start(bf16[8,16,512]{2,1,0:T(8,128)(2,1)S(1)} %pad_maximum_fusion.2.refs_28_), channel_id=1, source_target_pairs={{0,392},{8,384},{16,408},{24,400},{32,424},{40,416},{48,440},{56,4... | collective-permute-start | bytes 393224 | tf_op jit(solution)/shard_map/ppermute | solution.py:200
  65.3 92.1 %collective-permute-start.8 = (bf16[8,16,512]{2,1,0:T(8,128)(2,1)S(1)}, bf16[8,16,512]{2,1,0:T(8,128)(2,1)S(1)}, u32[]{:S(2)}, u32[]{:S(2)}) collective-permute-start(bf16[8,16,512]{2,1,0:T(8,128)(2,1)S(1)} %pad_maximum_fusion.2.refs_28_), channel_id=1, source_target_pairs={{0,384},{8,392},{16,400},{24,408},{32,416},{40,424},{48,432},{56,4... | collective-permute-start | bytes 393224 | tf_op jit(solution)/shard_map/ppermute | solution.py:200
  67.6 94.6 %collective-permute-start.7 = (bf16[8,16,512]{2,1,0:T(8,128)(2,1)S(1)}, bf16[8,16,512]{2,1,0:T(8,128)(2,1)}, u32[]{:S(2)}, u32[]{:S(2)}) collective-permute-start(bf16[8,16,512]{2,1,0:T(8,128)(2,1)S(1)} %pad_maximum_fusion.2.refs_28_), channel_id=1, source_target_pairs={{0,264},{8,256},{16,280},{24,272},{32,296},{40,288},{48,312},{56,3... | collective-permute-start | bytes 393224 | tf_op jit(solution)/shard_map/ppermute | solution.py:200
  73.0 89.2 %collective-permute-start.6 = (bf16[8,16,512]{2,1,0:T(8,128)(2,1)S(1)}, bf16[8,16,512]{2,1,0:T(8,128)(2,1)}, u32[]{:S(2)}, u32[]{:S(2)}) collective-permute-start(bf16[8,16,512]{2,1,0:T(8,128)(2,1)S(1)} %pad_maximum_fusion.2.refs_28_), channel_id=1, source_target_pairs={{0,256},{8,264},{16,272},{24,280},{32,288},{40,296},{48,304},{56,3... | collective-permute-start | bytes 393224 | tf_op jit(solution)/shard_map/ppermute | solution.py:200
  75.0 87.2 %collective-permute-start.5 = (bf16[8,16,512]{2,1,0:T(8,128)(2,1)S(1)}, bf16[8,16,512]{2,1,0:T(8,128)(2,1)}, u32[]{:S(2)}, u32[]{:S(2)}) collective-permute-start(bf16[8,16,512]{2,1,0:T(8,128)(2,1)S(1)} %pad_maximum_fusion.2.refs_28_), channel_id=1, source_target_pairs={{0,136},{8,128},{16,152},{24,144},{32,168},{40,160},{48,184},{56,1... | collective-permute-start | bytes 393224 | tf_op jit(solution)/shard_map/ppermute | solution.py:200
  154.0 11.0 %copy-start.10 = (bf16[8,16,512]{2,1,0:T(8,128)(2,1)}, bf16[8,16,512]{2,1,0:T(8,128)(2,1)S(1)}, u32[]{:S(2)}) copy-start(bf16[8,16,512]{2,1,0:T(8,128)(2,1)S(1)} %collective-permute-done.9.refs_35_) | copy-start | bytes 393220
  154.0 8.3 %collective-permute-start.4 = (bf16[8,16,512]{2,1,0:T(8,128)(2,1)S(1)}, bf16[8,16,512]{2,1,0:T(8,128)(2,1)}, u32[]{:S(2)}, u32[]{:S(2)}) collective-permute-start(bf16[8,16,512]{2,1,0:T(8,128)(2,1)S(1)} %pad_maximum_fusion.2.refs_28_), channel_id=1, source_target_pairs={{0,128},{8,136},{16,144},{24,152},{32,160},{40,168},{48,176},{56,1... | collective-permute-start | bytes 393224 | tf_op jit(solution)/shard_map/ppermute | solution.py:200
  158.0 7.0 %collective-permute-start.3 = (bf16[8,16,512]{2,1,0:T(8,128)(2,1)S(1)}, bf16[8,16,512]{2,1,0:T(8,128)(2,1)}, u32[]{:S(2)}, u32[]{:S(2)}) collective-permute-start(bf16[8,16,512]{2,1,0:T(8,128)(2,1)S(1)} %pad_maximum_fusion.2.refs_28_), channel_id=1, source_target_pairs={{0,8},{8,0},{16,24},{24,16},{32,40},{40,32},{48,56},{56,48},{64,72... | collective-permute-start | bytes 393224 | tf_op jit(solution)/shard_map/ppermute | solution.py:200
  165.0 8.3 %collective-permute-start.10 = (bf16[2,16,1024]{2,1,0:T(8,128)(2,1)S(1)}, bf16[2,16,1024]{2,1,0:T(8,128)(2,1)S(1)}, u32[]{:S(2)}, u32[]{:S(2)}) collective-permute-start(bf16[2,16,1024]{2,1,0:T(8,128)(2,1)S(1)} %slice.41), channel_id=1, source_target_pairs={{0,8},{8,16},{16,24},{24,32},{32,40},{40,48},{48,56},{56,64},{64,7... | collective-permute-start | bytes 196616 | tf_op jit(solution)/shard_map/ppermute | solution.py:20
  173.2 7.4 %copy-start.3 = (bf16[34,16,1024]{2,1,0:T(8,128)(2,1)}, bf16[34,16,1024]{2,1,0:T(8,128)(2,1)S(1)}, u32[]{:S(2)}) copy-start(bf16[34,16,1024]{2,1,0:T(8,128)(2,1)S(1)} %constant_dynamic-update-slice_fusion) | copy-start | bytes 3342340
  173.4 12.6 %collective-permute-start.11 = (bf16[34,16,512]{2,1,0:T(8,128)(2,1)S(1)}, bf16[34,16,512]{2,1,0:T(8,128)(2,1)S(1)}, u32[]{:S(2)}, u32[]{:S(2)}) collective-permute-start(bf16[34,16,512]{2,1,0:T(8,128)(2,1)S(1)} %get-tuple-element.43), channel_id=1, source_target_pairs={{0,2},{1,3},{2,4},{3,5},{4,6},{5,7},{6,0},{7,1},{8,10},{9,11},{10,... | collective-permute-start | bytes 1671176 | tf_op jit(solution)/shard_map/ppermute | solution.py:219
  176.8 11.7 %collective-permute-start.13 = (bf16[34,16,512]{2,1,0:T(8,128)(2,1)S(1)}, bf16[34,16,512]{2,1,0:T(8,128)(2,1)S(1)}, u32[]{:S(2)}, u32[]{:S(2)}) collective-permute-start(bf16[34,16,512]{2,1,0:T(8,128)(2,1)S(1)} %get-tuple-element.42), channel_id=1, source_target_pairs={{0,6},{1,7},{2,0},{3,1},{4,2},{5,3},{6,4},{7,5},{8,14},{9,15},{10,... | collective-permute-start | bytes 1671176 | tf_op jit(solution)/shard_map/ppermute | solution.py:219
  180.6 18.9 %collective-permute-start.15 = (bf16[34,16,1024]{2,1,0:T(8,128)(2,1)S(1)}, bf16[34,16,1024]{2,1,0:T(8,128)(2,1)S(1)}, u32[]{:S(2)}, u32[]{:S(2)}) collective-permute-start(bf16[34,16,1024]{2,1,0:T(8,128)(2,1)S(1)} %constant_dynamic-update-slice_fusion), channel_id=1, source_target_pairs={{0,1},{1,0},{2,3},{3,2},{4,5},{5,4},{6,7},{7,6},{8,9},{9,8},{10,11... | collective-permute-start | bytes 3342344 | tf_op jit(solution)/shard_map/ppermute | solution.py:224
  186.0 9.5 %copy-start.4 = (bf16[34,16,512]{2,1,0:T(8,128)(2,1)}, bf16[34,16,512]{2,1,0:T(8,128)(2,1)S(1)}, u32[]{:S(2)}) copy-start(bf16[34,16,512]{2,1,0:T(8,128)(2,1)S(1)} %collective-permute-done.11) | copy-start | bytes 1671172
  186.3 26.6 %collective-permute-start.12 = (bf16[68,16,512]{2,1,0:T(8,128)(2,1)S(1)}, bf16[68,16,512]{2,1,0:T(8,128)(2,1)S(1)}, u32[]{:S(2)}, u32[]{:S(2)}) collective-permute-start(bf16[68,16,512]{2,1,0:T(8,128)(2,1)S(1)} %pad_maximum_fusion), channel_id=1, source_target_pairs={{0,2},{1,3},{2,4},{3,5},{4,6},{5,7},{6,0},{7,1},{8,10},{9,11},{10,... | collective-permute-start | bytes 3342344 | tf_op jit(solution)/shard_map/ppermute | solution.py:219
  188.5 5.1 %copy-start.5 = (bf16[34,16,512]{2,1,0:T(8,128)(2,1)}, bf16[34,16,512]{2,1,0:T(8,128)(2,1)S(1)}, u32[]{:S(2)}) copy-start(bf16[34,16,512]{2,1,0:T(8,128)(2,1)S(1)} %collective-permute-done.13) | copy-start | bytes 1671172
  188.8 25.6 %collective-permute-start.14 = (bf16[68,16,512]{2,1,0:T(8,128)(2,1)S(1)}, bf16[68,16,512]{2,1,0:T(8,128)(2,1)S(1)}, u32[]{:S(2)}, u32[]{:S(2)}) collective-permute-start(bf16[68,16,512]{2,1,0:T(8,128)(2,1)S(1)} %pad_maximum_fusion.1), channel_id=1, source_target_pairs={{0,6},{1,7},{2,0},{3,1},{4,2},{5,3},{6,4},{7,5},{8,14},{9,15},{10,... | collective-permute-start | bytes 3342344 | tf_op jit(solution)/shard_map/ppermute | solution.py:219
  193.6 4.4 %collective-permute-start.17 = (bf16[34,16,512]{2,1,0:T(8,128)(2,1)S(1)}, bf16[34,16,512]{2,1,0:T(8,128)(2,1)S(1)}, u32[]{:S(2)}, u32[]{:S(2)}) collective-permute-start(bf16[34,16,512]{2,1,0:T(8,128)(2,1)S(1)} %collective-permute-done.13), channel_id=1, source_target_pairs={{0,1},{1,0},{2,3},{3,2},{4,5},{5,4},{6,7},{7,6},{8,9},{9,8},{10,11... | collective-permute-start | bytes 1671176 | tf_op jit(solution)/shard_map/ppermute | solution.py:224
  195.6 4.0 %collective-permute-start.16 = (bf16[34,16,512]{2,1,0:T(8,128)(2,1)S(1)}, bf16[34,16,512]{2,1,0:T(8,128)(2,1)S(1)}, u32[]{:S(2)}, u32[]{:S(2)}) collective-permute-start(bf16[34,16,512]{2,1,0:T(8,128)(2,1)S(1)} %collective-permute-done.11), channel_id=1, source_target_pairs={{0,1},{1,0},{2,3},{3,2},{4,5},{5,4},{6,7},{7,6},{8,9},{9,8},{10,11... | collective-permute-start | bytes 1671176 | tf_op jit(solution)/shard_map/ppermute | solution.py:224
  198.0 18.3 %copy-start.7 = (bf16[34,16,512]{2,1,0:T(8,128)(2,1)}, bf16[34,16,512]{2,1,0:T(8,128)(2,1)S(1)}, u32[]{:S(2)}) copy-start(bf16[34,16,512]{2,1,0:T(8,128)(2,1)S(1)} %collective-permute-done.17) | copy-start | bytes 1671172
  199.6 16.8 %copy-start.8 = (bf16[34,16,512]{2,1,0:T(8,128)(2,1)}, bf16[34,16,512]{2,1,0:T(8,128)(2,1)S(1)}, u32[]{:S(2)}) copy-start(bf16[34,16,512]{2,1,0:T(8,128)(2,1)S(1)} %collective-permute-done.16) | copy-start | bytes 1671172
  199.6 14.8 %copy-start.6 = (bf16[34,16,1024]{2,1,0:T(8,128)(2,1)}, bf16[34,16,1024]{2,1,0:T(8,128)(2,1)S(1)}, u32[]{:S(2)}) copy-start(bf16[34,16,1024]{2,1,0:T(8,128)(2,1)S(1)} %collective-permute-done.15) | copy-start | bytes 3342340
  212.9 8.3 %copy-start = (bf16[68,16,512]{2,1,0:T(8,128)(2,1)}, bf16[68,16,512]{2,1,0:T(8,128)(2,1)S(1)}, u32[]{:S(2)}) copy-start(bf16[68,16,512]{2,1,0:T(8,128)(2,1)S(1)} %collective-permute-done.12) | copy-start | bytes 3342340
  214.4 6.8 %copy-start.1 = (bf16[68,16,512]{2,1,0:T(8,128)(2,1)}, bf16[68,16,512]{2,1,0:T(8,128)(2,1)S(1)}, u32[]{:S(2)}) copy-start(bf16[68,16,512]{2,1,0:T(8,128)(2,1)S(1)} %collective-permute-done.14) | copy-start | bytes 3342340
  214.4 5.0 %collective-permute-start.18 = (bf16[68,16,512]{2,1,0:T(8,128)(2,1)S(1)}, bf16[68,16,512]{2,1,0:T(8,128)(2,1)S(1)}, u32[]{:S(2)}, u32[]{:S(2)}) collective-permute-start(bf16[68,16,512]{2,1,0:T(8,128)(2,1)S(1)} %collective-permute-done.12), channel_id=1, source_target_pairs={{0,1},{1,0},{2,3},{3,2},{4,5},{5,4},{6,7},{7,6},{8,9},{9,8},{10,11... | collective-permute-start | bytes 3342344 | tf_op jit(solution)/shard_map/ppermute | solution.py:224
  216.3 4.9 %collective-permute-start.19 = (bf16[68,16,512]{2,1,0:T(8,128)(2,1)S(1)}, bf16[68,16,512]{2,1,0:T(8,128)(2,1)}, u32[]{:S(2)}, u32[]{:S(2)}) collective-permute-start(bf16[68,16,512]{2,1,0:T(8,128)(2,1)S(1)} %collective-permute-done.14), channel_id=1, source_target_pairs={{0,1},{1,0},{2,3},{3,2},{4,5},{5,4},{6,7},{7,6},{8,9},{9,8},{10,11... | collective-permute-start | bytes 3342344 | tf_op jit(solution)/shard_map/ppermute | solution.py:224
  (2 other events, 2.5 us)

commit v7 on v5

--- a/solution.py
+++ b/solution.py
@@ -224,25 +224,40 @@
 
     low, high = asked[:, :, :half], asked[:, :, half:]
     before_low, after_high = along_x(low, 1), along_x(high, -1)
+    swapped, before_low, after_high = lax.optimization_barrier(
+        (other_core(asked), before_low, after_high)
+    )
     up, down = along_x(together(before_low, high), 1), along_x(together(after_high, low), -1)
     held = []
     for step in range(1, y_count):
         pairs = [(i, (i + step * Z) % seq_count) for i in range(seq_count)]
         held.append(lax.ppermute(weight, "seq", pairs))
-    near = [asked, before_low, after_high]
-    swapped = [other_core(a) for a in near]
-    up, down, swapped, held = lax.optimization_barrier((up, down, swapped, held))
+    swapped_half = other_core(together(before_low, after_high))
+    up, down, swapped_half, held = lax.optimization_barrier((up, down, swapped_half, held))
     held = [weight, *held]
     blocks = queries.shape[0] // BLOCK
-    pieces = []
-    for arrays in (near + [up, down], swapped + [other_core(up), other_core(down)]):
-        arrays = [a.reshape(-1, 2 * part_tokens, a.shape[-1]) for a in arrays]
-        asked, before_low, after_high, up, down = arrays
-        pieces += [(asked, 0, blocks)]
-        pieces += [(before_low, 0, blocks), (up, blocks, 2 * blocks + 1)]
-        pieces += [(down, blocks, 2 * blocks + 1), (after_high, 0, blocks)]
-        pieces += [(up, 0, 2 * blocks), (down, 0, 2 * blocks)]
-
+    alone, first_of, second_of = (0, blocks), (0, 2 * blocks), (blocks, 2 * blocks + 1)
+
+    def placed(array, where):
+        return (array.reshape(-1, 2 * part_tokens, array.shape[-1]), *where)
+
+    swapped_up, swapped_down = other_core(up), other_core(down)
+    pieces = [
+        placed(asked, alone),
+        placed(before_low, alone),
+        placed(up, second_of),
+        placed(down, second_of),
+        placed(after_high, alone),
+        placed(up, first_of),
+        placed(down, first_of),
+        placed(swapped, alone),
+        placed(swapped_half, first_of),
+        placed(swapped_up, second_of),
+        placed(swapped_down, second_of),
+        placed(swapped_half, second_of),
+        placed(swapped_up, first_of),
+        placed(swapped_down, first_of),
+    ]
     my_seq = lax.axis_index("seq")
     place = jnp.stack([my_seq // Z, my_seq % Z]).astype(jnp.int32)
     return attention(place, queries, context_grad, pieces, held)

time: 233 us -> 246 us (1.056)
  waiting for transfers between devices: 118 us -> 133 us
  starting transfers between devices: 87 us -> 83.6 us
    ppermute x4, waiting for transfers between devices: 4.26 us -> 15.8 us  [along_x(): lax.ppermute(value, 'head', [(i, (i + 2 * steps) % head_devices) for i in...]
    ppermute x3, waiting for transfers between devices: 12.8 us -> 18.8 us  [body(): held.append(lax.ppermute(weight, 'seq', pairs))]
    ppermute x5 -> x4, starting transfers between devices: 10.1 us -> 8.16 us  [other_core(): lax.ppermute(value, 'head', [(i, i ^ 1) for i in range(head_devices)])]
  transfers between devices with their start and end apart: 20 -> 19, of which waited for: 10 -> 11; matrix products, arithmetic and copies ran while one was open for 2% -> 2% of each run, Pallas kernels for 0% -> 0%
where the time goes in v7:
time: 246 us; the launch traced here: 243 us
  waiting for transfers between devices  133 us (54%)
  starting transfers between devices  83.6 us (34%)
  Pallas kernels  13.2 us (5%)
  local copies, waits for them, and re-layouts  6.86 us (3%)
  other arithmetic  4.83 us (2%)
    ppermute x5, waiting for transfers between devices, from_z(): return lax.ppermute(value, 'seq', [(i, i ^ step) for i in range(seq_count)])  85.2 us
    ppermute x5, starting transfers between devices, from_z(): return lax.ppermute(value, 'seq', [(i, i ^ step) for i in range(seq_count)])  33.1 us
    ppermute x3, waiting for transfers between devices, body(): held.append(lax.ppermute(weight, 'seq', pairs))  18.8 us
    ppermute x4, waiting for transfers between devices, along_x(): lax.ppermute(value, 'head', [(i, (i + 2 * steps) % head_devices) for i in...  15.8 us
    pallas_call x1, Pallas kernels, attention(): pl.pallas_call(functools.partial(main_kernel, len(pieces)), grid=(blocks...  13.2 us
    ppermute x4, starting transfers between devices, along_x(): lax.ppermute(value, 'head', [(i, (i + 2 * steps) % head_devices) for i in...  12.4 us
    all_to_all x1, starting transfers between devices, body(): lax.all_to_all(outgoing, 'seq', split_axis=0, concat_axis=0, tiled=True)  12.2 us
    all_to_all x1, starting transfers between devices, body(): lax.all_to_all(asked_rows.reshape(seq_count, 1), 'seq', split_axis=0, con...  8.64 us
  transfers between devices with their start and end apart: 19, of which 11 were waited for; matrix products, arithmetic and copies ran while one was open for 2% of the time, Pallas kernels for 0%

profile of v7, /device:TPU:24, one launch (start us, length us, event | category | flops | bytes accessed | tf_op | source)
XLA Modules:
  0.0 242.6 jit_solution(10350143222711363034)
XLA Ops:
  3.2 15.7 %collective-permute-start = (bf16[1,16,512]{2,1,0:T(8,128)(2,1)S(1)}, bf16[1,16,512]{2,1,0:T(8,128)(2,1)S(1)}, u32[]{:S(2)}, u32[]{:S(2)}) collective-permute-start(bf16[1,16,512]{2,1,0:T(8,128)(2,1)S(1)} %maximum_bitcast_fusion), channel_id=1, source_target_pairs={{0,64},{8,72},{16,80},{24,88},{32,96},{40,104},{48,112},{56,120},{... | collective-permute-start | bytes 49160 | tf_op jit(solution)/shard_map/ppermute | solution.py:196
  19.6 8.6 %all-to-all-start = ((s32[64,1,1]{2,1,0:T(1,128)}), s32[64,1,1]{2,1,0:T(1,128)S(1)}, u32[]{:S(2)}, u32[]{:S(2)}) async-start(s32[64,1,1]{2,1,0:T(1,128)} %copy.16), calls=%async_computation | async-start | bytes 65536 | tf_op jit(solution)/shard_map/all_to_all | solution.py:191
  28.3 7.3 %collective-permute-start.1 = (bf16[2,16,512]{2,1,0:T(8,128)(2,1)S(1)}, bf16[2,16,512]{2,1,0:T(8,128)(2,1)S(1)}, u32[]{:S(2)}, u32[]{:S(2)}) collective-permute-start(bf16[2,16,512]{2,1,0:T(8,128)(2,1)S(1)} %pad_maximum_fusion.7), channel_id=1, source_target_pairs={{0,32},{8,40},{16,48},{24,56},{32,0},{40,8},{48,16},{56,24},{64,96... | collective-permute-start | bytes 98312 | tf_op jit(solution)/shard_map/ppermute | solution.py:196
  35.6 1.1 dynamic-slice_bitcast_fusion
  36.7 4.1 %all-to-all-done = s32[64,1,1]{2,1,0:T(1,128)S(1)} async-done(((s32[64,1,1]{2,1,0:T(1,128)}), s32[64,1,1]{2,1,0:T(1,128)S(1)}, u32[]{:S(2)}, u32[]{:S(2)}) %all-to-all-start) | async-done | bytes 288 | tf_op jit(solution)/shard_map/all_to_all | solution.py:191
  40.8 1.2 reduce
  42.1 2.0 gather_fusion
  44.1 12.2 %all-to-all-start.1 = ((bf16[64,16,1024]{2,1,0:T(8,128)(2,1)}), bf16[64,16,1024]{2,1,0:T(8,128)(2,1)S(1)}, u32[]{:S(2)}, u32[]{:S(2)}) async-start(bf16[64,16,1024]{2,1,0:T(8,128)(2,1)} %gather_fusion), calls=%async_computation.1 | async-start | bytes 4194304 | tf_op jit(solution)/shard_map/all_to_all | solution.py:207
  56.3 5.2 %collective-permute-start.4 = (bf16[4,16,512]{2,1,0:T(8,128)(2,1)S(1)}, bf16[4,16,512]{2,1,0:T(8,128)(2,1)S(1)}, u32[]{:S(2)}, u32[]{:S(2)}) collective-permute-start(bf16[4,16,512]{2,1,0:T(8,128)(2,1)S(1)} %pad_maximum_fusion.6), channel_id=1, source_target_pairs={{0,24},{8,16},{16,8},{24,0},{32,56},{40,48},{48,40},{56,32},{64,88... | collective-permute-start | bytes 196616 | tf_op jit(solution)/shard_map/ppermute | solution.py:196
  61.5 1.9 collective-permute-start.3
  63.4 3.0 %collective-permute-start.2 = (bf16[4,16,512]{2,1,0:T(8,128)(2,1)S(1)}, bf16[4,16,512]{2,1,0:T(8,128)(2,1)S(1)}, u32[]{:S(2)}, u32[]{:S(2)}) collective-permute-start(bf16[4,16,512]{2,1,0:T(8,128)(2,1)S(1)} %pad_maximum_fusion.6), channel_id=1, source_target_pairs={{0,8},{8,0},{16,24},{24,16},{32,40},{40,32},{48,56},{56,48},{64,72... | collective-permute-start | bytes 196616 | tf_op jit(solution)/shard_map/ppermute | solution.py:196
  66.4 81.6 %collective-permute-done.4 = bf16[4,16,512]{2,1,0:T(8,128)(2,1)S(1)} collective-permute-done((bf16[4,16,512]{2,1,0:T(8,128)(2,1)S(1)}, bf16[4,16,512]{2,1,0:T(8,128)(2,1)S(1)}, u32[]{:S(2)}, u32[]{:S(2)}) %collective-permute-start.4) | collective-permute-done | bytes 65568 | tf_op jit(solution)/shard_map/ppermute | solution.py:196
  148.0 3.6 %collective-permute-done.3 = bf16[4,16,512]{2,1,0:T(8,128)(2,1)S(1)} collective-permute-done((bf16[4,16,512]{2,1,0:T(8,128)(2,1)S(1)}, bf16[4,16,512]{2,1,0:T(8,128)(2,1)S(1)}, u32[]{:S(2)}, u32[]{:S(2)}) %collective-permute-start.3) | collective-permute-done | bytes 65568 | tf_op jit(solution)/shard_map/ppermute | solution.py:196
  153.2 1.9 collective-permute-start.5
  155.2 7.1 %collective-permute-done.5 = bf16[2,16,1024]{2,1,0:T(8,128)(2,1)S(1)} collective-permute-done((bf16[2,16,1024]{2,1,0:T(8,128)(2,1)S(1)}, bf16[2,16,1024]{2,1,0:T(8,128)(2,1)S(1)}, u32[]{:S(2)}, u32[]{:S(2)}) %collective-permute-start.5) | collective-permute-done | bytes 65568 | tf_op jit(solution)/shard_map/ppermute | solution.py:20
  162.3 1.9 collective-permute-start.6
  164.4 4.7 %collective-permute-start.8 = (bf16[34,16,512]{2,1,0:T(8,128)(2,1)S(1)}, bf16[34,16,512]{2,1,0:T(8,128)(2,1)S(1)}, u32[]{:S(2)}, u32[]{:S(2)}) collective-permute-start(bf16[34,16,512]{2,1,0:T(8,128)(2,1)S(1)} %get-tuple-element.36), channel_id=1, source_target_pairs={{0,6},{1,7},{2,0},{3,1},{4,2},{5,3},{6,4},{7,5},{8,14},{9,15},{10,... | collective-permute-start | bytes 1671176 | tf_op jit(solution)/shard_map/ppermute | solution.py:214
  169.1 1.9 collective-permute-start.7
  171.1 10.5 %collective-permute-done.8 = bf16[34,16,512]{2,1,0:T(8,128)(2,1)S(1)} collective-permute-done((bf16[34,16,512]{2,1,0:T(8,128)(2,1)S(1)}, bf16[34,16,512]{2,1,0:T(8,128)(2,1)S(1)}, u32[]{:S(2)}, u32[]{:S(2)}) %collective-permute-start.8) | collective-permute-done | bytes 557088 | tf_op jit(solution)/shard_map/ppermute | solution.py:214
  181.6 5.3 %collective-permute-done.7 = bf16[34,16,512]{2,1,0:T(8,128)(2,1)S(1)} collective-permute-done((bf16[34,16,512]{2,1,0:T(8,128)(2,1)S(1)}, bf16[34,16,512]{2,1,0:T(8,128)(2,1)S(1)}, u32[]{:S(2)}, u32[]{:S(2)}) %collective-permute-start.7) | collective-permute-done | bytes 557088 | tf_op jit(solution)/shard_map/ppermute | solution.py:214
  188.6 1.9 collective-permute-start.11
  190.6 1.9 collective-permute-start.10
  192.5 3.9 %collective-permute-start.9 = (bf16[68,16,512]{2,1,0:T(8,128)(2,1)S(1)}, bf16[68,16,512]{2,1,0:T(8,128)(2,1)S(1)}, u32[]{:S(2)}, u32[]{:S(2)}) collective-permute-start(bf16[68,16,512]{2,1,0:T(8,128)(2,1)S(1)} %get-tuple-element.42), channel_id=1, source_target_pairs={{0,2},{1,3},{2,4},{3,5},{4,6},{5,7},{6,0},{7,1},{8,10},{9,11},{10,... | collective-permute-start | bytes 3342344 | tf_op jit(solution)/shard_map/ppermute | solution.py:214
  196.4 2.7 %collective-permute-start.14 = (bf16[16,16,512]{2,1,0:T(8,128)(2,1)S(1)}, bf16[16,16,512]{2,1,0:T(8,128)(2,1)S(1)}, u32[]{:S(2)}, u32[]{:S(2)}) collective-permute-start(bf16[16,16,512]{2,1,0:T(8,128)(2,1)S(1)} %copy-done.7), channel_id=1, source_target_pairs={{0,384},{8,392},{16,400},{24,408},{32,416},{40,424},{48,432},{56,4... | collective-permute-start | bytes 786440 | tf_op jit(solution)/shard_map/ppermute | solution.py:234
  199.1 2.6 %collective-permute-start.13 = (bf16[16,16,512]{2,1,0:T(8,128)(2,1)S(1)}, bf16[16,16,512]{2,1,0:T(8,128)(2,1)S(1)}, u32[]{:S(2)}, u32[]{:S(2)}) collective-permute-start(bf16[16,16,512]{2,1,0:T(8,128)(2,1)S(1)} %copy-done.7), channel_id=1, source_target_pairs={{0,256},{8,264},{16,272},{24,280},{32,288},{40,296},{48,304},{56,3... | collective-permute-start | bytes 786440 | tf_op jit(solution)/shard_map/ppermute | solution.py:234
  201.7 11.6 %collective-permute-done.14.refs_31_ = bf16[16,16,512]{2,1,0:T(8,128)(2,1)S(1)} collective-permute-done((bf16[16,16,512]{2,1,0:T(8,128)(2,1)S(1)}, bf16[16,16,512]{2,1,0:T(8,128)(2,1)S(1)}, u32[]{:S(2)}, u32[]{:S(2)}) %collective-permute-start.14) | collective-permute-done | bytes 262176 | tf_op jit(solution)/shard_map/ppermute | solution.py:234
  213.3 1.9 collective-permute-start.12
  215.2 7.2 %collective-permute-done.12.refs_29_ = bf16[16,16,512]{2,1,0:T(8,128)(2,1)S(1)} collective-permute-done((bf16[16,16,512]{2,1,0:T(8,128)(2,1)S(1)}, bf16[16,16,512]{2,1,0:T(8,128)(2,1)S(1)}, u32[]{:S(2)}, u32[]{:S(2)}) %collective-permute-start.12) | collective-permute-done | bytes 262176 | tf_op jit(solution)/shard_map/ppermute | solution.py:234
  222.6 1.9 collective-permute-start.15
  224.5 2.4 collective-permute-start.16
  227.5 1.9 collective-permute-done.16
  229.4 13.2 %blocks.1 = (bf16[1024,256]{1,0:T(8,128)(2,1)}, bf16[1024,256]{1,0:T(8,128)(2,1)}) custom-call(s32[2]{0:T(128)} %pad_add_fusion.place_ref, bf16[1024,256]{1,0:T(8,128)(2,1)} %next_query_ref.1, bf16[1024,256]{1,0:T(8,128)(2,1)} %next_query_ref.1, bf16[1024,256]{1,0:T(8,128)(2,1)} %next_grad_ref.1, bf16[1024,256]{1,0:T(8,128)(2,1)} %next_grad_ref.1, ...), custom_call_target="tpu_custom_call" | custom-call | flops 5133828096 | bytes 10485760 | tf_op jit(solution)/shard_map/blocks/pallas_call | solution.py:142
  (59 shorter events, 7.5 us)
Async XLA Ops:
  3.2 25.1 %collective-permute-start = (bf16[1,16,512]{2,1,0:T(8,128)(2,1)S(1)}, bf16[1,16,512]{2,1,0:T(8,128)(2,1)S(1)}, u32[]{:S(2)}, u32[]{:S(2)}) collective-permute-start(bf16[1,16,512]{2,1,0:T(8,128)(2,1)S(1)} %maximum_bitcast_fusion), channel_id=1, source_target_pairs={{0,64},{8,72},{16,80},{24,88},{32,96},{40,104},{48,112},{56,120},{... | collective-permute-start | bytes 49160 | tf_op jit(solution)/shard_map/ppermute | solution.py:196
  19.6 21.2 %all-to-all-start = ((s32[64,1,1]{2,1,0:T(1,128)}), s32[64,1,1]{2,1,0:T(1,128)S(1)}, u32[]{:S(2)}, u32[]{:S(2)}) async-start(s32[64,1,1]{2,1,0:T(1,128)} %copy.16), calls=%async_computation | async-start | bytes 65536 | tf_op jit(solution)/shard_map/all_to_all | solution.py:191
  28.3 13.7 %collective-permute-start.1 = (bf16[2,16,512]{2,1,0:T(8,128)(2,1)S(1)}, bf16[2,16,512]{2,1,0:T(8,128)(2,1)S(1)}, u32[]{:S(2)}, u32[]{:S(2)}) collective-permute-start(bf16[2,16,512]{2,1,0:T(8,128)(2,1)S(1)} %pad_maximum_fusion.7), channel_id=1, source_target_pairs={{0,32},{8,40},{16,48},{24,56},{32,0},{40,8},{48,16},{56,24},{64,96... | collective-permute-start | bytes 98312 | tf_op jit(solution)/shard_map/ppermute | solution.py:196
  44.1 108.4 %all-to-all-start.1 = ((bf16[64,16,1024]{2,1,0:T(8,128)(2,1)}), bf16[64,16,1024]{2,1,0:T(8,128)(2,1)S(1)}, u32[]{:S(2)}, u32[]{:S(2)}) async-start(bf16[64,16,1024]{2,1,0:T(8,128)(2,1)} %gather_fusion), calls=%async_computation.1 | async-start | bytes 4194304 | tf_op jit(solution)/shard_map/all_to_all | solution.py:207
  56.3 91.7 %collective-permute-start.4 = (bf16[4,16,512]{2,1,0:T(8,128)(2,1)S(1)}, bf16[4,16,512]{2,1,0:T(8,128)(2,1)S(1)}, u32[]{:S(2)}, u32[]{:S(2)}) collective-permute-start(bf16[4,16,512]{2,1,0:T(8,128)(2,1)S(1)} %pad_maximum_fusion.6), channel_id=1, source_target_pairs={{0,24},{8,16},{16,8},{24,0},{32,56},{40,48},{48,40},{56,32},{64,88... | collective-permute-start | bytes 196616 | tf_op jit(solution)/shard_map/ppermute | solution.py:196
  61.5 90.2 %collective-permute-start.3 = (bf16[4,16,512]{2,1,0:T(8,128)(2,1)S(1)}, bf16[4,16,512]{2,1,0:T(8,128)(2,1)S(1)}, u32[]{:S(2)}, u32[]{:S(2)}) collective-permute-start(bf16[4,16,512]{2,1,0:T(8,128)(2,1)S(1)} %pad_maximum_fusion.6), channel_id=1, source_target_pairs={{0,16},{8,24},{16,0},{24,8},{32,48},{40,56},{48,32},{56,40},{64,80... | collective-permute-start | bytes 196616 | tf_op jit(solution)/shard_map/ppermute | solution.py:196
  63.4 88.2 %collective-permute-start.2 = (bf16[4,16,512]{2,1,0:T(8,128)(2,1)S(1)}, bf16[4,16,512]{2,1,0:T(8,128)(2,1)S(1)}, u32[]{:S(2)}, u32[]{:S(2)}) collective-permute-start(bf16[4,16,512]{2,1,0:T(8,128)(2,1)S(1)} %pad_maximum_fusion.6), channel_id=1, source_target_pairs={{0,8},{8,0},{16,24},{24,16},{32,40},{40,32},{48,56},{56,48},{64,72... | collective-permute-start | bytes 196616 | tf_op jit(solution)/shard_map/ppermute | solution.py:196
  153.2 9.1 %collective-permute-start.5 = (bf16[2,16,1024]{2,1,0:T(8,128)(2,1)S(1)}, bf16[2,16,1024]{2,1,0:T(8,128)(2,1)S(1)}, u32[]{:S(2)}, u32[]{:S(2)}) collective-permute-start(bf16[2,16,1024]{2,1,0:T(8,128)(2,1)S(1)} %slice.45), channel_id=1, source_target_pairs={{0,8},{8,16},{16,24},{24,32},{32,40},{40,48},{48,56},{56,64},{64,7... | collective-permute-start | bytes 196616 | tf_op jit(solution)/shard_map/ppermute | solution.py:20
  162.3 2.1 copy-start.3
  162.3 24.6 %collective-permute-start.6 = (bf16[34,16,1024]{2,1,0:T(8,128)(2,1)S(1)}, bf16[34,16,1024]{2,1,0:T(8,128)(2,1)S(1)}, u32[]{:S(2)}, u32[]{:S(2)}) collective-permute-start(bf16[34,16,1024]{2,1,0:T(8,128)(2,1)S(1)} %constant_dynamic-update-slice_fusion), channel_id=1, source_target_pairs={{0,1},{1,0},{2,3},{3,2},{4,5},{5,4},{6,7},{7,6},{8,9},{9,8},{10,11... | collective-permute-start | bytes 3342344 | tf_op jit(solution)/shard_map/ppermute | solution.py:219
  164.4 17.2 %collective-permute-start.8 = (bf16[34,16,512]{2,1,0:T(8,128)(2,1)S(1)}, bf16[34,16,512]{2,1,0:T(8,128)(2,1)S(1)}, u32[]{:S(2)}, u32[]{:S(2)}) collective-permute-start(bf16[34,16,512]{2,1,0:T(8,128)(2,1)S(1)} %get-tuple-element.36), channel_id=1, source_target_pairs={{0,6},{1,7},{2,0},{3,1},{4,2},{5,3},{6,4},{7,5},{8,14},{9,15},{10,... | collective-permute-start | bytes 1671176 | tf_op jit(solution)/shard_map/ppermute | solution.py:214
  169.1 17.9 %collective-permute-start.7 = (bf16[34,16,512]{2,1,0:T(8,128)(2,1)S(1)}, bf16[34,16,512]{2,1,0:T(8,128)(2,1)S(1)}, u32[]{:S(2)}, u32[]{:S(2)}) collective-permute-start(bf16[34,16,512]{2,1,0:T(8,128)(2,1)S(1)} %get-tuple-element.37), channel_id=1, source_target_pairs={{0,2},{1,3},{2,4},{3,5},{4,6},{5,7},{6,0},{7,1},{8,10},{9,11},{10,... | collective-permute-start | bytes 1671176 | tf_op jit(solution)/shard_map/ppermute | solution.py:214
  181.6 5.4 %copy-start.4 = (bf16[34,16,512]{2,1,0:T(8,128)(2,1)}, bf16[34,16,512]{2,1,0:T(8,128)(2,1)S(1)}, u32[]{:S(2)}) copy-start(bf16[34,16,512]{2,1,0:T(8,128)(2,1)S(1)} %collective-permute-done.8) | copy-start | bytes 1671172
  186.9 0.9 copy-start.5
  186.9 1.2 copy-start.6
  188.1 8.3 %copy-start.7 = (bf16[16,16,512]{2,1,0:T(8,128)(2,1)S(1)}, bf16[16,16,512]{2,1,0:T(8,128)(2,1)}, u32[]{:S(2)}) copy-start(bf16[16,16,512]{2,1,0:T(8,128)(2,1)} %pad_maximum_fusion.5.refs_28_) | copy-start | bytes 786436
  188.6 33.8 %collective-permute-start.11 = (bf16[68,16,512]{2,1,0:T(8,128)(2,1)S(1)}, bf16[68,16,512]{2,1,0:T(8,128)(2,1)S(1)}, u32[]{:S(2)}, u32[]{:S(2)}) collective-permute-start(bf16[68,16,512]{2,1,0:T(8,128)(2,1)S(1)} %get-tuple-element.40), channel_id=1, source_target_pairs={{0,1},{1,0},{2,3},{3,2},{4,5},{5,4},{6,7},{7,6},{8,9},{9,8},{10,11... | collective-permute-start | bytes 3342344 | tf_op jit(solution)/shard_map/ppermute | solution.py:219
  190.6 31.9 %collective-permute-start.10 = (bf16[68,16,512]{2,1,0:T(8,128)(2,1)S(1)}, bf16[68,16,512]{2,1,0:T(8,128)(2,1)S(1)}, u32[]{:S(2)}, u32[]{:S(2)}) collective-permute-start(bf16[68,16,512]{2,1,0:T(8,128)(2,1)S(1)} %get-tuple-element.41), channel_id=1, source_target_pairs={{0,6},{1,7},{2,0},{3,1},{4,2},{5,3},{6,4},{7,5},{8,14},{9,15},{10,... | collective-permute-start | bytes 3342344 | tf_op jit(solution)/shard_map/ppermute | solution.py:214
  192.5 30.1 %collective-permute-start.9 = (bf16[68,16,512]{2,1,0:T(8,128)(2,1)S(1)}, bf16[68,16,512]{2,1,0:T(8,128)(2,1)S(1)}, u32[]{:S(2)}, u32[]{:S(2)}) collective-permute-start(bf16[68,16,512]{2,1,0:T(8,128)(2,1)S(1)} %get-tuple-element.42), channel_id=1, source_target_pairs={{0,2},{1,3},{2,4},{3,5},{4,6},{5,7},{6,0},{7,1},{8,10},{9,11},{10,... | collective-permute-start | bytes 3342344 | tf_op jit(solution)/shard_map/ppermute | solution.py:214
  196.4 16.9 %collective-permute-start.14 = (bf16[16,16,512]{2,1,0:T(8,128)(2,1)S(1)}, bf16[16,16,512]{2,1,0:T(8,128)(2,1)S(1)}, u32[]{:S(2)}, u32[]{:S(2)}) collective-permute-start(bf16[16,16,512]{2,1,0:T(8,128)(2,1)S(1)} %copy-done.7), channel_id=1, source_target_pairs={{0,384},{8,392},{16,400},{24,408},{32,416},{40,424},{48,432},{56,4... | collective-permute-start | bytes 786440 | tf_op jit(solution)/shard_map/ppermute | solution.py:234
  199.1 16.1 %collective-permute-start.13 = (bf16[16,16,512]{2,1,0:T(8,128)(2,1)S(1)}, bf16[16,16,512]{2,1,0:T(8,128)(2,1)S(1)}, u32[]{:S(2)}, u32[]{:S(2)}) collective-permute-start(bf16[16,16,512]{2,1,0:T(8,128)(2,1)S(1)} %copy-done.7), channel_id=1, source_target_pairs={{0,256},{8,264},{16,272},{24,280},{32,288},{40,296},{48,304},{56,3... | collective-permute-start | bytes 786440 | tf_op jit(solution)/shard_map/ppermute | solution.py:234
  213.3 9.3 %copy-start.8 = (bf16[16,16,512]{2,1,0:T(8,128)(2,1)}, bf16[16,16,512]{2,1,0:T(8,128)(2,1)S(1)}, u32[]{:S(2)}) copy-start(bf16[16,16,512]{2,1,0:T(8,128)(2,1)S(1)} %collective-permute-done.14.refs_31_) | copy-start | bytes 786436
  213.3 9.2 %collective-permute-start.12 = (bf16[16,16,512]{2,1,0:T(8,128)(2,1)S(1)}, bf16[16,16,512]{2,1,0:T(8,128)(2,1)S(1)}, u32[]{:S(2)}, u32[]{:S(2)}) collective-permute-start(bf16[16,16,512]{2,1,0:T(8,128)(2,1)S(1)} %copy-done.7), channel_id=1, source_target_pairs={{0,128},{8,136},{16,144},{24,152},{32,160},{40,168},{48,176},{56,1... | collective-permute-start | bytes 786440 | tf_op jit(solution)/shard_map/ppermute | solution.py:234
  215.2 9.3 %copy-start.9 = (bf16[16,16,512]{2,1,0:T(8,128)(2,1)}, bf16[16,16,512]{2,1,0:T(8,128)(2,1)S(1)}, u32[]{:S(2)}) copy-start(bf16[16,16,512]{2,1,0:T(8,128)(2,1)S(1)} %collective-permute-done.13.refs_30_) | copy-start | bytes 786436
  222.5 2.0 copy-start.10
  222.5 6.9 %copy-start = (bf16[68,16,512]{2,1,0:T(8,128)(2,1)}, bf16[68,16,512]{2,1,0:T(8,128)(2,1)S(1)}, u32[]{:S(2)}) copy-start(bf16[68,16,512]{2,1,0:T(8,128)(2,1)S(1)} %collective-permute-done.11) | copy-start | bytes 3342340
  222.5 6.9 %copy-start.1 = (bf16[68,16,512]{2,1,0:T(8,128)(2,1)}, bf16[68,16,512]{2,1,0:T(8,128)(2,1)S(1)}, u32[]{:S(2)}) copy-start(bf16[68,16,512]{2,1,0:T(8,128)(2,1)S(1)} %collective-permute-done.10) | copy-start | bytes 3342340
  222.6 6.9 %copy-start.2 = (bf16[68,16,512]{2,1,0:T(8,128)(2,1)}, bf16[68,16,512]{2,1,0:T(8,128)(2,1)S(1)}, u32[]{:S(2)}) copy-start(bf16[68,16,512]{2,1,0:T(8,128)(2,1)S(1)} %collective-permute-done.9) | copy-start | bytes 3342340
  222.6 5.0 %collective-permute-start.15 = (bf16[68,16,512]{2,1,0:T(8,128)(2,1)S(1)}, bf16[68,16,512]{2,1,0:T(8,128)(2,1)}, u32[]{:S(2)}, u32[]{:S(2)}) collective-permute-start(bf16[68,16,512]{2,1,0:T(8,128)(2,1)S(1)} %collective-permute-done.9), channel_id=1, source_target_pairs={{0,1},{1,0},{2,3},{3,2},{4,5},{5,4},{6,7},{7,6},{8,9},{9,8},{10,11... | collective-permute-start | bytes 3342344 | tf_op jit(solution)/shard_map/ppermute | solution.py:219
  224.5 4.9 %collective-permute-start.16 = (bf16[68,16,512]{2,1,0:T(8,128)(2,1)S(1)}, bf16[68,16,512]{2,1,0:T(8,128)(2,1)}, u32[]{:S(2)}, u32[]{:S(2)}) collective-permute-start(bf16[68,16,512]{2,1,0:T(8,128)(2,1)S(1)} %collective-permute-done.10), channel_id=1, source_target_pairs={{0,1},{1,0},{2,3},{3,2},{4,5},{5,4},{6,7},{7,6},{8,9},{9,8},{10,11... | collective-permute-start | bytes 3342344 | tf_op jit(solution)/shard_map/ppermute | solution.py:219

commit v8 on v3

--- a/solution.py
+++ b/solution.py
@@ -10,6 +10,7 @@
 DH = 128
 BLOCK = 64
 FEATURES = 1024
+SHARED = 640
 Z = 16
 GROUP = 4
 
@@ -28,18 +29,22 @@
 def grouped(refs):
     groups = []
     for ref in refs:
-        if groups and groups[-1][0].shape[-1] < FEATURES and len(groups[-1]) == 1:
+        if groups and sum(r.shape[-1] for r in groups[-1]) < FEATURES - SHARED:
             groups[-1].append(ref)
         else:
             groups.append([ref])
     return groups
 
 
-def project(piece_refs, weight_ref, kv_ref):
+def project(head, shared_ref, piece_refs, weight_ref, kv_ref):
+    count = shared_ref.shape[0]
     rows = []
-    for group in grouped(piece_refs):
-        parts = [ref[...].reshape(-1, ref.shape[-1]) for ref in group]
-        rows.append(parts[0] if len(parts) == 1 else jnp.concatenate(parts, axis=1))
+    for at, group in enumerate(grouped(piece_refs)):
+        steps = (0, -1, 1, 2)[at % 4]
+        source = lax.rem(head + 2 * steps + count, count) ^ (at // 4)
+        parts = [shared_ref[source]] + [ref[...] for ref in group]
+        parts = [part.reshape(-1, part.shape[-1]) for part in parts]
+        rows.append(jnp.concatenate(parts, axis=1))
     kv = jnp.dot(
         jnp.concatenate(rows, axis=0), weight_ref[...], preferred_element_type=jnp.float32
     )
@@ -81,6 +86,8 @@
 
 
 def main_kernel(pieces_count, place_ref, query_ref, next_query_ref, grad_ref, next_grad_ref, *refs):
+    shared_ref, before_shared_ref, *refs = refs
+    head = place_ref[2]
     piece_refs, refs = refs[:pieces_count], refs[pieces_count:]
     before_refs, refs = refs[:pieces_count], refs[pieces_count:]
     *held_refs, context_ref, qgrad_ref, weight_ref, kv_ref, before_kv_ref, carry_ref = refs
@@ -94,12 +101,12 @@
                 at = (m & 3) * 4 + (m >> 2 & 1) * 2 + (m >> 3)
                 start = (y * Z + (place_ref[1] ^ m)) * rows
                 weight_ref[pl.ds(pl.multiple_of(start, 16), rows), :] = held_ref[at]
-        project(before_refs, weight_ref, before_kv_ref)
+        project(head, before_shared_ref, before_refs, weight_ref, before_kv_ref)
         ((context, qgrad),) = attend([query_ref[:BLOCK, :]], [grad_ref[:BLOCK, :]], before_kv_ref)
         carry_ref[0] = context
         carry_ref[1] = qgrad
 
-    project(piece_refs, weight_ref, kv_ref)
+    project(head, shared_ref, piece_refs, weight_ref, kv_ref)
     count = kv_ref.shape[1]
     row = lax.broadcasted_iota(jnp.int32, (BLOCK, query_ref.shape[1]), 0)
     last_row = row == BLOCK - 1
@@ -114,11 +121,11 @@
     carry_ref[0], carry_ref[1] = before
 
 
-def attention(place, queries, grads, pieces, held):
+def attention(place, queries, grads, shared, pieces, held):
     tokens, width = queries.shape
     blocks = tokens // BLOCK
     part_tokens = pieces[0].shape[1]
-    parts = sum(p.shape[-1] for p in pieces) // FEATURES
+    parts = shared.shape[0]
     keys = parts * part_tokens
     tile = pl.BlockSpec((GROUP * BLOCK, width), lambda i: (i, 0))
     next_tile = pl.BlockSpec(
@@ -137,6 +144,10 @@
         grid=(blocks // GROUP,),
         out_shape=(out, out),
         in_specs=[pl.BlockSpec(memory_space=pltpu.SMEM), tile, next_tile, tile, next_tile]
+        + [
+            pl.BlockSpec((parts, GROUP, part_tokens, SHARED), lambda i: (0, i, 0, 0)),
+            pl.BlockSpec((parts, 1, part_tokens, SHARED), lambda i: (0, blocks, 0, 0)),
+        ]
         + [pl.BlockSpec((GROUP,) + p.shape[1:], lambda i: (i, 0, 0)) for p in pieces]
         + [pl.BlockSpec((1,) + p.shape[1:], lambda i: (blocks, 0, 0)) for p in pieces]
         + [whole(h) for h in held],
@@ -147,14 +158,16 @@
             kv_scratch(1),
             pltpu.VMEM((2, BLOCK, width), jnp.float32),
         ],
-        compiler_params=pltpu.CompilerParams(vmem_limit_bytes=32 * 1024 * 1024),
+        compiler_params=pltpu.CompilerParams(vmem_limit_bytes=56 * 1024 * 1024),
         cost_estimate=pl.CostEstimate(
             flops=2 * (blocks + 1) * keys * 2 * width * (FEATURES + 2 * BLOCK),
             bytes_accessed=2 * (blocks * keys * FEATURES + 4 * tokens * width),
             transcendentals=blocks * keys * BLOCK * width // DH,
         ),
         name="blocks",
-    )(place, queries, queries, grads, grads, *pieces, *pieces, *held)
+    )(
+        place, queries, queries, grads, grads, shared, shared, *pieces, *pieces, *held
+    )
 
 
 def body(queries, context_grad, database, neighbour_ids, owner_map, key_weight, value_weight):
@@ -180,6 +193,7 @@
         axis=0,
         dtype=jnp.int32,
     )
+    asked_rows, key_weight = lax.optimization_barrier((asked_rows, key_weight))
     wanted = lax.all_to_all(
         asked_rows.reshape(seq_count, 1), "seq", split_axis=0, concat_axis=0, tiled=True
     ).reshape(-1)
@@ -210,9 +224,11 @@
     def other_core(value):
         return lax.ppermute(value, "head", [(i, i ^ 1) for i in range(head_devices)])
 
-    half = enc_width // 2
+    shared = lax.all_gather(asked[:, :, :SHARED], "head", axis=0, tiled=False)
+    shared = shared.reshape(head_devices, -1, 2 * part_tokens, SHARED)
+    asked = asked[:, :, SHARED:]
     before, after = along_x(asked, 1), along_x(asked, -1)
-    across = along_x(before[:, :, :half], 1), along_x(after[:, :, half:], -1)
+    across = along_x(before[:, :, :DH], 1), along_x(after[:, :, DH:], -1)
     pieces = [asked, before, after, *across]
     pieces += [other_core(piece) for piece in pieces]
     pieces = [piece.reshape(-1, 2 * part_tokens, piece.shape[-1]) for piece in pieces]
@@ -222,8 +238,8 @@
         pairs = [(i, (i + step * Z) % seq_count) for i in range(seq_count)]
         held.append(lax.ppermute(weight, "seq", pairs))
     my_seq = lax.axis_index("seq")
-    place = jnp.stack([my_seq // Z, my_seq % Z]).astype(jnp.int32)
-    return attention(place, queries, context_grad, pieces, held)
+    place = jnp.stack([my_seq // Z, my_seq % Z, my_head]).astype(jnp.int32)
+    return attention(place, queries, context_grad, shared, pieces, held)
 
 
 def solution(mesh):

time: 237 us -> 238 us (level)
  between operations: 1.01 us -> 14.5 us
  waiting for transfers between devices: 117 us -> 108 us
  local copies, waits for them, and re-layouts: 13.4 us -> 6.47 us
    ppermute x4, waiting for transfers between devices: 18.7 us -> 8.08 us  [along_x(): lax.ppermute(value, 'head', [(i, (i + 2 * steps) % head_devices) for i in...]
    unnamed x22 -> x26, local copies, waits for them, and re-layouts: 8.8 us -> 0.91 us
  transfers between devices with their start and end apart: 20 -> 21, of which waited for: 10 -> 8; matrix products, arithmetic and copies ran while one was open for 2% -> 2% of each run, Pallas kernels for 0% -> 0%
where the time goes in v8:
time: 238 us; the launch traced here: 235 us
  waiting for transfers between devices  108 us (45%)
  starting transfers between devices  89.9 us (38%)
  between operations  14.5 us (6%)
  Pallas kernels  13.1 us (6%)
  local copies, waits for them, and re-layouts  6.47 us (3%)
  other arithmetic  3.61 us (2%)
    ppermute x5, waiting for transfers between devices, from_z(): return lax.ppermute(value, 'seq', [(i, i ^ step) for i in range(seq_count)])  85.2 us
    ppermute x5, starting transfers between devices, from_z(): return lax.ppermute(value, 'seq', [(i, i ^ step) for i in range(seq_count)])  33.1 us
    ppermute x4, starting transfers between devices, along_x(): lax.ppermute(value, 'head', [(i, (i + 2 * steps) % head_devices) for i in...  13.6 us
    pallas_call x1, Pallas kernels, attention(): pl.pallas_call(functools.partial(main_kernel, len(pieces)), grid=(blocks...  13.1 us
    all_to_all x1, starting transfers between devices, body(): lax.all_to_all(outgoing, 'seq', split_axis=0, concat_axis=0, tiled=True)  12.2 us
    ppermute x5, starting transfers between devices, other_core(): lax.ppermute(value, 'head', [(i, i ^ 1) for i in range(head_devices)])  10.6 us
    ppermute x3, starting transfers between devices, body(): held.append(lax.ppermute(weight, 'seq', pairs))  9.79 us
    all_to_all x1, starting transfers between devices, body(): lax.all_to_all(asked_rows.reshape(seq_count, 1), 'seq', split_axis=0, con...  8.64 us
  transfers between devices with their start and end apart: 21, of which 8 were waited for; matrix products, arithmetic and copies ran while one was open for 2% of the time, Pallas kernels for 0%

profile of v8, /device:TPU:24, one launch (start us, length us, event | category | flops | bytes accessed | tf_op | source)
XLA Modules:
  0.0 235.3 jit_solution(8227167037252450274)
XLA Ops:
  8.0 0.9 select_reduce_fusion
  9.7 15.7 %collective-permute-start = (bf16[1,16,512]{2,1,0:T(8,128)(2,1)S(1)}, bf16[1,16,512]{2,1,0:T(8,128)(2,1)S(1)}, u32[]{:S(2)}, u32[]{:S(2)}) collective-permute-start(bf16[1,16,512]{2,1,0:T(8,128)(2,1)S(1)} %maximum_bitcast_fusion), channel_id=1, source_target_pairs={{0,64},{8,72},{16,80},{24,88},{32,96},{40,104},{48,112},{56,120},{... | collective-permute-start | bytes 49160 | tf_op jit(solution)/shard_map/ppermute | solution.py:202
  26.2 8.6 %all-to-all-start = ((s32[64,1,1]{2,1,0:T(1,128)}), s32[64,1,1]{2,1,0:T(1,128)S(1)}, u32[]{:S(2)}, u32[]{:S(2)}) async-start(s32[64,1,1]{2,1,0:T(1,128)} %copy.16), calls=%async_computation | async-start | bytes 65536 | tf_op jit(solution)/shard_map/all_to_all | solution.py:197
  34.8 7.3 %collective-permute-start.1 = (bf16[2,16,512]{2,1,0:T(8,128)(2,1)S(1)}, bf16[2,16,512]{2,1,0:T(8,128)(2,1)S(1)}, u32[]{:S(2)}, u32[]{:S(2)}) collective-permute-start(bf16[2,16,512]{2,1,0:T(8,128)(2,1)S(1)} %pad_maximum_fusion.2), channel_id=1, source_target_pairs={{0,32},{8,40},{16,48},{24,56},{32,0},{40,8},{48,16},{56,24},{64,96... | collective-permute-start | bytes 98312 | tf_op jit(solution)/shard_map/ppermute | solution.py:202
  42.1 1.1 dynamic-slice_bitcast_fusion
  43.2 4.1 %all-to-all-done = s32[64,1,1]{2,1,0:T(1,128)S(1)} async-done(((s32[64,1,1]{2,1,0:T(1,128)}), s32[64,1,1]{2,1,0:T(1,128)S(1)}, u32[]{:S(2)}, u32[]{:S(2)}) %all-to-all-start) | async-done | bytes 288 | tf_op jit(solution)/shard_map/all_to_all | solution.py:197
  47.3 1.2 reduce
  48.6 2.0 gather_fusion
  50.6 12.2 %all-to-all-start.1 = ((bf16[64,16,1024]{2,1,0:T(8,128)(2,1)}), bf16[64,16,1024]{2,1,0:T(8,128)(2,1)S(1)}, u32[]{:S(2)}, u32[]{:S(2)}) async-start(bf16[64,16,1024]{2,1,0:T(8,128)(2,1)} %gather_fusion), calls=%async_computation.1 | async-start | bytes 4194304 | tf_op jit(solution)/shard_map/all_to_all | solution.py:213
  62.9 5.2 %collective-permute-start.4 = (bf16[4,16,512]{2,1,0:T(8,128)(2,1)S(1)}, bf16[4,16,512]{2,1,0:T(8,128)(2,1)S(1)}, u32[]{:S(2)}, u32[]{:S(2)}) collective-permute-start(bf16[4,16,512]{2,1,0:T(8,128)(2,1)S(1)} %pad_maximum_fusion.1), channel_id=1, source_target_pairs={{0,24},{8,16},{16,8},{24,0},{32,56},{40,48},{48,40},{56,32},{64,88... | collective-permute-start | bytes 196616 | tf_op jit(solution)/shard_map/ppermute | solution.py:202
  68.1 1.9 collective-permute-start.3
  70.0 3.0 %collective-permute-start.2 = (bf16[4,16,512]{2,1,0:T(8,128)(2,1)S(1)}, bf16[4,16,512]{2,1,0:T(8,128)(2,1)S(1)}, u32[]{:S(2)}, u32[]{:S(2)}) collective-permute-start(bf16[4,16,512]{2,1,0:T(8,128)(2,1)S(1)} %pad_maximum_fusion.1), channel_id=1, source_target_pairs={{0,8},{8,0},{16,24},{24,16},{32,40},{40,32},{48,56},{56,48},{64,72... | collective-permute-start | bytes 196616 | tf_op jit(solution)/shard_map/ppermute | solution.py:202
  73.0 81.5 %collective-permute-done.4 = bf16[4,16,512]{2,1,0:T(8,128)(2,1)S(1)} collective-permute-done((bf16[4,16,512]{2,1,0:T(8,128)(2,1)S(1)}, bf16[4,16,512]{2,1,0:T(8,128)(2,1)S(1)}, u32[]{:S(2)}, u32[]{:S(2)}) %collective-permute-start.4) | collective-permute-done | bytes 65568 | tf_op jit(solution)/shard_map/ppermute | solution.py:202
  154.6 3.6 %collective-permute-done.3 = bf16[4,16,512]{2,1,0:T(8,128)(2,1)S(1)} collective-permute-done((bf16[4,16,512]{2,1,0:T(8,128)(2,1)S(1)}, bf16[4,16,512]{2,1,0:T(8,128)(2,1)S(1)}, u32[]{:S(2)}, u32[]{:S(2)}) %collective-permute-start.3) | collective-permute-done | bytes 65568 | tf_op jit(solution)/shard_map/ppermute | solution.py:202
  159.7 1.9 collective-permute-start.5
  161.7 7.1 %collective-permute-done.5 = bf16[2,16,1024]{2,1,0:T(8,128)(2,1)S(1)} collective-permute-done((bf16[2,16,1024]{2,1,0:T(8,128)(2,1)S(1)}, bf16[2,16,1024]{2,1,0:T(8,128)(2,1)S(1)}, u32[]{:S(2)}, u32[]{:S(2)}) %collective-permute-start.5) | collective-permute-done | bytes 65568 | tf_op jit(solution)/shard_map/ppermute | solution.py:21
  168.8 0.9 slice.24
  169.8 4.7 %collective-permute-start.7 = (bf16[34,16,384]{2,1,0:T(8,128)(2,1)S(1)}, bf16[34,16,384]{2,1,0:T(8,128)(2,1)S(1)}, u32[]{:S(2)}, u32[]{:S(2)}) collective-permute-start(bf16[34,16,384]{2,1,0:T(8,128)(2,1)S(1)} %slice.25), channel_id=1, source_target_pairs={{0,6},{1,7},{2,0},{3,1},{4,2},{5,3},{6,4},{7,5},{8,14},{9,15},{10,... | collective-permute-start | bytes 1253384 | tf_op jit(solution)/shard_map/ppermute | solution.py:220
  174.5 1.9 collective-permute-start.6
  176.4 2.7 %collective-permute-start.17 = (bf16[16,16,512]{2,1,0:T(8,128)(2,1)S(1)}, bf16[16,16,512]{2,1,0:T(8,128)(2,1)}, u32[]{:S(2)}, u32[]{:S(2)}) collective-permute-start(bf16[16,16,512]{2,1,0:T(8,128)(2,1)S(1)} %pad_maximum_fusion.refs_22_), channel_id=1, source_target_pairs={{0,384},{8,392},{16,400},{24,408},{32,416},{40,424},{48,432},{56,4... | collective-permute-start | bytes 786440 | tf_op jit(solution)/shard_map/ppermute | solution.py:239
  179.1 2.6 %collective-permute-start.16 = (bf16[16,16,512]{2,1,0:T(8,128)(2,1)S(1)}, bf16[16,16,512]{2,1,0:T(8,128)(2,1)}, u32[]{:S(2)}, u32[]{:S(2)}) collective-permute-start(bf16[16,16,512]{2,1,0:T(8,128)(2,1)S(1)} %pad_maximum_fusion.refs_22_), channel_id=1, source_target_pairs={{0,256},{8,264},{16,272},{24,280},{32,288},{40,296},{48,304},{56,3... | collective-permute-start | bytes 786440 | tf_op jit(solution)/shard_map/ppermute | solution.py:239
  181.8 5.1 %collective-permute-start.9 = (bf16[34,16,256]{2,1,0:T(8,128)(2,1)S(1)}, bf16[34,16,256]{2,1,0:T(8,128)(2,1)S(1)}, u32[]{:S(2)}, u32[]{:S(2)}) collective-permute-start(bf16[34,16,256]{2,1,0:T(8,128)(2,1)S(1)} %slice.27), channel_id=1, source_target_pairs={{0,6},{1,7},{2,0},{3,1},{4,2},{5,3},{6,4},{7,5},{8,14},{9,15},{10,... | collective-permute-start | bytes 835592 | tf_op jit(solution)/shard_map/ppermute | solution.py:220
  186.9 4.5 %collective-permute-start.15 = (bf16[16,16,512]{2,1,0:T(8,128)(2,1)S(1)}, bf16[16,16,512]{2,1,0:T(8,128)(2,1)S(1)}, u32[]{:S(2)}, u32[]{:S(2)}) collective-permute-start(bf16[16,16,512]{2,1,0:T(8,128)(2,1)S(1)} %pad_maximum_fusion.refs_22_), channel_id=1, source_target_pairs={{0,128},{8,136},{16,144},{24,152},{32,160},{40,168},{48,176},{56,1... | collective-permute-start | bytes 786440 | tf_op jit(solution)/shard_map/ppermute | solution.py:239
  191.5 1.9 collective-permute-start.10
  193.4 2.4 %collective-permute-start.12 = (bf16[34,16,384]{2,1,0:T(8,128)(2,1)S(1)}, bf16[34,16,384]{2,1,0:T(8,128)(2,1)S(1)}, u32[]{:S(2)}, u32[]{:S(2)}) collective-permute-start(bf16[34,16,384]{2,1,0:T(8,128)(2,1)S(1)} %collective-permute-done.7), channel_id=1, source_target_pairs={{0,1},{1,0},{2,3},{3,2},{4,5},{5,4},{6,7},{7,6},{8,9},{9,8},{10,11... | collective-permute-start | bytes 1253384 | tf_op jit(solution)/shard_map/ppermute | solution.py:225
  195.9 1.9 collective-permute-start.11
  197.8 1.9 collective-permute-start.8
  199.8 2.4 %collective-permute-start.14 = (bf16[34,16,256]{2,1,0:T(8,128)(2,1)S(1)}, bf16[34,16,256]{2,1,0:T(8,128)(2,1)S(1)}, u32[]{:S(2)}, u32[]{:S(2)}) collective-permute-start(bf16[34,16,256]{2,1,0:T(8,128)(2,1)S(1)} %collective-permute-done.9), channel_id=1, source_target_pairs={{0,1},{1,0},{2,3},{3,2},{4,5},{5,4},{6,7},{7,6},{8,9},{9,8},{10,11... | collective-permute-start | bytes 835592 | tf_op jit(solution)/shard_map/ppermute | solution.py:225
  202.2 8.1 %collective-permute-done.8 = bf16[34,16,128]{2,1,0:T(8,128)(2,1)S(1)} collective-permute-done((bf16[34,16,128]{2,1,0:T(8,128)(2,1)S(1)}, bf16[34,16,128]{2,1,0:T(8,128)(2,1)S(1)}, u32[]{:S(2)}, u32[]{:S(2)}) %collective-permute-start.8) | collective-permute-done | bytes 139296 | tf_op jit(solution)/shard_map/ppermute | solution.py:220
  210.3 1.9 collective-permute-start.13
  213.6 1.6 all-gather.3.cloned.1.call-done
  215.3 13.1 %blocks.1 = (bf16[1024,256]{1,0:T(8,128)(2,1)}, bf16[1024,256]{1,0:T(8,128)(2,1)}) custom-call(s32[3]{0:T(128)} %pad_add_fusion.place_ref, bf16[1024,256]{1,0:T(8,128)(2,1)} %next_query_ref.1, bf16[1024,256]{1,0:T(8,128)(2,1)} %next_query_ref.1, bf16[1024,256]{1,0:T(8,128)(2,1)} %next_grad_ref.1, bf16[1024,256]{1,0:T(8,128)(2,1)} %next_grad_ref.1, ...), custom_call_target="tpu_custom_call" | custom-call | flops 5133828096 | bytes 10485760 | tf_op jit(solution)/shard_map/blocks/pallas_call | solution.py:142
  (62 shorter events, 5.5 us)
Async XLA Ops:
  9.7 25.1 %collective-permute-start = (bf16[1,16,512]{2,1,0:T(8,128)(2,1)S(1)}, bf16[1,16,512]{2,1,0:T(8,128)(2,1)S(1)}, u32[]{:S(2)}, u32[]{:S(2)}) collective-permute-start(bf16[1,16,512]{2,1,0:T(8,128)(2,1)S(1)} %maximum_bitcast_fusion), channel_id=1, source_target_pairs={{0,64},{8,72},{16,80},{24,88},{32,96},{40,104},{48,112},{56,120},{... | collective-permute-start | bytes 49160 | tf_op jit(solution)/shard_map/ppermute | solution.py:202
  26.2 21.2 %all-to-all-start = ((s32[64,1,1]{2,1,0:T(1,128)}), s32[64,1,1]{2,1,0:T(1,128)S(1)}, u32[]{:S(2)}, u32[]{:S(2)}) async-start(s32[64,1,1]{2,1,0:T(1,128)} %copy.16), calls=%async_computation | async-start | bytes 65536 | tf_op jit(solution)/shard_map/all_to_all | solution.py:197
  34.8 13.7 %collective-permute-start.1 = (bf16[2,16,512]{2,1,0:T(8,128)(2,1)S(1)}, bf16[2,16,512]{2,1,0:T(8,128)(2,1)S(1)}, u32[]{:S(2)}, u32[]{:S(2)}) collective-permute-start(bf16[2,16,512]{2,1,0:T(8,128)(2,1)S(1)} %pad_maximum_fusion.2), channel_id=1, source_target_pairs={{0,32},{8,40},{16,48},{24,56},{32,0},{40,8},{48,16},{56,24},{64,96... | collective-permute-start | bytes 98312 | tf_op jit(solution)/shard_map/ppermute | solution.py:202
  50.6 108.4 %all-to-all-start.1 = ((bf16[64,16,1024]{2,1,0:T(8,128)(2,1)}), bf16[64,16,1024]{2,1,0:T(8,128)(2,1)S(1)}, u32[]{:S(2)}, u32[]{:S(2)}) async-start(bf16[64,16,1024]{2,1,0:T(8,128)(2,1)} %gather_fusion), calls=%async_computation.1 | async-start | bytes 4194304 | tf_op jit(solution)/shard_map/all_to_all | solution.py:213
  62.8 152.4 %all-gather.3.cloned.1.call-start = ((), (), s32[]{:S(2)}) async-start(), calls=%async_computation.2 | async-start | bytes 6266880 | tf_op jit(solution)/shard_map/all_gather | solution.py:227
  62.9 91.7 %collective-permute-start.4 = (bf16[4,16,512]{2,1,0:T(8,128)(2,1)S(1)}, bf16[4,16,512]{2,1,0:T(8,128)(2,1)S(1)}, u32[]{:S(2)}, u32[]{:S(2)}) collective-permute-start(bf16[4,16,512]{2,1,0:T(8,128)(2,1)S(1)} %pad_maximum_fusion.1), channel_id=1, source_target_pairs={{0,24},{8,16},{16,8},{24,0},{32,56},{40,48},{48,40},{56,32},{64,88... | collective-permute-start | bytes 196616 | tf_op jit(solution)/shard_map/ppermute | solution.py:202
  68.1 90.1 %collective-permute-start.3 = (bf16[4,16,512]{2,1,0:T(8,128)(2,1)S(1)}, bf16[4,16,512]{2,1,0:T(8,128)(2,1)S(1)}, u32[]{:S(2)}, u32[]{:S(2)}) collective-permute-start(bf16[4,16,512]{2,1,0:T(8,128)(2,1)S(1)} %pad_maximum_fusion.1), channel_id=1, source_target_pairs={{0,16},{8,24},{16,0},{24,8},{32,48},{40,56},{48,32},{56,40},{64,80... | collective-permute-start | bytes 196616 | tf_op jit(solution)/shard_map/ppermute | solution.py:202
  70.0 88.2 %collective-permute-start.2 = (bf16[4,16,512]{2,1,0:T(8,128)(2,1)S(1)}, bf16[4,16,512]{2,1,0:T(8,128)(2,1)S(1)}, u32[]{:S(2)}, u32[]{:S(2)}) collective-permute-start(bf16[4,16,512]{2,1,0:T(8,128)(2,1)S(1)} %pad_maximum_fusion.1), channel_id=1, source_target_pairs={{0,8},{8,0},{16,24},{24,16},{32,40},{40,32},{48,56},{56,48},{64,72... | collective-permute-start | bytes 196616 | tf_op jit(solution)/shard_map/ppermute | solution.py:202
  158.2 28.7 %copy-start.8 = (bf16[16,16,512]{2,1,0:T(8,128)(2,1)}, bf16[16,16,512]{2,1,0:T(8,128)(2,1)S(1)}, u32[]{:S(2)}) copy-start(bf16[16,16,512]{2,1,0:T(8,128)(2,1)S(1)} %pad_maximum_fusion.refs_22_) | copy-start | bytes 786436
  159.7 9.1 %collective-permute-start.5 = (bf16[2,16,1024]{2,1,0:T(8,128)(2,1)S(1)}, bf16[2,16,1024]{2,1,0:T(8,128)(2,1)S(1)}, u32[]{:S(2)}, u32[]{:S(2)}) collective-permute-start(bf16[2,16,1024]{2,1,0:T(8,128)(2,1)S(1)} %slice.15), channel_id=1, source_target_pairs={{0,8},{8,16},{16,24},{24,32},{32,40},{40,48},{48,56},{56,64},{64,7... | collective-permute-start | bytes 196616 | tf_op jit(solution)/shard_map/ppermute | solution.py:21
  169.8 45.4 %copy-start = (bf16[34,16,384]{2,1,0:T(8,128)(2,1)}, bf16[34,16,384]{2,1,0:T(8,128)(2,1)S(1)}, u32[]{:S(2)}) copy-start(bf16[34,16,384]{2,1,0:T(8,128)(2,1)S(1)} %slice.25) | copy-start | bytes 1253380
  169.8 11.9 %collective-permute-start.7 = (bf16[34,16,384]{2,1,0:T(8,128)(2,1)S(1)}, bf16[34,16,384]{2,1,0:T(8,128)(2,1)S(1)}, u32[]{:S(2)}, u32[]{:S(2)}) collective-permute-start(bf16[34,16,384]{2,1,0:T(8,128)(2,1)S(1)} %slice.25), channel_id=1, source_target_pairs={{0,6},{1,7},{2,0},{3,1},{4,2},{5,3},{6,4},{7,5},{8,14},{9,15},{10,... | collective-permute-start | bytes 1253384 | tf_op jit(solution)/shard_map/ppermute | solution.py:220
  174.5 21.3 %collective-permute-start.6 = (bf16[34,16,384]{2,1,0:T(8,128)(2,1)S(1)}, bf16[34,16,384]{2,1,0:T(8,128)(2,1)S(1)}, u32[]{:S(2)}, u32[]{:S(2)}) collective-permute-start(bf16[34,16,384]{2,1,0:T(8,128)(2,1)S(1)} %slice.25), channel_id=1, source_target_pairs={{0,2},{1,3},{2,4},{3,5},{4,6},{5,7},{6,0},{7,1},{8,10},{9,11},{10,... | collective-permute-start | bytes 1253384 | tf_op jit(solution)/shard_map/ppermute | solution.py:220
  176.4 15.0 %collective-permute-start.17 = (bf16[16,16,512]{2,1,0:T(8,128)(2,1)S(1)}, bf16[16,16,512]{2,1,0:T(8,128)(2,1)}, u32[]{:S(2)}, u32[]{:S(2)}) collective-permute-start(bf16[16,16,512]{2,1,0:T(8,128)(2,1)S(1)} %pad_maximum_fusion.refs_22_), channel_id=1, source_target_pairs={{0,384},{8,392},{16,400},{24,408},{32,416},{40,424},{48,432},{56,4... | collective-permute-start | bytes 786440 | tf_op jit(solution)/shard_map/ppermute | solution.py:239
  179.1 14.3 %collective-permute-start.16 = (bf16[16,16,512]{2,1,0:T(8,128)(2,1)S(1)}, bf16[16,16,512]{2,1,0:T(8,128)(2,1)}, u32[]{:S(2)}, u32[]{:S(2)}) collective-permute-start(bf16[16,16,512]{2,1,0:T(8,128)(2,1)S(1)} %pad_maximum_fusion.refs_22_), channel_id=1, source_target_pairs={{0,256},{8,264},{16,272},{24,280},{32,288},{40,296},{48,304},{56,3... | collective-permute-start | bytes 786440 | tf_op jit(solution)/shard_map/ppermute | solution.py:239
  181.7 33.5 %copy-start.1 = (bf16[34,16,384]{2,1,0:T(8,128)(2,1)}, bf16[34,16,384]{2,1,0:T(8,128)(2,1)S(1)}, u32[]{:S(2)}) copy-start(bf16[34,16,384]{2,1,0:T(8,128)(2,1)S(1)} %collective-permute-done.7) | copy-start | bytes 1253380
  181.8 18.0 %collective-permute-start.9 = (bf16[34,16,256]{2,1,0:T(8,128)(2,1)S(1)}, bf16[34,16,256]{2,1,0:T(8,128)(2,1)S(1)}, u32[]{:S(2)}, u32[]{:S(2)}) collective-permute-start(bf16[34,16,256]{2,1,0:T(8,128)(2,1)S(1)} %slice.27), channel_id=1, source_target_pairs={{0,6},{1,7},{2,0},{3,1},{4,2},{5,3},{6,4},{7,5},{8,14},{9,15},{10,... | collective-permute-start | bytes 835592 | tf_op jit(solution)/shard_map/ppermute | solution.py:220
  186.9 10.9 %collective-permute-start.15 = (bf16[16,16,512]{2,1,0:T(8,128)(2,1)S(1)}, bf16[16,16,512]{2,1,0:T(8,128)(2,1)S(1)}, u32[]{:S(2)}, u32[]{:S(2)}) collective-permute-start(bf16[16,16,512]{2,1,0:T(8,128)(2,1)S(1)} %pad_maximum_fusion.refs_22_), channel_id=1, source_target_pairs={{0,128},{8,136},{16,144},{24,152},{32,160},{40,168},{48,176},{56,1... | collective-permute-start | bytes 786440 | tf_op jit(solution)/shard_map/ppermute | solution.py:239
  191.5 21.3 %collective-permute-start.10 = (bf16[34,16,384]{2,1,0:T(8,128)(2,1)S(1)}, bf16[34,16,384]{2,1,0:T(8,128)(2,1)S(1)}, u32[]{:S(2)}, u32[]{:S(2)}) collective-permute-start(bf16[34,16,384]{2,1,0:T(8,128)(2,1)S(1)} %slice.25), channel_id=1, source_target_pairs={{0,1},{1,0},{2,3},{3,2},{4,5},{5,4},{6,7},{7,6},{8,9},{9,8},{10,11... | collective-permute-start | bytes 1253384 | tf_op jit(solution)/shard_map/ppermute | solution.py:225
  193.4 20.1 %collective-permute-start.12 = (bf16[34,16,384]{2,1,0:T(8,128)(2,1)S(1)}, bf16[34,16,384]{2,1,0:T(8,128)(2,1)S(1)}, u32[]{:S(2)}, u32[]{:S(2)}) collective-permute-start(bf16[34,16,384]{2,1,0:T(8,128)(2,1)S(1)} %collective-permute-done.7), channel_id=1, source_target_pairs={{0,1},{1,0},{2,3},{3,2},{4,5},{5,4},{6,7},{7,6},{8,9},{9,8},{10,11... | collective-permute-start | bytes 1253384 | tf_op jit(solution)/shard_map/ppermute | solution.py:225
  195.8 19.4 %copy-start.2 = (bf16[34,16,384]{2,1,0:T(8,128)(2,1)}, bf16[34,16,384]{2,1,0:T(8,128)(2,1)S(1)}, u32[]{:S(2)}) copy-start(bf16[34,16,384]{2,1,0:T(8,128)(2,1)S(1)} %collective-permute-done.6) | copy-start | bytes 1253380
  195.9 17.7 %collective-permute-start.11 = (bf16[34,16,384]{2,1,0:T(8,128)(2,1)S(1)}, bf16[34,16,384]{2,1,0:T(8,128)(2,1)S(1)}, u32[]{:S(2)}, u32[]{:S(2)}) collective-permute-start(bf16[34,16,384]{2,1,0:T(8,128)(2,1)S(1)} %collective-permute-done.6), channel_id=1, source_target_pairs={{0,1},{1,0},{2,3},{3,2},{4,5},{5,4},{6,7},{7,6},{8,9},{9,8},{10,11... | collective-permute-start | bytes 1253384 | tf_op jit(solution)/shard_map/ppermute | solution.py:225
  197.8 12.5 %copy-start.11 = (bf16[16,16,512]{2,1,0:T(8,128)(2,1)}, bf16[16,16,512]{2,1,0:T(8,128)(2,1)S(1)}, u32[]{:S(2)}) copy-start(bf16[16,16,512]{2,1,0:T(8,128)(2,1)S(1)} %collective-permute-done.15.refs_23_) | copy-start | bytes 786436
  197.8 12.4 %collective-permute-start.8 = (bf16[34,16,128]{2,1,0:T(8,128)(2,1)S(1)}, bf16[34,16,128]{2,1,0:T(8,128)(2,1)S(1)}, u32[]{:S(2)}, u32[]{:S(2)}) collective-permute-start(bf16[34,16,128]{2,1,0:T(8,128)(2,1)S(1)} %slice.26), channel_id=1, source_target_pairs={{0,2},{1,3},{2,4},{3,5},{4,6},{5,7},{6,0},{7,1},{8,10},{9,11},{10,... | collective-permute-start | bytes 417800 | tf_op jit(solution)/shard_map/ppermute | solution.py:220
  199.8 15.4 %copy-start.6 = (bf16[34,16,256]{2,1,0:T(8,128)(2,1)}, bf16[34,16,256]{2,1,0:T(8,128)(2,1)S(1)}, u32[]{:S(2)}) copy-start(bf16[34,16,256]{2,1,0:T(8,128)(2,1)S(1)} %collective-permute-done.9) | copy-start | bytes 835588
  199.8 13.8 %collective-permute-start.14 = (bf16[34,16,256]{2,1,0:T(8,128)(2,1)S(1)}, bf16[34,16,256]{2,1,0:T(8,128)(2,1)S(1)}, u32[]{:S(2)}, u32[]{:S(2)}) collective-permute-start(bf16[34,16,256]{2,1,0:T(8,128)(2,1)S(1)} %collective-permute-done.9), channel_id=1, source_target_pairs={{0,1},{1,0},{2,3},{3,2},{4,5},{5,4},{6,7},{7,6},{8,9},{9,8},{10,11... | collective-permute-start | bytes 835592 | tf_op jit(solution)/shard_map/ppermute | solution.py:225
  210.3 4.9 %copy-start.9 = (bf16[34,16,128]{2,1,0:T(8,128)(2,1)}, bf16[34,16,128]{2,1,0:T(8,128)(2,1)S(1)}, u32[]{:S(2)}) copy-start(bf16[34,16,128]{2,1,0:T(8,128)(2,1)S(1)} %collective-permute-done.8) | copy-start | bytes 417796
  210.3 3.2 %collective-permute-start.13 = (bf16[34,16,128]{2,1,0:T(8,128)(2,1)S(1)}, bf16[34,16,128]{2,1,0:T(8,128)(2,1)S(1)}, u32[]{:S(2)}, u32[]{:S(2)}) collective-permute-start(bf16[34,16,128]{2,1,0:T(8,128)(2,1)S(1)} %collective-permute-done.8), channel_id=1, source_target_pairs={{0,1},{1,0},{2,3},{3,2},{4,5},{5,4},{6,7},{7,6},{8,9},{9,8},{10,11... | collective-permute-start | bytes 417800 | tf_op jit(solution)/shard_map/ppermute | solution.py:225
  212.8 2.4 %copy-start.3 = (bf16[34,16,384]{2,1,0:T(8,128)(2,1)}, bf16[34,16,384]{2,1,0:T(8,128)(2,1)S(1)}, u32[]{:S(2)}) copy-start(bf16[34,16,384]{2,1,0:T(8,128)(2,1)S(1)} %collective-permute-done.10) | copy-start | bytes 1253380
  213.5 1.7 copy-start.10
  213.5 1.7 copy-start.4
  213.5 1.7 copy-start.5
  (1 other events, 1.7 us)
Sparse Core Ops, SparseCore 0:
  169.9 45.2 all-gather.2

commit v9 on v6

--- a/solution.py
+++ b/solution.py
@@ -210,9 +210,10 @@
     weight = jnp.concatenate([weight, moved(weight, 0, 2)], axis=0)
     outgoing, weight = lax.optimization_barrier((outgoing, weight))
     incoming = lax.all_to_all(outgoing, "seq", split_axis=0, concat_axis=0, tiled=True)
-    held = [moved(weight, k // 2, k % 2) for k in range(1, 2 * y_count)]
+    late = (2, 2 * y_count - 2)
+    held = {k: moved(weight, k // 2, k % 2) for k in range(1, 2 * y_count) if k not in late}
     asked = incoming[owner_index]
-    asked, held = lax.optimization_barrier((asked, [weight, *held]))
+    asked, weight, held = lax.optimization_barrier((asked, weight, held))
     asked = jnp.concatenate([asked, shifted(asked[-2:], "seq", 1)], axis=0)
 
     def along_x(value, steps):
@@ -232,7 +233,10 @@
     up, down = along_x(together(before_low, high), 1), along_x(together(after_high, low), -1)
     near = [asked, before_low, after_high]
     swapped = [other_core(a) for a in near]
-    up, down, swapped = lax.optimization_barrier((up, down, swapped))
+    rest = {k: moved(weight, k // 2, k % 2) for k in late}
+    up, down, swapped, rest = lax.optimization_barrier((up, down, swapped, rest))
+    held = {0: weight, **held, **rest}
+    held = [held[k] for k in range(2 * y_count)]
     blocks = queries.shape[0] // BLOCK
     pieces = []
     for arrays in (near + [up, down], swapped + [other_core(up), other_core(down)]):

time: 238 us -> 235 us (0.987)
    all_to_all x1, waiting for transfers between devices: 0.01 us -> 77.1 us  [body(): lax.all_to_all(outgoing, 'seq', split_axis=0, concat_axis=0, tiled=True)]
    ppermute x10, waiting for transfers between devices: 79.3 us -> 7.31 us  [moved(): return lax.ppermute(value, 'seq', pairs)]
    ppermute x4, waiting for transfers between devices: 18.3 us -> 11.7 us  [along_x(): lax.ppermute(value, 'head', [(i, (i + 2 * steps) % head_devices) for i in...]
  transfers between devices with their start and end apart: 22 -> 22, of which waited for: 10 -> 12; matrix products, arithmetic and copies ran while one was open for 3% -> 3% of each run, Pallas kernels for 0% -> 0%
where the time goes in v9:
time: 235 us; the launch traced here: 232 us
  waiting for transfers between devices  109 us (46%)
  starting transfers between devices  98.8 us (42%)
  Pallas kernels  13.3 us (6%)
  local copies, waits for them, and re-layouts  5.8 us (2%)
  other arithmetic  3.92 us (2%)
    all_to_all x1, waiting for transfers between devices, body(): lax.all_to_all(outgoing, 'seq', split_axis=0, concat_axis=0, tiled=True)  77.1 us
    ppermute x10, starting transfers between devices, moved(): return lax.ppermute(value, 'seq', pairs)  51.3 us
    ppermute x4, starting transfers between devices, along_x(): lax.ppermute(value, 'head', [(i, (i + 2 * steps) % head_devices) for i in...  14.1 us
    pallas_call x1, Pallas kernels, attention(): pl.pallas_call(functools.partial(main_kernel, len(pieces)), grid=(blocks...  13.3 us
    all_to_all x1, starting transfers between devices, body(): lax.all_to_all(outgoing, 'seq', split_axis=0, concat_axis=0, tiled=True)  11.8 us
    ppermute x4, waiting for transfers between devices, along_x(): lax.ppermute(value, 'head', [(i, (i + 2 * steps) % head_devices) for i in...  11.7 us
    ppermute x5, starting transfers between devices, other_core(): lax.ppermute(value, 'head', [(i, i ^ 1) for i in range(head_devices)])  10.6 us
    all_to_all x1, starting transfers between devices, body(): lax.all_to_all(asked_rows.reshape(seq_count, 1), 'seq', split_axis=0, con...  8.64 us
  transfers between devices with their start and end apart: 22, of which 12 were waited for; matrix products, arithmetic and copies ran while one was open for 3% of the time, Pallas kernels for 0%

profile of v9, /device:TPU:24, one launch (start us, length us, event | category | flops | bytes accessed | tf_op | source)
XLA Modules:
  0.0 232.4 jit_solution(14780027618752684896)
XLA Ops:
  3.2 15.7 %collective-permute-start = (bf16[1,16,512]{2,1,0:T(8,128)(2,1)S(1)}, bf16[1,16,512]{2,1,0:T(8,128)(2,1)S(1)}, u32[]{:S(2)}, u32[]{:S(2)}) collective-permute-start(bf16[1,16,512]{2,1,0:T(8,128)(2,1)S(1)} %maximum_bitcast_fusion), channel_id=1, source_target_pairs={{0,64},{8,72},{16,80},{24,88},{32,96},{40,104},{48,112},{56,120},{... | collective-permute-start | bytes 49160 | tf_op jit(solution)/shard_map/ppermute | solution.py:200
  19.6 8.6 %all-to-all-start = ((s32[64,1,1]{2,1,0:T(1,128)}), s32[64,1,1]{2,1,0:T(1,128)S(1)}, u32[]{:S(2)}, u32[]{:S(2)}) async-start(s32[64,1,1]{2,1,0:T(1,128)} %copy.16), calls=%async_computation | async-start | bytes 65536 | tf_op jit(solution)/shard_map/all_to_all | solution.py:192
  28.3 7.3 %collective-permute-start.1 = (bf16[2,16,512]{2,1,0:T(8,128)(2,1)S(1)}, bf16[2,16,512]{2,1,0:T(8,128)(2,1)S(1)}, u32[]{:S(2)}, u32[]{:S(2)}) collective-permute-start(bf16[2,16,512]{2,1,0:T(8,128)(2,1)S(1)} %pad_maximum_fusion.4), channel_id=1, source_target_pairs={{0,32},{8,40},{16,48},{24,56},{32,0},{40,8},{48,16},{56,24},{64,96... | collective-permute-start | bytes 98312 | tf_op jit(solution)/shard_map/ppermute | solution.py:200
  36.7 4.1 %all-to-all-done = s32[64,1,1]{2,1,0:T(1,128)S(1)} async-done(((s32[64,1,1]{2,1,0:T(1,128)}), s32[64,1,1]{2,1,0:T(1,128)S(1)}, u32[]{:S(2)}, u32[]{:S(2)}) %all-to-all-start) | async-done | bytes 288 | tf_op jit(solution)/shard_map/all_to_all | solution.py:192
  42.0 2.5 %collective-permute-start.2 = (bf16[4,16,512]{2,1,0:T(8,128)(2,1)S(1)}, bf16[4,16,512]{2,1,0:T(8,128)(2,1)S(1)}, u32[]{:S(2)}, u32[]{:S(2)}) collective-permute-start(bf16[4,16,512]{2,1,0:T(8,128)(2,1)S(1)} %pad_maximum_fusion.3), channel_id=1, source_target_pairs={{0,16},{8,24},{16,0},{24,8},{32,48},{40,56},{48,32},{56,40},{64,80... | collective-permute-start | bytes 196616 | tf_op jit(solution)/shard_map/ppermute | solution.py:200
  44.6 2.0 gather_fusion
  46.6 3.2 %collective-permute-done.2 = bf16[4,16,512]{2,1,0:T(8,128)(2,1)S(1)} collective-permute-done((bf16[4,16,512]{2,1,0:T(8,128)(2,1)S(1)}, bf16[4,16,512]{2,1,0:T(8,128)(2,1)S(1)}, u32[]{:S(2)}, u32[]{:S(2)}) %collective-permute-start.2) | collective-permute-done | bytes 65568 | tf_op jit(solution)/shard_map/ppermute | solution.py:200
  49.8 11.8 %all-to-all-start.1 = ((bf16[64,16,1024]{2,1,0:T(8,128)(2,1)}), bf16[64,16,1024]{2,1,0:T(8,128)(2,1)S(1)}, u32[]{:S(2)}, u32[]{:S(2)}) async-start(bf16[64,16,1024]{2,1,0:T(8,128)(2,1)} %gather_fusion), calls=%async_computation.1 | async-start | bytes 4194304 | tf_op jit(solution)/shard_map/all_to_all | solution.py:212
  61.7 3.6 %collective-permute-start.7 = (bf16[8,16,512]{2,1,0:T(8,128)(2,1)S(1)}, bf16[8,16,512]{2,1,0:T(8,128)(2,1)S(1)}, u32[]{:S(2)}, u32[]{:S(2)}) collective-permute-start(bf16[8,16,512]{2,1,0:T(8,128)(2,1)S(1)} %pad_maximum_fusion.2.refs_28_), channel_id=1, source_target_pairs={{0,392},{8,384},{16,408},{24,400},{32,424},{40,416},{48,440},{56,4... | collective-permute-start | bytes 393224 | tf_op jit(solution)/shard_map/ppermute | solution.py:200
  65.3 2.9 %collective-permute-start.6 = (bf16[8,16,512]{2,1,0:T(8,128)(2,1)S(1)}, bf16[8,16,512]{2,1,0:T(8,128)(2,1)}, u32[]{:S(2)}, u32[]{:S(2)}) collective-permute-start(bf16[8,16,512]{2,1,0:T(8,128)(2,1)S(1)} %pad_maximum_fusion.2.refs_28_), channel_id=1, source_target_pairs={{0,264},{8,256},{16,280},{24,272},{32,296},{40,288},{48,312},{56,3... | collective-permute-start | bytes 393224 | tf_op jit(solution)/shard_map/ppermute | solution.py:200
  68.1 4.5 %collective-permute-start.5 = (bf16[8,16,512]{2,1,0:T(8,128)(2,1)S(1)}, bf16[8,16,512]{2,1,0:T(8,128)(2,1)}, u32[]{:S(2)}, u32[]{:S(2)}) collective-permute-start(bf16[8,16,512]{2,1,0:T(8,128)(2,1)S(1)} %pad_maximum_fusion.2.refs_28_), channel_id=1, source_target_pairs={{0,256},{8,264},{16,272},{24,280},{32,288},{40,296},{48,304},{56,3... | collective-permute-start | bytes 393224 | tf_op jit(solution)/shard_map/ppermute | solution.py:200
  72.6 5.3 %collective-permute-start.4 = (bf16[8,16,512]{2,1,0:T(8,128)(2,1)S(1)}, bf16[8,16,512]{2,1,0:T(8,128)(2,1)}, u32[]{:S(2)}, u32[]{:S(2)}) collective-permute-start(bf16[8,16,512]{2,1,0:T(8,128)(2,1)S(1)} %pad_maximum_fusion.2.refs_28_), channel_id=1, source_target_pairs={{0,136},{8,128},{16,152},{24,144},{32,168},{40,160},{48,184},{56,1... | collective-permute-start | bytes 393224 | tf_op jit(solution)/shard_map/ppermute | solution.py:200
  77.9 2.5 %collective-permute-start.3 = (bf16[8,16,512]{2,1,0:T(8,128)(2,1)S(1)}, bf16[8,16,512]{2,1,0:T(8,128)(2,1)}, u32[]{:S(2)}, u32[]{:S(2)}) collective-permute-start(bf16[8,16,512]{2,1,0:T(8,128)(2,1)S(1)} %pad_maximum_fusion.2.refs_28_), channel_id=1, source_target_pairs={{0,8},{8,0},{16,24},{24,16},{32,40},{40,32},{48,56},{56,48},{64,72... | collective-permute-start | bytes 393224 | tf_op jit(solution)/shard_map/ppermute | solution.py:200
  80.4 77.1 %all-to-all-done.1 = bf16[64,16,1024]{2,1,0:T(8,128)(2,1)S(1)} async-done(((bf16[64,16,1024]{2,1,0:T(8,128)(2,1)}), bf16[64,16,1024]{2,1,0:T(8,128)(2,1)S(1)}, u32[]{:S(2)}, u32[]{:S(2)}) %all-to-all-start.1) | async-done | bytes 2097184 | tf_op jit(solution)/shard_map/all_to_all | solution.py:212
  158.2 2.0 collective-permute-done.4.refs_31_
  161.4 2.4 %collective-permute-start.8 = (bf16[2,16,1024]{2,1,0:T(8,128)(2,1)S(1)}, bf16[2,16,1024]{2,1,0:T(8,128)(2,1)S(1)}, u32[]{:S(2)}, u32[]{:S(2)}) collective-permute-start(bf16[2,16,1024]{2,1,0:T(8,128)(2,1)S(1)} %slice.41), channel_id=1, source_target_pairs={{0,8},{8,16},{16,24},{24,32},{32,40},{40,48},{48,56},{56,64},{64,7... | collective-permute-start | bytes 196616 | tf_op jit(solution)/shard_map/ppermute | solution.py:20
  163.8 5.8 %collective-permute-done.8 = bf16[2,16,1024]{2,1,0:T(8,128)(2,1)S(1)} collective-permute-done((bf16[2,16,1024]{2,1,0:T(8,128)(2,1)S(1)}, bf16[2,16,1024]{2,1,0:T(8,128)(2,1)S(1)}, u32[]{:S(2)}, u32[]{:S(2)}) %collective-permute-start.8) | collective-permute-done | bytes 65568 | tf_op jit(solution)/shard_map/ppermute | solution.py:20
  169.8 3.4 %collective-permute-start.9 = (bf16[34,16,512]{2,1,0:T(8,128)(2,1)S(1)}, bf16[34,16,512]{2,1,0:T(8,128)(2,1)S(1)}, u32[]{:S(2)}, u32[]{:S(2)}) collective-permute-start(bf16[34,16,512]{2,1,0:T(8,128)(2,1)S(1)} %get-tuple-element.43), channel_id=1, source_target_pairs={{0,2},{1,3},{2,4},{3,5},{4,6},{5,7},{6,0},{7,1},{8,10},{9,11},{10,... | collective-permute-start | bytes 1671176 | tf_op jit(solution)/shard_map/ppermute | solution.py:220
  173.2 3.7 %collective-permute-start.11 = (bf16[34,16,512]{2,1,0:T(8,128)(2,1)S(1)}, bf16[34,16,512]{2,1,0:T(8,128)(2,1)S(1)}, u32[]{:S(2)}, u32[]{:S(2)}) collective-permute-start(bf16[34,16,512]{2,1,0:T(8,128)(2,1)S(1)} %get-tuple-element.42), channel_id=1, source_target_pairs={{0,6},{1,7},{2,0},{3,1},{4,2},{5,3},{6,4},{7,5},{8,14},{9,15},{10,... | collective-permute-start | bytes 1671176 | tf_op jit(solution)/shard_map/ppermute | solution.py:220
  177.0 1.9 collective-permute-start.13
  179.0 5.7 %collective-permute-done.9 = bf16[34,16,512]{2,1,0:T(8,128)(2,1)S(1)} collective-permute-done((bf16[34,16,512]{2,1,0:T(8,128)(2,1)S(1)}, bf16[34,16,512]{2,1,0:T(8,128)(2,1)S(1)}, u32[]{:S(2)}, u32[]{:S(2)}) %collective-permute-start.9) | collective-permute-done | bytes 557088 | tf_op jit(solution)/shard_map/ppermute | solution.py:220
  184.9 2.2 collective-permute-start.10
  187.4 4.9 %collective-permute-start.12 = (bf16[68,16,512]{2,1,0:T(8,128)(2,1)S(1)}, bf16[68,16,512]{2,1,0:T(8,128)(2,1)S(1)}, u32[]{:S(2)}, u32[]{:S(2)}) collective-permute-start(bf16[68,16,512]{2,1,0:T(8,128)(2,1)S(1)} %pad_maximum_fusion.1), channel_id=1, source_target_pairs={{0,6},{1,7},{2,0},{3,1},{4,2},{5,3},{6,4},{7,5},{8,14},{9,15},{10,... | collective-permute-start | bytes 3342344 | tf_op jit(solution)/shard_map/ppermute | solution.py:220
  192.3 2.7 %collective-permute-start.17 = (bf16[8,16,512]{2,1,0:T(8,128)(2,1)S(1)}, bf16[8,16,512]{2,1,0:T(8,128)(2,1)S(1)}, u32[]{:S(2)}, u32[]{:S(2)}) collective-permute-start(bf16[8,16,512]{2,1,0:T(8,128)(2,1)S(1)} %pad_maximum_fusion.2.refs_28_), channel_id=1, source_target_pairs={{0,384},{8,392},{16,400},{24,408},{32,416},{40,424},{48,432},{56,4... | collective-permute-start | bytes 393224 | tf_op jit(solution)/shard_map/ppermute | solution.py:200
  195.0 4.3 %collective-permute-start.16 = (bf16[8,16,512]{2,1,0:T(8,128)(2,1)S(1)}, bf16[8,16,512]{2,1,0:T(8,128)(2,1)S(1)}, u32[]{:S(2)}, u32[]{:S(2)}) collective-permute-start(bf16[8,16,512]{2,1,0:T(8,128)(2,1)S(1)} %pad_maximum_fusion.2.refs_28_), channel_id=1, source_target_pairs={{0,128},{8,136},{16,144},{24,152},{32,160},{40,168},{48,176},{56,1... | collective-permute-start | bytes 393224 | tf_op jit(solution)/shard_map/ppermute | solution.py:200
  200.3 1.9 collective-permute-start.15
  202.3 2.4 %collective-permute-start.14 = (bf16[34,16,512]{2,1,0:T(8,128)(2,1)S(1)}, bf16[34,16,512]{2,1,0:T(8,128)(2,1)S(1)}, u32[]{:S(2)}, u32[]{:S(2)}) collective-permute-start(bf16[34,16,512]{2,1,0:T(8,128)(2,1)S(1)} %collective-permute-done.9), channel_id=1, source_target_pairs={{0,1},{1,0},{2,3},{3,2},{4,5},{5,4},{6,7},{7,6},{8,9},{9,8},{10,11... | collective-permute-start | bytes 1671176 | tf_op jit(solution)/shard_map/ppermute | solution.py:225
  206.3 4.5 %collective-permute-done.10 = bf16[68,16,512]{2,1,0:T(8,128)(2,1)S(1)} collective-permute-done((bf16[68,16,512]{2,1,0:T(8,128)(2,1)S(1)}, bf16[68,16,512]{2,1,0:T(8,128)(2,1)S(1)}, u32[]{:S(2)}, u32[]{:S(2)}) %collective-permute-start.10) | collective-permute-done | bytes 1114144 | tf_op jit(solution)/shard_map/ppermute | solution.py:220
  212.3 1.9 collective-permute-start.18
  214.2 2.4 %collective-permute-start.19 = (bf16[68,16,512]{2,1,0:T(8,128)(2,1)S(1)}, bf16[68,16,512]{2,1,0:T(8,128)(2,1)}, u32[]{:S(2)}, u32[]{:S(2)}) collective-permute-start(bf16[68,16,512]{2,1,0:T(8,128)(2,1)S(1)} %collective-permute-done.12), channel_id=1, source_target_pairs={{0,1},{1,0},{2,3},{3,2},{4,5},{5,4},{6,7},{7,6},{8,9},{9,8},{10,11... | collective-permute-start | bytes 3342344 | tf_op jit(solution)/shard_map/ppermute | solution.py:225
  217.2 1.9 collective-permute-done.19
  219.1 13.3 %blocks.1 = (bf16[1024,256]{1,0:T(8,128)(2,1)}, bf16[1024,256]{1,0:T(8,128)(2,1)}) custom-call(s32[2]{0:T(128)} %pad_add_fusion.place_ref, bf16[1024,256]{1,0:T(8,128)(2,1)} %next_query_ref.1, bf16[1024,256]{1,0:T(8,128)(2,1)} %next_query_ref.1, bf16[1024,256]{1,0:T(8,128)(2,1)} %next_grad_ref.1, bf16[1024,256]{1,0:T(8,128)(2,1)} %next_grad_ref.1, ...), custom_call_target="tpu_custom_call" | custom-call | flops 5133828096 | bytes 10485760 | tf_op jit(solution)/shard_map/blocks/pallas_call | solution.py:143
  (70 shorter events, 12.9 us)
Async XLA Ops:
  3.2 25.1 %collective-permute-start = (bf16[1,16,512]{2,1,0:T(8,128)(2,1)S(1)}, bf16[1,16,512]{2,1,0:T(8,128)(2,1)S(1)}, u32[]{:S(2)}, u32[]{:S(2)}) collective-permute-start(bf16[1,16,512]{2,1,0:T(8,128)(2,1)S(1)} %maximum_bitcast_fusion), channel_id=1, source_target_pairs={{0,64},{8,72},{16,80},{24,88},{32,96},{40,104},{48,112},{56,120},{... | collective-permute-start | bytes 49160 | tf_op jit(solution)/shard_map/ppermute | solution.py:200
  19.6 21.2 %all-to-all-start = ((s32[64,1,1]{2,1,0:T(1,128)}), s32[64,1,1]{2,1,0:T(1,128)S(1)}, u32[]{:S(2)}, u32[]{:S(2)}) async-start(s32[64,1,1]{2,1,0:T(1,128)} %copy.16), calls=%async_computation | async-start | bytes 65536 | tf_op jit(solution)/shard_map/all_to_all | solution.py:192
  28.3 13.7 %collective-permute-start.1 = (bf16[2,16,512]{2,1,0:T(8,128)(2,1)S(1)}, bf16[2,16,512]{2,1,0:T(8,128)(2,1)S(1)}, u32[]{:S(2)}, u32[]{:S(2)}) collective-permute-start(bf16[2,16,512]{2,1,0:T(8,128)(2,1)S(1)} %pad_maximum_fusion.4), channel_id=1, source_target_pairs={{0,32},{8,40},{16,48},{24,56},{32,0},{40,8},{48,16},{56,24},{64,96... | collective-permute-start | bytes 98312 | tf_op jit(solution)/shard_map/ppermute | solution.py:200
  42.0 7.8 %collective-permute-start.2 = (bf16[4,16,512]{2,1,0:T(8,128)(2,1)S(1)}, bf16[4,16,512]{2,1,0:T(8,128)(2,1)S(1)}, u32[]{:S(2)}, u32[]{:S(2)}) collective-permute-start(bf16[4,16,512]{2,1,0:T(8,128)(2,1)S(1)} %pad_maximum_fusion.3), channel_id=1, source_target_pairs={{0,16},{8,24},{16,0},{24,8},{32,48},{40,56},{48,32},{56,40},{64,80... | collective-permute-start | bytes 196616 | tf_op jit(solution)/shard_map/ppermute | solution.py:200
  49.8 145.2 %copy-start.9 = (bf16[8,16,512]{2,1,0:T(8,128)(2,1)}, bf16[8,16,512]{2,1,0:T(8,128)(2,1)S(1)}, u32[]{:S(2)}) copy-start(bf16[8,16,512]{2,1,0:T(8,128)(2,1)S(1)} %pad_maximum_fusion.2.refs_28_) | copy-start | bytes 393220
  49.8 107.7 %all-to-all-start.1 = ((bf16[64,16,1024]{2,1,0:T(8,128)(2,1)}), bf16[64,16,1024]{2,1,0:T(8,128)(2,1)S(1)}, u32[]{:S(2)}, u32[]{:S(2)}) async-start(bf16[64,16,1024]{2,1,0:T(8,128)(2,1)} %gather_fusion), calls=%async_computation.1 | async-start | bytes 4194304 | tf_op jit(solution)/shard_map/all_to_all | solution.py:212
  61.7 96.5 %collective-permute-start.7 = (bf16[8,16,512]{2,1,0:T(8,128)(2,1)S(1)}, bf16[8,16,512]{2,1,0:T(8,128)(2,1)S(1)}, u32[]{:S(2)}, u32[]{:S(2)}) collective-permute-start(bf16[8,16,512]{2,1,0:T(8,128)(2,1)S(1)} %pad_maximum_fusion.2.refs_28_), channel_id=1, source_target_pairs={{0,392},{8,384},{16,408},{24,400},{32,424},{40,416},{48,440},{56,4... | collective-permute-start | bytes 393224 | tf_op jit(solution)/shard_map/ppermute | solution.py:200
  65.3 92.9 %collective-permute-start.6 = (bf16[8,16,512]{2,1,0:T(8,128)(2,1)S(1)}, bf16[8,16,512]{2,1,0:T(8,128)(2,1)}, u32[]{:S(2)}, u32[]{:S(2)}) collective-permute-start(bf16[8,16,512]{2,1,0:T(8,128)(2,1)S(1)} %pad_maximum_fusion.2.refs_28_), channel_id=1, source_target_pairs={{0,264},{8,256},{16,280},{24,272},{32,296},{40,288},{48,312},{56,3... | collective-permute-start | bytes 393224 | tf_op jit(solution)/shard_map/ppermute | solution.py:200
  68.1 90.1 %collective-permute-start.5 = (bf16[8,16,512]{2,1,0:T(8,128)(2,1)S(1)}, bf16[8,16,512]{2,1,0:T(8,128)(2,1)}, u32[]{:S(2)}, u32[]{:S(2)}) collective-permute-start(bf16[8,16,512]{2,1,0:T(8,128)(2,1)S(1)} %pad_maximum_fusion.2.refs_28_), channel_id=1, source_target_pairs={{0,256},{8,264},{16,272},{24,280},{32,288},{40,296},{48,304},{56,3... | collective-permute-start | bytes 393224 | tf_op jit(solution)/shard_map/ppermute | solution.py:200
  72.6 87.6 %collective-permute-start.4 = (bf16[8,16,512]{2,1,0:T(8,128)(2,1)S(1)}, bf16[8,16,512]{2,1,0:T(8,128)(2,1)}, u32[]{:S(2)}, u32[]{:S(2)}) collective-permute-start(bf16[8,16,512]{2,1,0:T(8,128)(2,1)S(1)} %pad_maximum_fusion.2.refs_28_), channel_id=1, source_target_pairs={{0,136},{8,128},{16,152},{24,144},{32,168},{40,160},{48,184},{56,1... | collective-permute-start | bytes 393224 | tf_op jit(solution)/shard_map/ppermute | solution.py:200
  77.9 83.4 %collective-permute-start.3 = (bf16[8,16,512]{2,1,0:T(8,128)(2,1)S(1)}, bf16[8,16,512]{2,1,0:T(8,128)(2,1)}, u32[]{:S(2)}, u32[]{:S(2)}) collective-permute-start(bf16[8,16,512]{2,1,0:T(8,128)(2,1)S(1)} %pad_maximum_fusion.2.refs_28_), channel_id=1, source_target_pairs={{0,8},{8,0},{16,24},{24,16},{32,40},{40,32},{48,56},{56,48},{64,72... | collective-permute-start | bytes 393224 | tf_op jit(solution)/shard_map/ppermute | solution.py:200
  158.2 11.4 %copy-start.10 = (bf16[8,16,512]{2,1,0:T(8,128)(2,1)}, bf16[8,16,512]{2,1,0:T(8,128)(2,1)S(1)}, u32[]{:S(2)}) copy-start(bf16[8,16,512]{2,1,0:T(8,128)(2,1)S(1)} %collective-permute-done.7.refs_35_) | copy-start | bytes 393220
  161.4 8.3 %collective-permute-start.8 = (bf16[2,16,1024]{2,1,0:T(8,128)(2,1)S(1)}, bf16[2,16,1024]{2,1,0:T(8,128)(2,1)S(1)}, u32[]{:S(2)}, u32[]{:S(2)}) collective-permute-start(bf16[2,16,1024]{2,1,0:T(8,128)(2,1)S(1)} %slice.41), channel_id=1, source_target_pairs={{0,8},{8,16},{16,24},{24,32},{32,40},{40,48},{48,56},{56,64},{64,7... | collective-permute-start | bytes 196616 | tf_op jit(solution)/shard_map/ppermute | solution.py:20
  169.6 7.4 %copy-start.3 = (bf16[34,16,1024]{2,1,0:T(8,128)(2,1)}, bf16[34,16,1024]{2,1,0:T(8,128)(2,1)S(1)}, u32[]{:S(2)}) copy-start(bf16[34,16,1024]{2,1,0:T(8,128)(2,1)S(1)} %constant_dynamic-update-slice_fusion) | copy-start | bytes 3342340
  169.8 14.9 %collective-permute-start.9 = (bf16[34,16,512]{2,1,0:T(8,128)(2,1)S(1)}, bf16[34,16,512]{2,1,0:T(8,128)(2,1)S(1)}, u32[]{:S(2)}, u32[]{:S(2)}) collective-permute-start(bf16[34,16,512]{2,1,0:T(8,128)(2,1)S(1)} %get-tuple-element.43), channel_id=1, source_target_pairs={{0,2},{1,3},{2,4},{3,5},{4,6},{5,7},{6,0},{7,1},{8,10},{9,11},{10,... | collective-permute-start | bytes 1671176 | tf_op jit(solution)/shard_map/ppermute | solution.py:220
  173.2 13.9 %collective-permute-start.11 = (bf16[34,16,512]{2,1,0:T(8,128)(2,1)S(1)}, bf16[34,16,512]{2,1,0:T(8,128)(2,1)S(1)}, u32[]{:S(2)}, u32[]{:S(2)}) collective-permute-start(bf16[34,16,512]{2,1,0:T(8,128)(2,1)S(1)} %get-tuple-element.42), channel_id=1, source_target_pairs={{0,6},{1,7},{2,0},{3,1},{4,2},{5,3},{6,4},{7,5},{8,14},{9,15},{10,... | collective-permute-start | bytes 1671176 | tf_op jit(solution)/shard_map/ppermute | solution.py:220
  177.0 29.2 %collective-permute-start.13 = (bf16[34,16,1024]{2,1,0:T(8,128)(2,1)S(1)}, bf16[34,16,1024]{2,1,0:T(8,128)(2,1)S(1)}, u32[]{:S(2)}, u32[]{:S(2)}) collective-permute-start(bf16[34,16,1024]{2,1,0:T(8,128)(2,1)S(1)} %constant_dynamic-update-slice_fusion), channel_id=1, source_target_pairs={{0,1},{1,0},{2,3},{3,2},{4,5},{5,4},{6,7},{7,6},{8,9},{9,8},{10,11... | collective-permute-start | bytes 3342344 | tf_op jit(solution)/shard_map/ppermute | solution.py:225
  184.7 17.6 %copy-start.4 = (bf16[34,16,512]{2,1,0:T(8,128)(2,1)}, bf16[34,16,512]{2,1,0:T(8,128)(2,1)S(1)}, u32[]{:S(2)}) copy-start(bf16[34,16,512]{2,1,0:T(8,128)(2,1)S(1)} %collective-permute-done.9) | copy-start | bytes 1671172
  184.9 25.9 %collective-permute-start.10 = (bf16[68,16,512]{2,1,0:T(8,128)(2,1)S(1)}, bf16[68,16,512]{2,1,0:T(8,128)(2,1)S(1)}, u32[]{:S(2)}, u32[]{:S(2)}) collective-permute-start(bf16[68,16,512]{2,1,0:T(8,128)(2,1)S(1)} %pad_maximum_fusion), channel_id=1, source_target_pairs={{0,2},{1,3},{2,4},{3,5},{4,6},{5,7},{6,0},{7,1},{8,10},{9,11},{10,... | collective-permute-start | bytes 3342344 | tf_op jit(solution)/shard_map/ppermute | solution.py:220
  187.1 13.2 %copy-start.5 = (bf16[34,16,512]{2,1,0:T(8,128)(2,1)}, bf16[34,16,512]{2,1,0:T(8,128)(2,1)S(1)}, u32[]{:S(2)}) copy-start(bf16[34,16,512]{2,1,0:T(8,128)(2,1)S(1)} %collective-permute-done.11) | copy-start | bytes 1671172
  187.4 24.9 %collective-permute-start.12 = (bf16[68,16,512]{2,1,0:T(8,128)(2,1)S(1)}, bf16[68,16,512]{2,1,0:T(8,128)(2,1)S(1)}, u32[]{:S(2)}, u32[]{:S(2)}) collective-permute-start(bf16[68,16,512]{2,1,0:T(8,128)(2,1)S(1)} %pad_maximum_fusion.1), channel_id=1, source_target_pairs={{0,6},{1,7},{2,0},{3,1},{4,2},{5,3},{6,4},{7,5},{8,14},{9,15},{10,... | collective-permute-start | bytes 3342344 | tf_op jit(solution)/shard_map/ppermute | solution.py:220
  192.3 8.1 %collective-permute-start.17 = (bf16[8,16,512]{2,1,0:T(8,128)(2,1)S(1)}, bf16[8,16,512]{2,1,0:T(8,128)(2,1)S(1)}, u32[]{:S(2)}, u32[]{:S(2)}) collective-permute-start(bf16[8,16,512]{2,1,0:T(8,128)(2,1)S(1)} %pad_maximum_fusion.2.refs_28_), channel_id=1, source_target_pairs={{0,384},{8,392},{16,400},{24,408},{32,416},{40,424},{48,432},{56,4... | collective-permute-start | bytes 393224 | tf_op jit(solution)/shard_map/ppermute | solution.py:200
  195.0 7.3 %collective-permute-start.16 = (bf16[8,16,512]{2,1,0:T(8,128)(2,1)S(1)}, bf16[8,16,512]{2,1,0:T(8,128)(2,1)S(1)}, u32[]{:S(2)}, u32[]{:S(2)}) collective-permute-start(bf16[8,16,512]{2,1,0:T(8,128)(2,1)S(1)} %pad_maximum_fusion.2.refs_28_), channel_id=1, source_target_pairs={{0,128},{8,136},{16,144},{24,152},{32,160},{40,168},{48,176},{56,1... | collective-permute-start | bytes 393224 | tf_op jit(solution)/shard_map/ppermute | solution.py:200
  200.3 10.5 %copy-start.11 = (bf16[8,16,512]{2,1,0:T(8,128)(2,1)}, bf16[8,16,512]{2,1,0:T(8,128)(2,1)S(1)}, u32[]{:S(2)}) copy-start(bf16[8,16,512]{2,1,0:T(8,128)(2,1)S(1)} %collective-permute-done.17.refs_34_) | copy-start | bytes 393220
  200.3 4.4 %collective-permute-start.15 = (bf16[34,16,512]{2,1,0:T(8,128)(2,1)S(1)}, bf16[34,16,512]{2,1,0:T(8,128)(2,1)S(1)}, u32[]{:S(2)}, u32[]{:S(2)}) collective-permute-start(bf16[34,16,512]{2,1,0:T(8,128)(2,1)S(1)} %collective-permute-done.11), channel_id=1, source_target_pairs={{0,1},{1,0},{2,3},{3,2},{4,5},{5,4},{6,7},{7,6},{8,9},{9,8},{10,11... | collective-permute-start | bytes 1671176 | tf_op jit(solution)/shard_map/ppermute | solution.py:225
  202.3 8.5 %copy-start.12 = (bf16[8,16,512]{2,1,0:T(8,128)(2,1)}, bf16[8,16,512]{2,1,0:T(8,128)(2,1)S(1)}, u32[]{:S(2)}) copy-start(bf16[8,16,512]{2,1,0:T(8,128)(2,1)S(1)} %collective-permute-done.16.refs_30_) | copy-start | bytes 393220
  202.3 4.0 %collective-permute-start.14 = (bf16[34,16,512]{2,1,0:T(8,128)(2,1)S(1)}, bf16[34,16,512]{2,1,0:T(8,128)(2,1)S(1)}, u32[]{:S(2)}, u32[]{:S(2)}) collective-permute-start(bf16[34,16,512]{2,1,0:T(8,128)(2,1)S(1)} %collective-permute-done.9), channel_id=1, source_target_pairs={{0,1},{1,0},{2,3},{3,2},{4,5},{5,4},{6,7},{7,6},{8,9},{9,8},{10,11... | collective-permute-start | bytes 1671176 | tf_op jit(solution)/shard_map/ppermute | solution.py:225
  204.7 9.5 %copy-start.7 = (bf16[34,16,512]{2,1,0:T(8,128)(2,1)}, bf16[34,16,512]{2,1,0:T(8,128)(2,1)S(1)}, u32[]{:S(2)}) copy-start(bf16[34,16,512]{2,1,0:T(8,128)(2,1)S(1)} %collective-permute-done.15) | copy-start | bytes 1671172
  206.3 7.9 %copy-start.8 = (bf16[34,16,512]{2,1,0:T(8,128)(2,1)}, bf16[34,16,512]{2,1,0:T(8,128)(2,1)S(1)}, u32[]{:S(2)}) copy-start(bf16[34,16,512]{2,1,0:T(8,128)(2,1)S(1)} %collective-permute-done.14) | copy-start | bytes 1671172
  210.8 8.3 %copy-start = (bf16[68,16,512]{2,1,0:T(8,128)(2,1)}, bf16[68,16,512]{2,1,0:T(8,128)(2,1)S(1)}, u32[]{:S(2)}) copy-start(bf16[68,16,512]{2,1,0:T(8,128)(2,1)S(1)} %collective-permute-done.10) | copy-start | bytes 3342340
  212.3 4.9 %collective-permute-start.18 = (bf16[68,16,512]{2,1,0:T(8,128)(2,1)S(1)}, bf16[68,16,512]{2,1,0:T(8,128)(2,1)S(1)}, u32[]{:S(2)}, u32[]{:S(2)}) collective-permute-start(bf16[68,16,512]{2,1,0:T(8,128)(2,1)S(1)} %collective-permute-done.10), channel_id=1, source_target_pairs={{0,1},{1,0},{2,3},{3,2},{4,5},{5,4},{6,7},{7,6},{8,9},{9,8},{10,11... | collective-permute-start | bytes 3342344 | tf_op jit(solution)/shard_map/ppermute | solution.py:225
  214.2 4.9 %collective-permute-start.19 = (bf16[68,16,512]{2,1,0:T(8,128)(2,1)S(1)}, bf16[68,16,512]{2,1,0:T(8,128)(2,1)}, u32[]{:S(2)}, u32[]{:S(2)}) collective-permute-start(bf16[68,16,512]{2,1,0:T(8,128)(2,1)S(1)} %collective-permute-done.12), channel_id=1, source_target_pairs={{0,1},{1,0},{2,3},{3,2},{4,5},{5,4},{6,7},{7,6},{8,9},{9,8},{10,11... | collective-permute-start | bytes 3342344 | tf_op jit(solution)/shard_map/ppermute | solution.py:225
  (3 other events, 14.8 us)
